TPU v7x, 32 devices: a whole 2x2x4 slice. The times are simulated.
32 devices in a mesh: wide: 8 (over y, x, core), narrow: 4 (over z).
Axes of the slice: x: 2, y: 2, z: 4, core: 2. Of those that a mesh axis runs over, the one named last changes fastest.
Arguments:
- tokens: bfloat16 [18432, 1024], P(('wide', 'narrow')), may hold values from -6 to 6
- clip_cond: bfloat16 [2, 1024], replicated, may hold values from -6 to 6
- image_cond: bfloat16 [8, 1024], P('wide'), may hold values from -6 to 6
- image_count: int32 [8], P('wide'), may hold values from 0 to 1, as said below
- space_modulate: bfloat16 [1024, 6144], P('wide', 'narrow'), may hold values from -0.1875 to 0.1875
- space_project: bfloat16 [1024, 3072], P('wide', 'narrow'), may hold values from -0.1875 to 0.1875
- space_output: bfloat16 [1024, 1024], P('wide', 'narrow'), may hold values from -0.75 to 0.75
- space_expand: bfloat16 [1024, 4096], P('wide', 'narrow'), may hold values from -0.1875 to 0.1875
- space_reduce: bfloat16 [4096, 1024], P('wide', 'narrow'), may hold values from -0.09375 to 0.09375
- space_bias: float32 [16, 961], replicated, may hold values from -4 to 4
- joint_modulate: bfloat16 [1024, 6144], P('wide', 'narrow'), may hold values from -0.1875 to 0.1875
- joint_project: bfloat16 [1024, 3072], P('wide', 'narrow'), may hold values from -0.1875 to 0.1875
- joint_output: bfloat16 [1024, 1024], P('wide', 'narrow'), may hold values from -0.75 to 0.75
- joint_expand: bfloat16 [1024, 4096], P('wide', 'narrow'), may hold values from -0.1875 to 0.1875
- joint_reduce: bfloat16 [4096, 1024], P('wide', 'narrow'), may hold values from -0.09375 to 0.09375
- joint_bias: float32 [16, 2025], replicated, may hold values from -4 to 4
- cotangent: bfloat16 [18432, 1024], P(('wide', 'narrow')), may hold values from -6 to 6
Outputs:
- output_tokens: bfloat16 [18432, 1024], P(('wide', 'narrow'))
- grad_tokens: float32 [18432, 1024], P(('wide', 'narrow'))
- grad_space_modulate: float32 [1024, 6144], P('wide', 'narrow')
- grad_space_project: float32 [1024, 3072], P('wide', 'narrow')
- grad_space_output: float32 [1024, 1024], P('wide', 'narrow')
- grad_space_expand: float32 [1024, 4096], P('wide', 'narrow')
- grad_space_reduce: float32 [4096, 1024], P('wide', 'narrow')
- grad_space_bias: float32 [16, 961], replicated
- grad_joint_modulate: float32 [1024, 6144], P('wide', 'narrow')
- grad_joint_project: float32 [1024, 3072], P('wide', 'narrow')
- grad_joint_output: float32 [1024, 1024], P('wide', 'narrow')
- grad_joint_expand: float32 [1024, 4096], P('wide', 'narrow')
- grad_joint_reduce: float32 [4096, 1024], P('wide', 'narrow')
- grad_joint_bias: float32 [16, 2025], replicated
Inputs may be any that keep to these rules, and one draw needn't show every extreme that they name: Image slots 0 to image_count[w] - 1 of group w hold images, the others are ignored; some group has all 1 slots live.
All inputs are finite; a program needn't handle non-finite values.
Results may differ from a plain program's by a relative error of at most 0.03.
The roundings to bfloat16 on the way count: a program that leaves them out, or rounds other values in their place, can miss the bound.
Values may be sent and summed in bfloat16 or wider, within the bound.
A program may use at most 448 MiB of HBM per device.

v0:
```python
import jax
import jax.numpy as jnp
import numpy as np
from jax import lax
from jax.sharding import PartitionSpec as P

D = 1024
HEADS = 16
HEAD_DIM = 64
SW = 8
TW = 5
CLIP_DEV = 1
IMG_DEV = 1


epsilon = 1e-06


def layer_norm(values):
    centred = values - jnp.mean(values, axis=-1, keepdims=True)
    spread = jnp.mean(centred * centred, axis=-1, keepdims=True)
    return centred * lax.rsqrt(spread + epsilon)


def gelu_exact(values):
    return jax.nn.gelu(values, approximate=False)


def spread_rows(per_sequence):
    repeats = np.array([TW * SW * SW] * CLIP_DEV + [4 * SW * SW] * IMG_DEV)
    return jnp.repeat(
        per_sequence,
        repeats,
        axis=0,
        total_repeat_length=CLIP_DEV * TW * SW * SW + 4 * IMG_DEV * SW * SW,
    )


def collapse(row_values):
    clip_rows = CLIP_DEV * TW * SW * SW
    clip_part = jnp.sum(row_values[:clip_rows].reshape(CLIP_DEV, TW * SW * SW, -1), axis=1)
    image_part = jnp.sum(row_values[clip_rows:].reshape(IMG_DEV, 4 * SW * SW, -1), axis=1)
    return jnp.concatenate([clip_part, image_part], axis=0)


def live_rows(live_count):
    slot_live = (jnp.arange(IMG_DEV) < live_count).astype(jnp.float32)
    return jnp.concatenate(
        [jnp.ones((CLIP_DEV * TW * SW * SW,), jnp.float32), jnp.repeat(slot_live, 4 * SW * SW)]
    )


def premix(residual, modseq, offset):
    mod_rows = spread_rows(modseq[:, offset * D : (offset + 2) * D])
    return layer_norm(residual) * (1.0 + mod_rows[:, D:]) + mod_rows[:, :D]


def space_index(query_quarter, query_cells):
    key_quarter = jnp.repeat(jnp.arange(4), SW * SW)
    key_cells = jnp.tile(jnp.arange(SW * SW), 4)
    span_side = 4 * SW - 1
    row_gap = (query_quarter // 2 * SW + query_cells // SW)[:, None] - (
        key_quarter // 2 * SW + key_cells // SW
    )[None, :]
    col_gap = (query_quarter % 2 * SW + query_cells % SW)[:, None] - (
        key_quarter % 2 * SW + key_cells % SW
    )[None, :]
    return (row_gap + 2 * SW - 1) * span_side + col_gap + 2 * SW - 1


def joint_index(frames):
    cell_ids = jnp.arange(frames * SW * SW)
    frame_pos = cell_ids // (SW * SW)
    row_pos = cell_ids // SW % SW
    col_pos = cell_ids % SW
    span_side = 2 * SW - 1
    frame_gap = frame_pos[:, None] - frame_pos[None, :] + TW - 1
    row_gap = row_pos[:, None] - row_pos[None, :] + SW - 1
    col_gap = col_pos[:, None] - col_pos[None, :] + SW - 1
    return (frame_gap * span_side + row_gap) * span_side + col_gap


def attend(queries, key_rows, values, rel_bias):
    win_count, query_len, key_len = (queries.shape[0], queries.shape[1], key_rows.shape[1])
    query_heads = queries.reshape(win_count, query_len, HEADS, HEAD_DIM)
    key_heads = key_rows.reshape(win_count, key_len, HEADS, HEAD_DIM)
    value_heads = values.reshape(win_count, key_len, HEADS, HEAD_DIM)
    scores = (
        jnp.einsum("wqhd,wkhd->whqk", query_heads, key_heads, preferred_element_type=jnp.float32)
        * HEAD_DIM ** (-0.5)
        + rel_bias[None]
    )
    row_top = jnp.max(scores, axis=-1, keepdims=True)
    powered = jnp.exp(scores - row_top)
    softmaxed = powered / jnp.sum(powered, axis=-1, keepdims=True)
    attended = jnp.einsum(
        "whqk,wkhd->wqhd",
        softmaxed.astype(jnp.bfloat16),
        value_heads,
        preferred_element_type=jnp.float32,
    )
    return (softmaxed, attended.reshape(win_count, query_len, D).astype(jnp.bfloat16))


def attend_back(queries, key_rows, values, softmaxed, grad_attended):
    win_count, query_len, key_len = (queries.shape[0], queries.shape[1], key_rows.shape[1])
    scaling = HEAD_DIM ** (-0.5)
    query_heads = queries.reshape(win_count, query_len, HEADS, HEAD_DIM)
    key_heads = key_rows.reshape(win_count, key_len, HEADS, HEAD_DIM)
    value_heads = values.reshape(win_count, key_len, HEADS, HEAD_DIM)
    grad_heads = grad_attended.reshape(win_count, query_len, HEADS, HEAD_DIM)
    grad_values = jnp.einsum(
        "whqk,wqhd->wkhd",
        softmaxed.astype(jnp.bfloat16),
        grad_heads,
        preferred_element_type=jnp.float32,
    )
    grad_probs = jnp.einsum(
        "wqhd,wkhd->whqk", grad_heads, value_heads, preferred_element_type=jnp.float32
    )
    grad_scores = (
        softmaxed * (grad_probs - jnp.sum(softmaxed * grad_probs, axis=-1, keepdims=True))
    ).astype(jnp.bfloat16)
    grad_queries = (
        jnp.einsum("whqk,wkhd->wqhd", grad_scores, key_heads, preferred_element_type=jnp.float32)
        * scaling
    )
    grad_keys = (
        jnp.einsum("whqk,wqhd->wkhd", grad_scores, query_heads, preferred_element_type=jnp.float32)
        * scaling
    )
    grad_bias = jnp.sum(grad_scores.astype(jnp.float32), axis=0)
    return (
        grad_queries.reshape(win_count, query_len, D),
        grad_keys.reshape(win_count, key_len, D),
        grad_values.reshape(win_count, key_len, D),
        grad_bias,
    )


def space_attention(triple, lookup, quarter, source):
    win_count = triple.shape[0] // (SW * SW)
    queries = triple[:, :D].reshape(win_count, SW * SW, D)
    gathered = source(triple[:, D:].reshape(win_count, SW * SW, 2 * D))
    bias_index = space_index(jnp.full((SW * SW,), quarter), jnp.arange(SW * SW))
    softmaxed, attended = attend(
        queries, gathered[..., :D], gathered[..., D:], lookup[:, bias_index]
    )
    return (attended.reshape(-1, D), (gathered, softmaxed))


def space_back(triple, stored, lookup, quarter, grad_attended):
    gathered, softmaxed = stored
    win_count = triple.shape[0] // (SW * SW)
    queries = triple[:, :D].reshape(win_count, SW * SW, D)
    grad_queries, grad_keys, grad_values, grad_bias = attend_back(
        queries,
        gathered[..., :D],
        gathered[..., D:],
        softmaxed,
        grad_attended.reshape(win_count, SW * SW, D),
    )
    own_grads = lax.psum_scatter(
        jnp.concatenate([grad_keys, grad_values], axis=-1).astype(jnp.bfloat16),
        "narrow",
        scatter_dimension=1,
        tiled=True,
    ).astype(jnp.float32)
    grad_triple = jnp.concatenate(
        [grad_queries.reshape(-1, D), own_grads.reshape(-1, 2 * D)], axis=1
    ).astype(jnp.bfloat16)
    bias_index = space_index(jnp.full((SW * SW,), quarter), jnp.arange(SW * SW))
    _, bias_back = jax.vjp(lambda values: values[:, bias_index], lookup)
    return (grad_triple, bias_back(grad_bias)[0])


def joint_attention(triple, lookup):
    clip_rows = CLIP_DEV * TW * SW * SW
    clip_triple = triple[:clip_rows].reshape(CLIP_DEV, TW * SW * SW, 3 * D)
    image_triple = triple[clip_rows:].reshape(4 * IMG_DEV, SW * SW, 3 * D)
    clip_probs, clip_out = attend(
        clip_triple[..., :D],
        clip_triple[..., D : 2 * D],
        clip_triple[..., 2 * D :],
        lookup[:, joint_index(TW)],
    )
    image_probs, image_out = attend(
        image_triple[..., :D],
        image_triple[..., D : 2 * D],
        image_triple[..., 2 * D :],
        lookup[:, joint_index(1)],
    )
    return (
        jnp.concatenate([clip_out.reshape(-1, D), image_out.reshape(-1, D)], axis=0),
        (clip_probs, image_probs),
    )


def joint_back(triple, stored, lookup, grad_attended):
    clip_probs, image_probs = stored
    clip_rows = CLIP_DEV * TW * SW * SW
    clip_triple = triple[:clip_rows].reshape(CLIP_DEV, TW * SW * SW, 3 * D)
    image_triple = triple[clip_rows:].reshape(4 * IMG_DEV, SW * SW, 3 * D)
    clip_grads = attend_back(
        clip_triple[..., :D],
        clip_triple[..., D : 2 * D],
        clip_triple[..., 2 * D :],
        clip_probs,
        grad_attended[:clip_rows].reshape(CLIP_DEV, TW * SW * SW, D),
    )
    image_grads = attend_back(
        image_triple[..., :D],
        image_triple[..., D : 2 * D],
        image_triple[..., 2 * D :],
        image_probs,
        grad_attended[clip_rows:].reshape(4 * IMG_DEV, SW * SW, D),
    )
    clip_part = jnp.concatenate([clip_grads[0], clip_grads[1], clip_grads[2]], axis=-1).reshape(
        -1, 3 * D
    )
    image_part = jnp.concatenate([image_grads[0], image_grads[1], image_grads[2]], axis=-1).reshape(
        -1, 3 * D
    )
    grad_triple = jnp.concatenate([clip_part, image_part], axis=0).astype(jnp.bfloat16)
    _, bias_back = jax.vjp(
        lambda values: (values[:, joint_index(TW)], values[:, joint_index(1)]), lookup
    )
    return (grad_triple, bias_back((clip_grads[3], image_grads[3]))[0])


def block_forward(residual, modseq, weights, attention):
    modulate, project, output, expand, shrink = weights
    normed = premix(residual, modseq, 0).astype(jnp.bfloat16)
    triple = jnp.dot(normed, project, preferred_element_type=jnp.float32).astype(jnp.bfloat16)
    attended, attention_saved = attention(triple)
    branch = jnp.dot(attended, output, preferred_element_type=jnp.float32)
    middle = residual + spread_rows(modseq[:, 2 * D : 3 * D]) * branch
    normed_two = premix(middle, modseq, 3).astype(jnp.bfloat16)
    before = jnp.dot(normed_two, expand, preferred_element_type=jnp.float32)
    active = gelu_exact(before).astype(jnp.bfloat16)
    reduced = jnp.dot(active, shrink, preferred_element_type=jnp.float32)
    result = middle + spread_rows(modseq[:, 5 * D :]) * reduced
    return (
        result,
        (
            normed,
            triple,
            attention_saved,
            attended,
            branch,
            middle,
            normed_two,
            before,
            active,
            reduced,
        ),
    )


def block_backward(residual, modseq, cond_low, weights, stored, grad_result, attention_back):
    modulate, project, output, expand, shrink = weights
    (
        normed,
        triple,
        attention_saved,
        attended,
        branch,
        middle,
        normed_two,
        before,
        active,
        reduced,
    ) = stored
    gate_one = spread_rows(modseq[:, 2 * D : 3 * D])
    gate_two = spread_rows(modseq[:, 5 * D :])
    grad_reduced = (gate_two * grad_result).astype(jnp.bfloat16)
    grad_shrink = jnp.einsum("rf,rd->fd", active, grad_reduced, preferred_element_type=jnp.float32)
    grad_active = jnp.einsum("rd,fd->rf", grad_reduced, shrink, preferred_element_type=jnp.float32)
    _, gelu_back = jax.vjp(gelu_exact, before)
    grad_before = gelu_back(grad_active)[0].astype(jnp.bfloat16)
    grad_expand = jnp.einsum(
        "rd,rf->df", normed_two, grad_before, preferred_element_type=jnp.float32
    )
    grad_normed_two = jnp.einsum(
        "rf,df->rd", grad_before, expand, preferred_element_type=jnp.float32
    )
    _, second_back = jax.vjp(
        lambda inner_rows, table_mod: premix(inner_rows, table_mod, 3), middle, modseq
    )
    grad_inner, grad_mod_two = second_back(grad_normed_two)
    grad_middle = grad_inner + grad_result
    grad_branch = (gate_one * grad_middle).astype(jnp.bfloat16)
    grad_output = jnp.einsum("rd,re->de", attended, grad_branch, preferred_element_type=jnp.float32)
    grad_attended = jnp.einsum(
        "re,de->rd", grad_branch, output, preferred_element_type=jnp.float32
    ).astype(jnp.bfloat16)
    grad_triple, grad_lookup = attention_back(triple, attention_saved, grad_attended)
    grad_project = jnp.einsum("rd,re->de", normed, grad_triple, preferred_element_type=jnp.float32)
    grad_normed = jnp.einsum("re,de->rd", grad_triple, project, preferred_element_type=jnp.float32)
    _, first_back = jax.vjp(
        lambda inner_rows, table_mod: premix(inner_rows, table_mod, 0), residual, modseq
    )
    grad_residual, grad_mod_one = first_back(grad_normed)
    grad_modseq = grad_mod_one + grad_mod_two
    grad_modseq = grad_modseq.at[:, 2 * D : 3 * D].add(collapse(branch * grad_middle))
    grad_modseq = grad_modseq.at[:, 5 * D :].add(collapse(reduced * grad_result))
    grad_modulate = jnp.einsum(
        "sc,sm->cm", cond_low.astype(jnp.float32), grad_modseq, precision=lax.Precision.HIGHEST
    )
    return (
        grad_residual + grad_middle,
        (grad_modulate, grad_project, grad_output, grad_expand, grad_shrink),
        grad_lookup,
    )


def collect_weights(shards):
    partial_rows = (
        lax.all_gather(shards[0], "narrow", axis=1, tiled=True),
        lax.all_gather(shards[1], "narrow", axis=1, tiled=True),
        lax.all_gather(shards[2], "narrow", axis=1, tiled=True),
        lax.all_gather(shards[3], "narrow", axis=1, tiled=True),
        lax.all_gather(shards[4], "narrow", axis=1, tiled=True),
    )
    return (
        lax.all_gather(partial_rows[0], "wide", axis=0, tiled=True),
        lax.all_gather(partial_rows[1], "wide", axis=0, tiled=True),
        lax.all_gather(partial_rows[2], "wide", axis=0, tiled=True),
        lax.all_gather(partial_rows[3], "wide", axis=0, tiled=True),
        lax.all_gather(partial_rows[4], "wide", axis=0, tiled=True),
    )


def settle(grads):
    partial_rows = (
        lax.psum_scatter(grads[0], "wide", scatter_dimension=0, tiled=True),
        lax.psum_scatter(grads[1], "wide", scatter_dimension=0, tiled=True),
        lax.psum_scatter(grads[2], "wide", scatter_dimension=0, tiled=True),
        lax.psum_scatter(grads[3], "wide", scatter_dimension=0, tiled=True),
        lax.psum_scatter(grads[4], "wide", scatter_dimension=0, tiled=True),
    )
    return (
        lax.psum_scatter(
            partial_rows[0].astype(jnp.bfloat16), "narrow", scatter_dimension=1, tiled=True
        ).astype(jnp.float32),
        lax.psum_scatter(
            partial_rows[1].astype(jnp.bfloat16), "narrow", scatter_dimension=1, tiled=True
        ).astype(jnp.float32),
        lax.psum_scatter(
            partial_rows[2].astype(jnp.bfloat16), "narrow", scatter_dimension=1, tiled=True
        ).astype(jnp.float32),
        lax.psum_scatter(
            partial_rows[3].astype(jnp.bfloat16), "narrow", scatter_dimension=1, tiled=True
        ).astype(jnp.float32),
        lax.psum_scatter(
            partial_rows[4].astype(jnp.bfloat16), "narrow", scatter_dimension=1, tiled=True
        ).astype(jnp.float32),
    )


def body(
    tokens,
    clip_cond,
    image_cond,
    image_count,
    space_modulate,
    space_project,
    space_output,
    space_expand,
    space_reduce,
    space_bias,
    joint_modulate,
    joint_project,
    joint_output,
    joint_expand,
    joint_reduce,
    joint_bias,
    cotangent,
):
    quarter = lax.axis_index("narrow")
    group_index = lax.axis_index("wide")
    space_shards = (space_modulate, space_project, space_output, space_expand, space_reduce)
    joint_shards = (joint_modulate, joint_project, joint_output, joint_expand, joint_reduce)
    clip_start = group_index // 4 * CLIP_DEV
    own_clips = lax.dynamic_slice_in_dim(clip_cond, clip_start, CLIP_DEV, 0)
    cond_low = jax.nn.silu(
        jnp.concatenate([own_clips, image_cond], axis=0).astype(jnp.float32)
    ).astype(jnp.bfloat16)
    row_live = live_rows(image_count[0])[:, None]
    residual = tokens.astype(jnp.float32)

    def first_source(key_values):
        return lax.all_gather(key_values, "narrow", axis=1, tiled=True)

    def joint_forward_attention(triple):
        return joint_attention(triple, joint_bias)

    def joint_backward_attention(triple, stored, grad_attended):
        return joint_back(triple, stored, joint_bias, grad_attended)

    def space_backward_attention(triple, stored, grad_attended):
        return space_back(triple, stored, space_bias, quarter, grad_attended)

    space_weights = collect_weights(space_shards)
    space_mod = jnp.dot(cond_low, space_weights[0], preferred_element_type=jnp.float32)
    middle_residual, space_first = block_forward(
        residual,
        space_mod,
        space_weights,
        lambda triple: space_attention(triple, space_bias, quarter, first_source),
    )
    joint_weights = collect_weights(joint_shards)
    joint_mod = jnp.dot(cond_low, joint_weights[0], preferred_element_type=jnp.float32)
    final_residual, joint_first = block_forward(
        middle_residual, joint_mod, joint_weights, joint_forward_attention
    )
    output_tokens = (final_residual * row_live).astype(jnp.bfloat16)
    grad_final = cotangent.astype(jnp.float32) * row_live
    grad_middle, joint_grads, joint_bias_grad = block_backward(
        middle_residual,
        joint_mod,
        cond_low,
        joint_weights,
        joint_first,
        grad_final,
        joint_backward_attention,
    )
    joint_local = settle(joint_grads)
    grad_tokens, space_grads, space_bias_grad = block_backward(
        residual,
        space_mod,
        cond_low,
        space_weights,
        space_first,
        grad_middle,
        space_backward_attention,
    )
    space_local = settle(space_grads)
    totals = lax.psum((space_bias_grad, joint_bias_grad), ("wide", "narrow"))
    return (
        output_tokens,
        grad_tokens,
        space_local[0],
        space_local[1],
        space_local[2],
        space_local[3],
        space_local[4],
        totals[0],
        joint_local[0],
        joint_local[1],
        joint_local[2],
        joint_local[3],
        joint_local[4],
        totals[1],
    )


def solution(mesh):
    in_specs = (
        P(("wide", "narrow"), None),
        P(),
        P("wide", None),
        P("wide"),
        P("wide", "narrow"),
        P("wide", "narrow"),
        P("wide", "narrow"),
        P("wide", "narrow"),
        P("wide", "narrow"),
        P(),
        P("wide", "narrow"),
        P("wide", "narrow"),
        P("wide", "narrow"),
        P("wide", "narrow"),
        P("wide", "narrow"),
        P(),
        P(("wide", "narrow"), None),
    )
    out_specs = (
        P(("wide", "narrow"), None),
        P(("wide", "narrow"), None),
        P("wide", "narrow"),
        P("wide", "narrow"),
        P("wide", "narrow"),
        P("wide", "narrow"),
        P("wide", "narrow"),
        P(),
        P("wide", "narrow"),
        P("wide", "narrow"),
        P("wide", "narrow"),
        P("wide", "narrow"),
        P("wide", "narrow"),
        P(),
    )
    return jax.shard_map(body, mesh=mesh, in_specs=in_specs, out_specs=out_specs, check_vma=False)
```

profile of v0, /device:TPU:0, one launch (start us, length us, event | category | flops | bytes accessed | tf_op | source)
XLA Modules:
  0.0 2896.5 jit_solution(16550100194361603248)
XLA Ops:
  8.7 40.7 %all-gather.18.cloned.1.call-done = bf16[128,6144]{1,0:T(8,128)(2,1)} async-done(((bf16[128,1536]{1,0:T(8,128)(2,1)}), bf16[128,6144]{1,0:T(8,128)(2,1)}) %all-gather.18.cloned.1.call-update) | async-done | bytes 1572880 | tf_op jit(solution)/shard_map/all_gather | solution.py:319
  49.5 23.7 all_gather.65
  75.9 16.6 all-gather.36.cloned.1.call-done
  93.5 72.5 %all-gather.20.cloned.1.call-done = bf16[1024,6144]{1,0:T(8,128)(2,1)} async-done(((bf16[128,6144]{1,0:T(8,128)(2,1)}), bf16[1024,6144]{1,0:T(8,128)(2,1)}) %all-gather.20.cloned.1.call-update) | async-done | bytes 12582928 | tf_op jit(solution)/shard_map/all_gather | solution.py:326
  179.3 34.0 %all-gather.22.cloned.1.call-done = bf16[1024,3072]{1,0:T(8,128)(2,1)} async-done(((bf16[128,3072]{1,0:T(8,128)(2,1)}), bf16[1024,3072]{1,0:T(8,128)(2,1)}) %all-gather.22.cloned.1.call-update) | async-done | bytes 6291472 | tf_op jit(solution)/shard_map/all_gather | solution.py:327
  222.8 17.0 all_gather.68
  246.9 31.1 %all-gather.32.cloned.1.call-done = bf16[512,1024]{1,0:T(8,128)(2,1)} async-done(((bf16[512,256]{1,0:T(8,128)(2,1)}), bf16[512,1024]{1,0:T(8,128)(2,1)}) %all-gather.32.cloned.1.call-update) | async-done | bytes 1048592 | tf_op jit(solution)/shard_map/all_gather | solution.py:323
  278.1 25.0 all_gather.76
  303.2 16.4 all_gather.78
  321.5 54.8 %gather_fusion = f32[16384,16]{1,0:T(8,128)} fusion(f32[16,961]{0,1:T(8,128)S(1)} %copy.186, s32[16384]{0:T(1024)S(1)} %broadcast_clamp_fusion.1), kind=kCustom, calls=%fused_computation.12 | custom fusion | bytes 2162688 | tf_op jit(solution)/shard_map/gather | solution.py:147
  382.1 14.2 gather_fusion.2
  400.5 338.8 %gather_fusion.1 = f32[102400,16]{1,0:T(8,128)} fusion(f32[16,2025]{0,1:T(8,128)S(1)} %copy.192, s32[102400]{0:T(1024)S(1)} %broadcast_clamp_fusion), kind=kCustom, calls=%fused_computation.13 | custom fusion | bytes 13516800 | tf_op jit(solution)/shard_map/gather | solution.py:185
  739.3 34.9 %copy.194 = f32[320,320,16]{0,1,2:T(8,128)} copy(f32[320,320,16]{2,1,0:T(8,128)} %bitcast.178) | data formatting | bytes 13107200 | tf_op jit(solution)/shard_map/gather | solution.py:185
  816.1 8.9 fusion.151
  838.8 9.8 fusion.158
  849.2 8.1 convert_bitcast_fusion.1
  874.2 29.1 %multiply_convert_fusion.3 = (bf16[576,4096]{1,0:T(8,128)(2,1)}, f32[576,4096]{1,0:T(8,128)}, f32[576,4096]{1,0:T(8,128)}) fusion(bf16[576,1024]{1,0:T(8,128)(2,1)S(1)} %fusion.49, bf16[1024,4096]{1,0:T(8,128)(2,1)} %all-gather.30.cloned.1.call-done), kind=kOutput, calls=%fused_computation.49 | convolution fusion | flops 4985192448 | bytes 33161216 | tf_op jit(solution)/shard_map/dot_general | solution.py:239
  903.4 10.6 fusion.148
  916.6 7.5 convolution_convert_fusion
  949.9 8.6 fusion.67
  967.7 10.8 fusion.161
  978.5 29.9 %add_convert_fusion.1 = (bf16[576,4096]{1,0:T(8,128)(2,1)S(1)}, f32[576,4096]{1,0:T(8,128)}) fusion(f32[576,4096]{1,0:T(8,128)} %fusion.161, bf16[576,1024]{1,0:T(8,128)(2,1)S(1)} %copy-done.70, bf16[4096,1024]{1,0:T(8,128)(2,1)} %all-gather.50.cloned.1.call-done), kind=kOutput, calls=%fused_computation.35 | convolution fusion | flops 5001707520 | bytes 33161216 | tf_op jit(solution)/shard_map/rd,fd->rf/dot_general | solution.py:278
  1008.5 9.1 multiply_reduce_fusion.4
  1017.6 11.0 multiply_convert_fusion.2
  1028.6 15.8 fusion.50
  1061.9 8.6 fusion.70
  1098.7 10.1 multiply_reduce_fusion.3
  1119.4 16.3 add_convert_fusion
  1135.8 9.3 multiply_reduce_fusion.2
  1161.8 8.2 convolution_convert_fusion.2
  1170.5 8.0 multiply_reduce_fusion
  1185.2 9.2 convert_reduce_fusion
  1204.6 7.7 pad_maximum_fusion
  1225.7 11.2 fusion.40
  1238.1 12.8 fusion.163
  1252.1 12.6 fusion.164
  1266.0 12.5 fusion.165
  1279.8 12.7 fusion.166
  1304.4 68.8 %reduce-scatter.22.cloned.1.call-done = bf16[9,64,2048]{2,1,0:T(8,128)(2,1)} async-done(((bf16[9,256,2048]{2,1,0:T(8,128)(2,1)}), bf16[9,64,2048]{2,1,0:T(8,128)(2,1)}) %reduce-scatter.22.cloned.1.call-update) | async-done | bytes 2359312 | tf_op jit(solution)/shard_map/reduce_scatter | solution.py:163
  1373.2 9.6 fusion.54
  1384.4 38.1 %scatter_custom_fusion.4 = f32[2,2048]{1,0:T(2,128)S(1)} fusion(s32[576]{0:T(1024)} %constant.1053, f32[576,1024]{1,0:T(8,128)} %get-tuple-element.365, f32[]{:T(128)} %constant.814.clone.1, f32[576,1024]{1,0:T(8,128)S(1)} %copy-done.58), kind=kCustom, calls=%fused_computation.72 | custom fusion | flops 2359296 | bytes 4736000 | tf_op jit(solution)/shard_map/transpose(jvp(jit(_take)))/scatter-add | solution.py:31
  1422.5 38.7 %scatter_custom_fusion.3 = f32[2,2048]{1,0:T(2,128)S(1)} fusion(s32[576]{0:T(1024)} %constant.1053, f32[576,1024]{1,0:T(8,128)} %get-tuple-element.358, f32[]{:T(128)} %constant.814.clone.1, f32[576,1024]{1,0:T(8,128)} %copy-done.33), kind=kCustom, calls=%fused_computation.76 | custom fusion | flops 2359296 | bytes 4736000 | tf_op jit(solution)/shard_map/transpose(jvp(jit(_take)))/scatter-add | solution.py:31
  1463.7 13.5 fusion.131
  1477.3 38.2 %scatter_custom_fusion.1 = f32[2,2048]{1,0:T(2,128)S(1)} fusion(s32[576]{0:T(1024)} %constant.1053, f32[576,1024]{1,0:T(8,128)} %get-tuple-element.360, f32[]{:T(128)} %constant.814.clone.1, f32[576,1024]{1,0:T(8,128)} %copy-done.34), kind=kCustom, calls=%fused_computation.80 | custom fusion | flops 2359296 | bytes 4736000 | tf_op jit(solution)/shard_map/transpose(jvp(jit(_take)))/scatter-add | solution.py:31
  1519.4 7.8 fusion.45
  1530.5 38.0 %scatter_custom_fusion = f32[2,2048]{1,0:T(2,128)S(1)} fusion(s32[576]{0:T(1024)} %constant.1053, f32[576,1024]{1,0:T(8,128)} %get-tuple-element.362, f32[]{:T(128)} %constant.814.clone.1, f32[576,1024]{1,0:T(8,128)S(1)} %get-tuple-element.407), kind=kCustom, calls=%fused_computation.84 | custom fusion | flops 2359296 | bytes 4736000 | tf_op jit(solution)/shard_map/transpose(jvp(jit(_take)))/scatter-add | solution.py:31
  1569.3 13.5 fusion.133
  1585.6 22.7 scatter_custom_fusion.5
  1608.3 32.1 %copy.251 = f32[320,320,16]{2,1,0:T(8,128)} copy(f32[320,320,16]{0,1,2:T(8,128)} %get-tuple-element.328) | data formatting | bytes 13107200 | tf_op jit(solution)/shard_map/convert_element_type | solution.py:132
  1640.4 542.5 %scatter_custom_fusion.6 = f32[16,2025]{0,1:T(8,128)S(1)} fusion(s32[102400]{0:T(1024)} %copy-done.66, f32[102400,16]{1,0:T(8,128)} %bitcast.179, f32[]{:T(128)} %constant.814.clone.1), kind=kCustom, calls=%fused_computation.205 | custom fusion | flops 1638400 | bytes 130112 | tf_op jit(solution)/shard_map/transpose(jvp())/scatter-add | solution.py:226
  2205.2 108.7 %reduce-scatter.44.cloned.1.call-done = f32[128,6144]{1,0:T(8,128)} async-done(((f32[1024,6144]{1,0:T(8,128)}), f32[128,6144]{1,0:T(8,128)}) %reduce-scatter.44.cloned.1.call-update) | async-done | bytes 3145744 | tf_op jit(solution)/shard_map/reduce_scatter | solution.py:336
  2317.3 157.2 %reduce-scatter.24.cloned.1.call-done = f32[128,6144]{1,0:T(8,128)} async-done(((f32[1024,6144]{1,0:T(8,128)}), f32[128,6144]{1,0:T(8,128)}) %reduce-scatter.24.cloned.1.call-update) | async-done | bytes 3145744 | tf_op jit(solution)/shard_map/reduce_scatter | solution.py:336
  2482.7 87.8 %scatter_custom_fusion.2 = f32[16,961]{0,1:T(8,128)S(1)} fusion(s32[16384]{0:T(1024)} %bitcast.232, f32[16384,16]{1,0:T(8,128)} %bitcast.203, f32[]{:T(128)} %constant.814.clone.1), kind=kCustom, calls=%fused_computation.209 | custom fusion | flops 262144 | bytes 62016 | tf_op jit(solution)/shard_map/transpose(jvp())/scatter-add | solution.py:173
  2570.5 46.4 %psum.14 = f32[16,961]{0,1:T(8,128)S(1)} all-reduce(f32[16,961]{0,1:T(8,128)S(1)} %scatter_custom_fusion.2), channel_id=1, replica_groups=mesh['wide'=8,'narrow'=4] {'wide','narrow'}, use_global_device_ids=true, to_apply=%region_109.113 | all-reduce | flops 15376 | bytes 123008 | tf_op jit(solution)/shard_map/psum | solution.py:439
  2619.9 10.8 reduce-scatter.34.cloned.1.call-done
  2632.2 19.4 reduce-scatter.54.cloned.1.call-done
  2656.5 19.6 reduce-scatter.50.cloned.1.call-done
  2677.9 27.0 reduce-scatter.38.cloned.1.call-done
  2706.6 26.3 reduce-scatter.42.cloned.1.call-done
  2734.7 26.4 reduce-scatter.58.cloned.1.call-done
  2763.0 26.2 reduce-scatter.62.cloned.1.call-done
  2790.9 23.0 reduce-scatter.30.cloned.1.call-done
  2815.7 35.3 %reduce-scatter.46.cloned.1.call-done = bf16[128,1536]{1,0:T(8,128)(2,1)} async-done(((bf16[128,6144]{1,0:T(8,128)(2,1)}), bf16[128,1536]{1,0:T(8,128)(2,1)}) %reduce-scatter.46.cloned.1.call-update) | async-done | bytes 393232 | tf_op jit(solution)/shard_map/reduce_scatter | solution.py:343
  2852.9 34.6 %reduce-scatter.26.cloned.1.call-done = bf16[128,1536]{1,0:T(8,128)(2,1)} async-done(((bf16[128,6144]{1,0:T(8,128)(2,1)}), bf16[128,1536]{1,0:T(8,128)(2,1)}) %reduce-scatter.26.cloned.1.call-update) | async-done | bytes 393232 | tf_op jit(solution)/shard_map/reduce_scatter | solution.py:343
  (556 shorter events, 348.9 us)
Async XLA Ops:
  7.2 85.5 %copy-start = (bf16[2,1024]{1,0:T(2,128)(2,1)S(1)}, bf16[2,1024]{1,0:T(2,128)(2,1)}, u32[]{:S(2)}) copy-start(bf16[2,1024]{1,0:T(2,128)(2,1)} %param.80) | copy-start | bytes 12292
  7.2 85.5 %copy-start.118 = (s32[576]{0:T(1024)S(1)}, s32[576]{0:T(1024)}, u32[]{:S(2)}) copy-start(s32[576]{0:T(1024)} %constant.1053) | copy-start | bytes 6916
  7.2 85.5 %copy-start.8 = (bf16[576,1024]{1,0:T(8,128)(2,1)S(1)}, bf16[576,1024]{1,0:T(8,128)(2,1)}, u32[]{:S(2)}) copy-start(bf16[576,1024]{1,0:T(8,128)(2,1)} %param.79) | copy-start | bytes 3538948
  7.2 42.2 %all-gather.18.cloned.1.call-start = ((), (), s32[]{:S(2)}) async-start(), calls=%async_computation.21 | async-start | bytes 1966080 | tf_op jit(solution)/shard_map/all_gather | solution.py:319
  8.0 84.6 %all-gather.36.cloned.1.call-start = ((), (), s32[]{:S(2)}) async-start(), calls=%async_computation.30 | async-start | bytes 1966080 | tf_op jit(solution)/shard_map/all_gather | solution.py:319
  8.7 157.3 %all-gather.20.cloned.1.call-start = ((), (), s32[]{:S(2)}) async-start(), calls=%async_computation.22 | async-start | bytes 14155776 | tf_op jit(solution)/shard_map/all_gather | solution.py:326
  49.5 116.5 %copy-start.92 = (bf16[1,1024]{1,0:T(2,128)(2,1)S(1)}, bf16[1,1024]{1,0:T(2,128)(2,1)}, u32[]{:S(2)}) copy-start(bf16[1,1024]{1,0:T(2,128)(2,1)} %param.81) | copy-start | bytes 6148
  49.5 163.8 %all-gather.22.cloned.1.call-start = ((), (), s32[]{:S(2)}) async-start(), calls=%async_computation.23 | async-start | bytes 7077888 | tf_op jit(solution)/shard_map/all_gather | solution.py:327
  73.2 173.6 %all-gather.28.cloned.1.call-start = ((), (), s32[]{:S(2)}) async-start(), calls=%async_computation.26 | async-start | bytes 1310720 | tf_op jit(solution)/shard_map/all_gather | solution.py:322
  73.8 204.2 %all-gather.32.cloned.1.call-start = ((), (), s32[]{:S(2)}) async-start(), calls=%async_computation.28 | async-start | bytes 1310720 | tf_op jit(solution)/shard_map/all_gather | solution.py:323
  74.4 245.3 %all-gather.44.cloned.1.call-start = ((), (), s32[]{:S(2)}) async-start(), calls=%async_computation.34 | async-start | bytes 1310720 | tf_op jit(solution)/shard_map/all_gather | solution.py:322
  75.2 699.0 %all-gather.48.cloned.1.call-start = ((), (), s32[]{:S(2)}) async-start(), calls=%async_computation.36 | async-start | bytes 1310720 | tf_op jit(solution)/shard_map/all_gather | solution.py:323
  75.9 698.7 %all-gather.38.cloned.1.call-start = ((), (), s32[]{:S(2)}) async-start(), calls=%async_computation.31 | async-start | bytes 14155776 | tf_op jit(solution)/shard_map/all_gather | solution.py:326
  92.6 723.5 %all-gather.24.cloned.1.call-start = ((), (), s32[]{:S(2)}) async-start(), calls=%async_computation.24 | async-start | bytes 11796480 | tf_op jit(solution)/shard_map/all_gather | solution.py:393
  92.7 681.9 %copy-start.88 = (bf16[1,1024]{1,0:T(2,128)(2,1)}, bf16[1,1024]{1,0:T(2,128)(2,1)S(1)}, u32[]{:S(2)}) copy-start(bf16[1,1024]{1,0:T(2,128)(2,1)S(1)} %constant_dynamic-slice_fusion) | copy-start | bytes 6148
  93.0 83.2 %copy-start.94 = (f32[576]{0:T(1024)}, f32[576]{0:T(1024)S(1)}, u32[]{:S(2)}) copy-start(f32[576]{0:T(1024)S(1)} %broadcast_multiply_fusion.3) | copy-start | bytes 6916
  93.4 78.8 %copy-start.112 = (f32[576]{0:T(1024)}, f32[576]{0:T(1024)S(1)}, u32[]{:S(2)}) copy-start(f32[576]{0:T(1024)S(1)} %fusion.44) | copy-start | bytes 6916
  93.5 82.7 %copy-start.106 = (f32[576]{0:T(1024)}, f32[576]{0:T(1024)S(1)}, u32[]{:S(2)}) copy-start(f32[576]{0:T(1024)S(1)} %fusion.105) | copy-start | bytes 6916
  179.2 40.9 %copy-start.47 = (bf16[576,1024]{1,0:T(8,128)(2,1)}, bf16[576,1024]{1,0:T(8,128)(2,1)S(1)}, u32[]{:S(2)}) copy-start(bf16[576,1024]{1,0:T(8,128)(2,1)S(1)} %fusion.43) | copy-start | bytes 3538948
  222.7 55.3 %copy-start.84 = (bf16[128,768]{1,0:T(8,128)(2,1)S(1)}, bf16[128,768]{1,0:T(8,128)(2,1)}, u32[]{:S(2)}) copy-start(bf16[128,768]{1,0:T(8,128)(2,1)} %param.90) | copy-start | bytes 589828
  222.7 80.4 %copy-start.101 = (bf16[128,256]{1,0:T(8,128)(2,1)S(1)}, bf16[128,256]{1,0:T(8,128)(2,1)}, u32[]{:S(2)}) copy-start(bf16[128,256]{1,0:T(8,128)(2,1)} %param.91) | copy-start | bytes 196612
  222.8 98.1 %copy-start.102 = (f32[16,961]{1,0:T(8,128)S(1)}, f32[16,961]{1,0:T(8,128)}, u32[]{:S(2)}) copy-start(f32[16,961]{1,0:T(8,128)} %param.88) | copy-start | bytes 184516
  222.8 640.9 %all-gather.26.cloned.1.call-start = ((), (), s32[]{:S(2)}) async-start(), calls=%async_computation.25 | async-start | bytes 2359296 | tf_op jit(solution)/shard_map/all_gather | solution.py:328
  239.9 634.4 %all-gather.30.cloned.1.call-start = ((), (), s32[]{:S(2)}) async-start(), calls=%async_computation.27 | async-start | bytes 9437184 | tf_op jit(solution)/shard_map/all_gather | solution.py:329
  246.9 656.5 %all-gather.34.cloned.1.call-start = ((), (), s32[]{:S(2)}) async-start(), calls=%async_computation.29 | async-start | bytes 9437184 | tf_op jit(solution)/shard_map/all_gather | solution.py:330
  278.0 638.6 %all-gather.40.cloned.1.call-start = ((), (), s32[]{:S(2)}) async-start(), calls=%async_computation.32 | async-start | bytes 7077888 | tf_op jit(solution)/shard_map/all_gather | solution.py:327
  303.1 655.4 %all-gather.42.cloned.1.call-start = ((), (), s32[]{:S(2)}) async-start(), calls=%async_computation.33 | async-start | bytes 2359296 | tf_op jit(solution)/shard_map/all_gather | solution.py:328
  319.6 647.1 %all-gather.46.cloned.1.call-start = ((), (), s32[]{:S(2)}) async-start(), calls=%async_computation.35 | async-start | bytes 9437184 | tf_op jit(solution)/shard_map/all_gather | solution.py:329
  320.2 658.3 %all-gather.50.cloned.1.call-start = ((), (), s32[]{:S(2)}) async-start(), calls=%async_computation.37 | async-start | bytes 9437184 | tf_op jit(solution)/shard_map/all_gather | solution.py:330
  321.4 54.8 %copy-start.83 = (s32[8,2,8,128]{3,1,2,0:T(2,128)}, s32[8,2,8,128]{3,1,2,0:T(2,128)S(1)}, u32[]{:S(2)}) copy-start(s32[8,2,8,128]{3,1,2,0:T(2,128)S(1)} %copy.257) | copy-start | bytes 196612
  400.4 338.8 %copy-start.66 = (s32[102400]{0:T(1024)}, s32[102400]{0:T(1024)S(1)}, u32[]{:S(2)}) copy-start(s32[102400]{0:T(1024)S(1)} %reshape.2161) | copy-start | bytes 1228804
  774.2 38.1 %copy-start.104 = (f32[576]{0:T(1024)}, f32[576]{0:T(1024)S(1)}, u32[]{:S(2)}) copy-start(f32[576]{0:T(1024)S(1)} %concatenate.147) | copy-start | bytes 6916
  774.2 598.9 %reduce-scatter.22.cloned.1.call-start = ((), (), s32[]{:S(2)}) async-start(), calls=%async_computation.38 | async-start | bytes 11796480 | tf_op jit(solution)/shard_map/reduce_scatter | solution.py:163
  790.6 48.2 %copy-start.11 = (bf16[9,64,16,64]{1,3,2,0:T(8,128)(2,1)}, bf16[9,64,16,64]{1,3,2,0:T(8,128)(2,1)S(1)}, u32[]{:S(2)}) copy-start(bf16[9,64,16,64]{1,3,2,0:T(8,128)(2,1)S(1)} %copy.224) | copy-start | bytes 3538948
  869.2 34.2 %copy-start.3 = (f32[576,1024]{1,0:T(8,128)}, f32[576,1024]{1,0:T(8,128)S(1)}, u32[]{:S(2)}) copy-start(f32[576,1024]{1,0:T(8,128)S(1)} %get-tuple-element.355) | copy-start | bytes 7077892
  978.5 30.0 %copy-start.15 = (f32[576,1024]{1,0:T(8,128)S(1)}, f32[576,1024]{1,0:T(8,128)}, u32[]{:S(2)}) copy-start(f32[576,1024]{1,0:T(8,128)} %copy-done.14) | copy-start | bytes 7077892
  1212.4 971.8 %reduce-scatter.32.cloned.1.call-start = ((), (), s32[]{:S(2)}) async-start(), calls=%async_computation.43 | async-start | bytes 4718592 | tf_op jit(solution)/shard_map/reduce_scatter | solution.py:338
  1217.9 968.3 %reduce-scatter.52.cloned.1.call-start = ((), (), s32[]{:S(2)}) async-start(), calls=%async_computation.53 | async-start | bytes 4718592 | tf_op jit(solution)/shard_map/reduce_scatter | solution.py:338
  1223.7 964.4 %reduce-scatter.48.cloned.1.call-start = ((), (), s32[]{:S(2)}) async-start(), calls=%async_computation.51 | async-start | bytes 14155776 | tf_op jit(solution)/shard_map/reduce_scatter | solution.py:337
  1236.8 954.0 %reduce-scatter.36.cloned.1.call-start = ((), (), s32[]{:S(2)}) async-start(), calls=%async_computation.45 | async-start | bytes 18874368 | tf_op jit(solution)/shard_map/reduce_scatter | solution.py:339
  1250.9 943.0 %reduce-scatter.40.cloned.1.call-start = ((), (), s32[]{:S(2)}) async-start(), calls=%async_computation.47 | async-start | bytes 18874368 | tf_op jit(solution)/shard_map/reduce_scatter | solution.py:340
  1264.7 932.0 %reduce-scatter.56.cloned.1.call-start = ((), (), s32[]{:S(2)}) async-start(), calls=%async_computation.55 | async-start | bytes 18874368 | tf_op jit(solution)/shard_map/reduce_scatter | solution.py:339
  1278.5 921.0 %reduce-scatter.60.cloned.1.call-start = ((), (), s32[]{:S(2)}) async-start(), calls=%async_computation.57 | async-start | bytes 18874368 | tf_op jit(solution)/shard_map/reduce_scatter | solution.py:340
  1292.5 910.2 %reduce-scatter.28.cloned.1.call-start = ((), (), s32[]{:S(2)}) async-start(), calls=%async_computation.41 | async-start | bytes 14155776 | tf_op jit(solution)/shard_map/reduce_scatter | solution.py:337
  1304.4 78.4 %copy-start.45 = (bf16[576,1024]{1,0:T(8,128)(2,1)}, bf16[576,1024]{1,0:T(8,128)(2,1)S(1)}, u32[]{:S(2)}) copy-start(bf16[576,1024]{1,0:T(8,128)(2,1)S(1)} %reshape_reshape.18) | copy-start | bytes 3538948
  1382.8 931.2 %reduce-scatter.44.cloned.1.call-start = ((), (), s32[]{:S(2)}) async-start(), calls=%async_computation.49 | async-start | bytes 28311552 | tf_op jit(solution)/shard_map/reduce_scatter | solution.py:336
  1422.5 38.7 %copy-start.25 = (f32[576,1024]{1,0:T(8,128)S(1)}, f32[576,1024]{1,0:T(8,128)}, u32[]{:S(2)}) copy-start(f32[576,1024]{1,0:T(8,128)} %get-tuple-element.361) | copy-start | bytes 7077892
  1477.2 40.1 %copy-start.24 = (f32[576,1024]{1,0:T(8,128)S(1)}, f32[576,1024]{1,0:T(8,128)}, u32[]{:S(2)}) copy-start(f32[576,1024]{1,0:T(8,128)} %get-tuple-element.334) | copy-start | bytes 7077892
  1477.3 997.2 %reduce-scatter.24.cloned.1.call-start = ((), (), s32[]{:S(2)}) async-start(), calls=%async_computation.39 | async-start | bytes 28311552 | tf_op jit(solution)/shard_map/reduce_scatter | solution.py:336
  1477.3 49.9 %slice-start.5 = ((s8[4718592]{0:T(1024)(128)(4,1)}), s8[524288]{0:T(1024)(128)(4,1)S(1)}, s32[]{:S(2)}) async-start(s8[4718592]{0:T(1024)(128)(4,1)} %bitcast.187), calls=%async_computation.65 | async-start | bytes 1048576
  1582.8 1034.9 %all-reduce.31.cloned.1.call-start = ((), (), s32[]{:S(2)}) async-start(), calls=%async_computation.59 | async-start | bytes 2080768 | tf_op jit(solution)/shard_map/psum | solution.py:439
  2184.1 446.6 %reduce-scatter.34.cloned.1.call-start = ((), (), s32[]{:S(2)}) async-start(), calls=%async_computation.44 | async-start | bytes 327680 | tf_op jit(solution)/shard_map/reduce_scatter | solution.py:349
  2186.1 465.5 %reduce-scatter.54.cloned.1.call-start = ((), (), s32[]{:S(2)}) async-start(), calls=%async_computation.54 | async-start | bytes 327680 | tf_op jit(solution)/shard_map/reduce_scatter | solution.py:349
  2188.1 488.1 %reduce-scatter.50.cloned.1.call-start = ((), (), s32[]{:S(2)}) async-start(), calls=%async_computation.52 | async-start | bytes 983040 | tf_op jit(solution)/shard_map/reduce_scatter | solution.py:346
  2190.8 514.0 %reduce-scatter.38.cloned.1.call-start = ((), (), s32[]{:S(2)}) async-start(), calls=%async_computation.46 | async-start | bytes 1310720 | tf_op jit(solution)/shard_map/reduce_scatter | solution.py:352
  2193.8 539.2 %reduce-scatter.42.cloned.1.call-start = ((), (), s32[]{:S(2)}) async-start(), calls=%async_computation.48 | async-start | bytes 1310720 | tf_op jit(solution)/shard_map/reduce_scatter | solution.py:355
  2196.6 564.6 %reduce-scatter.58.cloned.1.call-start = ((), (), s32[]{:S(2)}) async-start(), calls=%async_computation.56 | async-start | bytes 1310720 | tf_op jit(solution)/shard_map/reduce_scatter | solution.py:352
  2199.5 589.7 %reduce-scatter.62.cloned.1.call-start = ((), (), s32[]{:S(2)}) async-start(), calls=%async_computation.58 | async-start | bytes 1310720 | tf_op jit(solution)/shard_map/reduce_scatter | solution.py:355
  2202.7 611.3 %reduce-scatter.30.cloned.1.call-start = ((), (), s32[]{:S(2)}) async-start(), calls=%async_computation.42 | async-start | bytes 983040 | tf_op jit(solution)/shard_map/reduce_scatter | solution.py:346
  2205.2 645.8 %reduce-scatter.46.cloned.1.call-start = ((), (), s32[]{:S(2)}) async-start(), calls=%async_computation.50 | async-start | bytes 1966080 | tf_op jit(solution)/shard_map/reduce_scatter | solution.py:343
  2317.2 160.6 %copy-start.50 = (f32[16,64,256]{2,1,0:T(8,128)S(1)}, f32[16,64,256]{2,1,0:T(8,128)}, u32[]{:S(2)}) copy-start(f32[16,64,256]{2,1,0:T(8,128)} %get-tuple-element.332) | copy-start | bytes 3145732
  2317.2 570.3 %reduce-scatter.26.cloned.1.call-start = ((), (), s32[]{:S(2)}) async-start(), calls=%async_computation.40 | async-start | bytes 1966080 | tf_op jit(solution)/shard_map/reduce_scatter | solution.py:343
  2482.7 170.5 %copy-start.19 = (f32[576,1024]{1,0:T(8,128)S(1)}, f32[576,1024]{1,0:T(8,128)}, u32[]{:S(2)}) copy-start(f32[576,1024]{1,0:T(8,128)} %copy-done.18) | copy-start | bytes 7077892
  2653.1 236.4 %copy-start.1 = (bf16[2,1024]{1,0:T(2,128)(2,1)S(1)}, bf16[2,1024]{1,0:T(2,128)(2,1)}, u32[]{:S(2)}) copy-start(bf16[2,1024]{1,0:T(2,128)(2,1)} %param.80) | copy-start | bytes 12292
  (112 other events, 640.5 us)
Sparse Core Ops, SparseCore 0:
  9.6 39.7 all-gather.17
  51.0 41.4 all-gather.35
  94.5 71.4 all-gather.19
  167.7 45.5 all-gather.21
  214.7 32.1 all-gather.27
  248.3 29.6 all-gather.31
  279.6 34.6 all-gather.43
  315.8 30.7 all-gather.47
  348.5 70.2 all-gather.37
  420.2 166.7 all-gather.23
  588.9 26.0 all-gather.25
  616.7 54.3 all-gather.29
  673.0 54.3 all-gather.33
  729.2 45.5 all-gather.39
  776.5 27.8 all-gather.41
  806.2 54.3 all-gather.45
  862.3 54.3 all-gather.49
  1212.5 160.6 reduce-scatter.21
  1376.5 52.1 reduce-scatter.31
  1432.3 51.3 reduce-scatter.51
  1487.1 92.3 reduce-scatter.47
  1583.1 115.9 reduce-scatter.35
  1702.7 115.9 reduce-scatter.39
  1822.1 115.9 reduce-scatter.55
  1941.7 115.9 reduce-scatter.59
  2061.1 92.4 reduce-scatter.27
  2157.0 156.8 reduce-scatter.43
  2317.6 156.8 reduce-scatter.23
  2479.6 129.6 all-reduce.30
  2612.1 18.5 reduce-scatter.33
  2633.5 18.0 reduce-scatter.53
  2654.6 21.5 reduce-scatter.49
  2678.4 26.3 reduce-scatter.37
  2707.1 25.7 reduce-scatter.41
  2735.4 25.7 reduce-scatter.57
  2763.3 25.7 reduce-scatter.61
  2792.0 21.9 reduce-scatter.29
  2816.4 34.5 reduce-scatter.45
  2853.2 34.2 reduce-scatter.25
where the time goes:
time: 2910 us; the launch traced here: 2900 us
  other arithmetic  936 us (32%)
  waiting for transfers between devices  790 us (27%)
  local copies, waits for them, and re-layouts  641 us (22%)
  matrix products  382 us (13%)
  blocking collectives  128 us (4%)
    scatter-add x1, other arithmetic, joint_back(): values[:, joint_index(TW)]  543 us
    gather x2, local copies, waits for them, and re-layouts, joint_attention(): lookup[:, joint_index(TW)]  374 us
    reduce_scatter x2, waiting for transfers between devices, settle(): lax.psum_scatter(grads[0], 'wide', scatter_dimension=0, tiled=True)  266 us
    scatter-add x4, other arithmetic, spread_rows(): jnp.repeat(per_sequence, repeats, axis=0, total_repeat_length=CLIP_DEV *...  153 us
    scatter-add x1, other arithmetic, space_back(): _, bias_back = jax.vjp(lambda values: values[:, bias_index], lookup)  87.8 us
    all_gather x2, waiting for transfers between devices, collect_weights(): lax.all_gather(partial_rows[0], 'wide', axis=0, tiled=True)  72.5 us
    reduce_scatter x2, waiting for transfers between devices, settle(): lax.psum_scatter(partial_rows[0].astype(jnp.bfloat16), 'narrow', scatter_...  69.9 us
    reduce_scatter x1, waiting for transfers between devices, space_back(): lax.psum_scatter(jnp.concatenate([grad_keys, grad_values], axis=-1).astyp...  68.8 us
  transfers between devices with their start and end apart: 39, of which 19 were waited for; matrix products, arithmetic and copies ran while one was open for 59% of the time, Pallas kernels for 0%

commit v1 on v0

v1 whole, which is shorter than its diff:
```python
import functools
import math

import jax
import jax.numpy as jnp
import numpy as np
from jax import lax
from jax.experimental import pallas as pl
from jax.experimental.pallas import tpu as pltpu
from jax.sharding import PartitionSpec as P

D = 1024
HEADS = 16
HEAD_DIM = 64
FF = 4096
SW = 8
TW = 5
CHUNK = SW * SW
CLIP_ROWS = TW * CHUNK
ROWS_DEV = CLIP_ROWS + 4 * CHUNK
SPAN_S = 4 * SW - 1
SPAN_T = 2 * SW - 1
MESH = pl.DeviceIdType.MESH


epsilon = 1e-06


def normalise(values):
    centred = values - jnp.mean(values, axis=-1, keepdims=True)
    spread = jnp.mean(centred * centred, axis=-1, keepdims=True)
    scale = lax.rsqrt(spread + epsilon)
    return centred * scale, scale


def norm_back(unit, scale, grad):
    return scale * (
        grad
        - jnp.mean(grad, axis=-1, keepdims=True)
        - unit * jnp.mean(grad * unit, axis=-1, keepdims=True)
    )


def nn(left, right):
    return lax.dot_general(left, right, (((1,), (0,)), ((), ())), preferred_element_type=jnp.float32)


def nt(left, right):
    return lax.dot_general(left, right, (((1,), (1,)), ((), ())), preferred_element_type=jnp.float32)


def tn(left, right):
    return lax.dot_general(left, right, (((0,), (0,)), ((), ())), preferred_element_type=jnp.float32)


def each_chunk(body, count=ROWS_DEV // CHUNK):
    @pl.loop(0, count)
    def _(i):
        inner = lax.rem(i, ROWS_DEV // CHUNK)
        seq = jnp.where(inner >= CLIP_ROWS // CHUNK, 1, 0)
        body(pl.ds(pl.multiple_of(i * CHUNK, CHUNK), CHUNK), pl.ds(seq, 1))


def part(index):
    return slice(index * D, (index + 1) * D)


def whole(shape):
    return pl.BlockSpec(shape, lambda *_: (0,) * len(shape), pipeline_mode=pl.Buffered(1))


def spec(shape, index):
    return pl.BlockSpec(shape, index)


def params(limit=56):
    return pltpu.CompilerParams(vmem_limit_bytes=limit * 2**20)


def shape(dims, kind):
    return jax.ShapeDtypeStruct(dims, kind)


LOW = jnp.bfloat16
FULL = jnp.float32


def space_triple_kernel(quarter, rows, mods, weight, normed, queries, pairs):
    step = pl.program_id(0)

    @pl.when(step == 0)
    def _():
        def chunk(at, seq):
            unit, _ = normalise(rows[at, :].astype(FULL))
            normed[at, :] = (unit * (1.0 + mods[seq, part(1)]) + mods[seq, part(0)]).astype(LOW)

        each_chunk(chunk, 4 * ROWS_DEV // CHUNK)

    @pl.when(step < 2)
    def _():
        own = pl.ds(pl.multiple_of(quarter[0] * ROWS_DEV, ROWS_DEV), ROWS_DEV)
        queries[...] = nn(normed[own, :], weight[...]).astype(LOW)

    @pl.when(step >= 2)
    def _():
        for q in range(4):
            pairs[q] = nn(normed[q * ROWS_DEV : (q + 1) * ROWS_DEV, :], weight[...]).astype(LOW)


def space_triple(quarter, rows, mods, weight):
    tile = 512
    return pl.pallas_call(
        space_triple_kernel,
        grid=(3 * D // tile,),
        in_specs=[
            pl.BlockSpec(memory_space=pltpu.SMEM),
            whole((4 * ROWS_DEV, D)),
            whole((2, 6 * D)),
            spec((D, tile), lambda t: (0, t)),
        ],
        out_specs=[
            whole((4 * ROWS_DEV, D)),
            spec((ROWS_DEV, tile), lambda t: (0, jnp.minimum(t, 1))),
            spec((4, ROWS_DEV, tile), lambda t: (0, 0, jnp.maximum(t - 2, 0))),
        ],
        out_shape=[
            shape((4 * ROWS_DEV, D), LOW),
            shape((ROWS_DEV, D), LOW),
            shape((4, ROWS_DEV, 2 * D), LOW),
        ],
        compiler_params=params(),
        name="space_triple",
    )(quarter, rows, mods, weight)


def joint_triple_kernel(rows, mods, weight, normed, triple):
    @pl.when(pl.program_id(0) == 0)
    def _():
        def chunk(at, seq):
            unit, _ = normalise(rows[at, :])
            normed[at, :] = (unit * (1.0 + mods[seq, part(1)]) + mods[seq, part(0)]).astype(LOW)

        each_chunk(chunk)

    triple[...] = nn(normed[...], weight[...]).astype(LOW)


def joint_triple(rows, mods, weight):
    tile = 512
    return pl.pallas_call(
        joint_triple_kernel,
        grid=(3 * D // tile,),
        in_specs=[whole((ROWS_DEV, D)), whole((2, 6 * D)), spec((D, tile), lambda t: (0, t))],
        out_specs=[whole((ROWS_DEV, D)), spec((ROWS_DEV, tile), lambda t: (0, t))],
        out_shape=[shape((ROWS_DEV, D), LOW), shape((ROWS_DEV, 3 * D), LOW)],
        compiler_params=params(),
        name="joint_triple",
    )(rows, mods, weight)


def half_mask():
    return lax.broadcasted_iota(jnp.int32, (1, 2 * HEAD_DIM), 1) < HEAD_DIM


def split_heads(rows):
    first = half_mask()
    zero = jnp.zeros_like(rows)
    return jnp.concatenate([jnp.where(first, rows, zero), jnp.where(first, zero, rows)], axis=0)


def join_heads(stacked):
    return jnp.where(half_mask(), stacked[:CHUNK], stacked[CHUNK:])


def softmax_keys(keys, queries, bias):
    scores = nt(keys, queries) * HEAD_DIM**-0.5 + bias
    powered = jnp.exp(scores - jnp.max(scores, axis=0, keepdims=True))
    return powered / jnp.sum(powered, axis=0, keepdims=True)


def attend(queries, keys, values, bias):
    probs = softmax_keys(keys, split_heads(queries), bias)
    return join_heads(tn(values, probs.astype(LOW)).T).astype(LOW)


def attend_back(queries, keys, values, bias, grad):
    queries, grad = split_heads(queries), split_heads(grad)
    probs = softmax_keys(keys, queries, bias)
    grad_values = nn(probs.astype(LOW), grad)
    grad_probs = nt(values, grad)
    centre = jnp.sum(probs * grad_probs, axis=0, keepdims=True)
    grad_scores = (probs * (grad_probs - centre)).astype(LOW)
    grad_queries = join_heads(tn(keys, grad_scores).T) * HEAD_DIM**-0.5
    grad_keys = nn(grad_scores, queries) * HEAD_DIM**-0.5
    return grad_queries, grad_keys, grad_values, grad_scores.astype(FULL)


def space_attend_kernel(queries, keys, values, bias, out):
    table = bias[0]
    for i in range(ROWS_DEV // CHUNK):
        at = slice(i * CHUNK, (i + 1) * CHUNK)
        key_rows = keys[:, at, :].reshape(4 * CHUNK, 2 * HEAD_DIM)
        value_rows = values[:, at, :].reshape(4 * CHUNK, 2 * HEAD_DIM)
        out[at, :] = attend(queries[at, :], key_rows, value_rows, table)


def space_attend(queries, pairs, bias):
    wide = 2 * HEAD_DIM
    return pl.pallas_call(
        space_attend_kernel,
        grid=(HEADS // 2,),
        in_specs=[
            spec((ROWS_DEV, wide), lambda h: (0, h)),
            spec((4, ROWS_DEV, wide), lambda h: (0, 0, h)),
            spec((4, ROWS_DEV, wide), lambda h: (0, 0, h + HEADS // 2)),
            spec((1, 4 * CHUNK, wide), lambda h: (h, 0, 0)),
        ],
        out_specs=spec((ROWS_DEV, wide), lambda h: (0, h)),
        out_shape=shape((ROWS_DEV, D), LOW),
        compiler_params=params(),
        name="space_attend",
    )(queries, pairs, pairs, bias)


def space_attend_back_kernel(queries, keys, values, bias, grad, grad_q, grad_pairs, grad_bias):
    table = bias[0]
    for i in range(ROWS_DEV // CHUNK):
        at = slice(i * CHUNK, (i + 1) * CHUNK)
        key_rows = keys[:, at, :].reshape(4 * CHUNK, 2 * HEAD_DIM)
        value_rows = values[:, at, :].reshape(4 * CHUNK, 2 * HEAD_DIM)
        to_q, to_k, to_v, to_bias = attend_back(
            queries[at, :], key_rows, value_rows, table, grad[at, :]
        )
        grad_q[at, :] = to_q.astype(LOW)
        grad_pairs[0, :, at, :] = to_k.astype(LOW).reshape(4, CHUNK, 2 * HEAD_DIM)
        grad_pairs[1, :, at, :] = to_v.astype(LOW).reshape(4, CHUNK, 2 * HEAD_DIM)
        if i == 0:
            grad_bias[0] = to_bias
        else:
            grad_bias[0] += to_bias


def space_attend_back(queries, pairs, bias, grad):
    wide = 2 * HEAD_DIM
    head = spec((ROWS_DEV, wide), lambda h: (0, h))
    four = spec((4, ROWS_DEV, wide), lambda h: (0, 0, h))
    table = spec((1, 4 * CHUNK, wide), lambda h: (h, 0, 0))
    return pl.pallas_call(
        space_attend_back_kernel,
        grid=(HEADS // 2,),
        in_specs=[
            head,
            four,
            spec((4, ROWS_DEV, wide), lambda h: (0, 0, h + HEADS // 2)),
            table,
            head,
        ],
        out_specs=[head, spec((2, 4, ROWS_DEV, wide), lambda h: (0, 0, 0, h)), table],
        out_shape=[
            shape((ROWS_DEV, D), LOW),
            shape((2, 4, ROWS_DEV, D), LOW),
            shape((HEADS // 2, 4 * CHUNK, wide), FULL),
        ],
        compiler_params=params(),
        name="space_attend_back",
    )(queries, pairs, pairs, bias, grad)


def clip_table(bias, frame):
    return jnp.concatenate([bias[0, frame - t + TW - 1] for t in range(TW)], axis=0)


def joint_attend_kernel(queries, keys, values, bias, out):
    for i in range(ROWS_DEV // CHUNK):
        at = slice(i * CHUNK, (i + 1) * CHUNK)
        seen = slice(0, CLIP_ROWS) if i < TW else at
        table = clip_table(bias, i) if i < TW else bias[0, TW - 1]
        out[at, :] = attend(queries[at, :], keys[seen, :], values[seen, :], table)


def joint_specs():
    wide = 2 * HEAD_DIM
    return [
        spec((ROWS_DEV, wide), lambda h: (0, h)),
        spec((ROWS_DEV, wide), lambda h: (0, h + HEADS // 2)),
        spec((ROWS_DEV, wide), lambda h: (0, h + HEADS)),
        spec((1, 2 * TW - 1, CHUNK, wide), lambda h: (h, 0, 0, 0)),
    ]


def joint_attend(triple, bias):
    return pl.pallas_call(
        joint_attend_kernel,
        grid=(HEADS // 2,),
        in_specs=joint_specs(),
        out_specs=spec((ROWS_DEV, 2 * HEAD_DIM), lambda h: (0, h)),
        out_shape=shape((ROWS_DEV, D), LOW),
        compiler_params=params(),
        name="joint_attend",
    )(triple, triple, triple, bias)


def joint_attend_back_kernel(
    queries, keys, values, bias, grad, grads, grad_bias, sum_k, sum_v
):
    grad_bias[...] = jnp.zeros_like(grad_bias)
    for i in range(ROWS_DEV // CHUNK):
        at = slice(i * CHUNK, (i + 1) * CHUNK)
        seen = slice(0, CLIP_ROWS) if i < TW else at
        table = clip_table(bias, i) if i < TW else bias[0, TW - 1]
        to_q, to_k, to_v, to_bias = attend_back(
            queries[at, :], keys[seen, :], values[seen, :], table, grad[at, :]
        )
        grads[0, at, :] = to_q.astype(LOW)
        if i >= TW:
            grad_bias[0, TW - 1] += to_bias
            grads[1, at, :] = to_k.astype(LOW)
            grads[2, at, :] = to_v.astype(LOW)
            continue
        for t in range(TW):
            grad_bias[0, i - t + TW - 1] += to_bias[t * CHUNK : (t + 1) * CHUNK]
        if i == 0:
            sum_k[...] = to_k
            sum_v[...] = to_v
        elif i < TW - 1:
            sum_k[...] += to_k
            sum_v[...] += to_v
        else:
            grads[1, seen, :] = (sum_k[...] + to_k).astype(LOW)
            grads[2, seen, :] = (sum_v[...] + to_v).astype(LOW)


def joint_attend_back(triple, bias, grad):
    wide = 2 * HEAD_DIM
    head = spec((ROWS_DEV, wide), lambda h: (0, h))
    return pl.pallas_call(
        joint_attend_back_kernel,
        grid=(HEADS // 2,),
        in_specs=joint_specs() + [head],
        out_specs=[spec((3, ROWS_DEV, wide), lambda h: (0, 0, h)), joint_specs()[3]],
        out_shape=[
            shape((3, ROWS_DEV, D), LOW),
            shape((HEADS // 2, 2 * TW - 1, CHUNK, wide), FULL),
        ],
        scratch_shapes=[pltpu.VMEM((CLIP_ROWS, wide), FULL)] * 2,
        compiler_params=params(),
        name="joint_attend_back",
    )(triple, triple, triple, bias, grad)


def mlp_kernel(last_block, live, rows, attended, mods, output, expand, shrink, *refs):
    branch, middle, normed, active, slope, reduced, result, total = refs
    step = pl.program_id(0)

    @pl.when(step == 0)
    def _():
        def chunk(at, seq):
            grown = nn(attended[at, :], output[...])
            branch[at, :] = grown.astype(LOW)
            mixed = rows[at, :].astype(FULL) + mods[seq, part(2)] * grown
            middle[at, :] = mixed
            unit, _ = normalise(mixed)
            normed[at, :] = (unit * (1.0 + mods[seq, part(4)]) + mods[seq, part(3)]).astype(LOW)

        each_chunk(chunk)
        total[...] = jnp.zeros_like(total)

    before = nn(normed[...], expand[...])
    inner = 0.5 * (1.0 + lax.erf(before * 0.5**0.5))
    low_active = (before * inner).astype(LOW)
    active[...] = low_active
    slope[...] = (inner + before * jnp.exp(-0.5 * before * before) * (2.0 * math.pi) ** -0.5).astype(LOW)
    total[...] += nn(low_active, shrink[...])

    @pl.when(step == pl.num_programs(0) - 1)
    def _():
        def chunk(at, seq):
            reduced[at, :] = total[at, :].astype(LOW)
            value = middle[at, :] + mods[seq, part(5)] * total[at, :]
            if last_block:
                value = value * jnp.where(seq.start > 0, live[0], 1.0)
            result[at, :] = value.astype(result.dtype)

        each_chunk(chunk)


def mlp(last_block, live, rows, attended, mods, output, expand, shrink):
    tile = 512
    square = whole((ROWS_DEV, D))
    strip = spec((ROWS_DEV, tile), lambda f: (0, f))
    return pl.pallas_call(
        functools.partial(mlp_kernel, last_block),
        grid=(FF // tile,),
        in_specs=[
            pl.BlockSpec(memory_space=pltpu.SMEM),
            square,
            square,
            whole((2, 6 * D)),
            whole((D, D)),
            spec((D, tile), lambda f: (0, f)),
            spec((tile, D), lambda f: (f, 0)),
        ],
        out_specs=[square, square, square, strip, strip, square, square],
        out_shape=[
            shape((ROWS_DEV, D), LOW),
            shape((ROWS_DEV, D), FULL),
            shape((ROWS_DEV, D), LOW),
            shape((ROWS_DEV, FF), LOW),
            shape((ROWS_DEV, FF), LOW),
            shape((ROWS_DEV, D), LOW),
            shape((ROWS_DEV, D), LOW if last_block else FULL),
        ],
        scratch_shapes=[pltpu.VMEM((ROWS_DEV, D), FULL)],
        compiler_params=params(),
        name="mlp",
    )(live, rows, attended, mods, output, expand, shrink)


def mlp_back_kernel(first_block, live, *refs):
    (grad_result, attended, mods, branch, middle, normed, reduced, output, active, slope) = refs[:10]
    expand, shrink = refs[10:12]
    grad_shrink, grad_expand, grad_output, grad_middle, grad_attended, grad_mods = refs[12:18]
    grad_reduced, normed_t, total, grad_branch = refs[18:]
    step = pl.program_id(0)

    def incoming(at, seq):
        value = grad_result[at, :].astype(FULL)
        if first_block:
            value = value * jnp.where(seq.start > 0, live[0], 1.0)
        return value

    @pl.when(step == 0)
    def _():
        grad_mods[...] = jnp.zeros_like(grad_mods)

        def chunk(at, seq):
            value = incoming(at, seq)
            grad_reduced[at, :] = (mods[seq, part(5)] * value).astype(LOW)
            grad_mods[seq, part(5)] += jnp.sum(
                reduced[at, :].astype(FULL) * value, axis=0, keepdims=True
            )

        each_chunk(chunk)
        total[...] = jnp.zeros_like(total)
        normed_t[...] = normed[...].T

    grad_active = nt(grad_reduced[...], shrink[...])
    grad_before = (grad_active * slope[...].astype(FULL)).astype(LOW)
    grad_shrink[...] = tn(active[...], grad_reduced[...]).astype(LOW)
    grad_expand[...] = nn(normed_t[...], grad_before).astype(LOW)
    total[...] += nt(grad_before, expand[...])

    @pl.when(step == pl.num_programs(0) - 1)
    def _():
        def chunk(at, seq):
            grad = total[at, :]
            unit, scale = normalise(middle[at, :])
            grad_mods[seq, part(3)] += jnp.sum(grad, axis=0, keepdims=True)
            grad_mods[seq, part(4)] += jnp.sum(unit * grad, axis=0, keepdims=True)
            value = incoming(at, seq) + norm_back(unit, scale, (1.0 + mods[seq, part(4)]) * grad)
            grad_middle[at, :] = value
            grad_mods[seq, part(2)] += jnp.sum(
                branch[at, :].astype(FULL) * value, axis=0, keepdims=True
            )
            grad_branch[at, :] = (mods[seq, part(2)] * value).astype(LOW)

        each_chunk(chunk)
        grad_attended[...] = nt(grad_branch[...], output[...]).astype(LOW)
        grad_output[...] = tn(attended[...], grad_branch[...]).astype(LOW)


def mlp_back(first_block, live, grad_result, attended, mods, saved, output, expand, shrink):
    branch, middle, normed, active, slope, reduced = saved
    tile = 512
    square = whole((ROWS_DEV, D))
    strip = spec((ROWS_DEV, tile), lambda f: (0, f))
    across = spec((D, tile), lambda f: (0, f))
    down = spec((tile, D), lambda f: (f, 0))
    return pl.pallas_call(
        functools.partial(mlp_back_kernel, first_block),
        grid=(FF // tile,),
        in_specs=[
            pl.BlockSpec(memory_space=pltpu.SMEM),
            square,
            square,
            whole((2, 6 * D)),
            square,
            square,
            square,
            square,
            whole((D, D)),
            strip,
            strip,
            across,
            down,
        ],
        out_specs=[down, across, whole((D, D)), square, square, whole((2, 6 * D))],
        out_shape=[
            shape((FF, D), LOW),
            shape((D, FF), LOW),
            shape((D, D), LOW),
            shape((ROWS_DEV, D), FULL),
            shape((ROWS_DEV, D), LOW),
            shape((2, 6 * D), FULL),
        ],
        scratch_shapes=[
            pltpu.VMEM((ROWS_DEV, D), LOW),
            pltpu.VMEM((D, ROWS_DEV), LOW),
            pltpu.VMEM((ROWS_DEV, D), FULL),
            pltpu.VMEM((ROWS_DEV, D), LOW),
        ],
        compiler_params=params(),
        name="mlp_back",
    )(live, grad_result, attended, mods, branch, middle, normed, reduced, output, active, slope, expand, shrink)


def finish_rows(rows, grad_normed, grad_middle, mods, grad_rows, grad_mods):
    grad_mods[...] = jnp.zeros_like(grad_mods)

    def chunk(at, seq):
        grad = grad_normed[at, :].astype(FULL)
        unit, scale = normalise(rows[at, :].astype(FULL))
        grad_mods[seq, part(0)] += jnp.sum(grad, axis=0, keepdims=True)
        grad_mods[seq, part(1)] += jnp.sum(unit * grad, axis=0, keepdims=True)
        grad_rows[at, :] = grad_middle[at, :] + norm_back(
            unit, scale, (1.0 + mods[seq, part(1)]) * grad
        )

    each_chunk(chunk)


def joint_project_back_kernel(
    rows, mods, normed, grad_middle, weight, grad, grad_weight, grad_rows, grad_mods, total, normed_t
):
    step = pl.program_id(0)

    @pl.when(step == 0)
    def _():
        total[...] = jnp.zeros_like(total)
        normed_t[...] = normed[...].T

    grad_weight[...] = nn(normed_t[...], grad[0]).astype(LOW)
    total[...] += nt(grad[0], weight[...])

    @pl.when(step == pl.num_programs(0) - 1)
    def _():
        finish_rows(rows, total, grad_middle, mods, grad_rows, grad_mods)


def joint_project_back(rows, mods, normed, grad_middle, weight, grads):
    tile = 1024
    square = whole((ROWS_DEV, D))
    across = spec((D, tile), lambda t: (0, t))
    return pl.pallas_call(
        joint_project_back_kernel,
        grid=(3 * D // tile,),
        in_specs=[square, whole((2, 6 * D)), square, square, across, spec((1, ROWS_DEV, tile), lambda t: (t, 0, 0))],
        out_specs=[across, square, whole((2, 2 * D))],
        out_shape=[shape((D, 3 * D), LOW), shape((ROWS_DEV, D), FULL), shape((2, 2 * D), FULL)],
        scratch_shapes=[pltpu.VMEM((ROWS_DEV, D), FULL), pltpu.VMEM((D, ROWS_DEV), LOW)],
        compiler_params=params(),
        name="joint_project_back",
    )(rows, mods, normed, grad_middle, weight, grads)


def space_project_back_kernel(quarter, normed, weight, grad_q, grad_pairs, grad_weight, grad_normed, total):
    step = pl.program_id(0)

    @pl.when(step == 0)
    def _():
        own = pl.ds(pl.multiple_of(quarter[0] * ROWS_DEV, ROWS_DEV), ROWS_DEV)
        total[...] = jnp.zeros_like(total)
        grad_weight[...] = tn(normed[own, :], grad_q[...]).astype(LOW)
        total[own, :] = nt(grad_q[...], weight[...])

    @pl.when(step > 0)
    def _():
        flat = grad_pairs[0].reshape(4 * ROWS_DEV, D)
        grad_weight[...] = tn(normed[...], flat).astype(LOW)
        for q in range(4):
            at = slice(q * ROWS_DEV, (q + 1) * ROWS_DEV)
            value = total[at, :] + nt(grad_pairs[0, q], weight[...])
            total[at, :] = value

    @pl.when(step == pl.num_programs(0) - 1)
    def _():
        grad_normed[...] = total[...].astype(LOW)


def space_project_back(quarter, normed, weight, grad_q, grad_pairs):
    across = spec((D, D), lambda t: (0, t))
    return pl.pallas_call(
        space_project_back_kernel,
        grid=(3,),
        in_specs=[
            pl.BlockSpec(memory_space=pltpu.SMEM),
            whole((4 * ROWS_DEV, D)),
            across,
            whole((ROWS_DEV, D)),
            spec((1, 4, ROWS_DEV, D), lambda t: (jnp.maximum(t - 1, 0), 0, 0, 0)),
        ],
        out_specs=[across, whole((4 * ROWS_DEV, D))],
        out_shape=[shape((D, 3 * D), LOW), shape((4 * ROWS_DEV, D), LOW)],
        scratch_shapes=[pltpu.VMEM((4 * ROWS_DEV, D), FULL)],
        compiler_params=params(),
        name="space_project_back",
    )(quarter, normed, weight, grad_q, grad_pairs)


def finish_kernel(rows, mods, grad_normed, grad_middle, grad_rows, grad_mods):
    finish_rows(rows, grad_normed, grad_middle, mods, grad_rows, grad_mods)


def finish(rows, mods, grad_normed, grad_middle):
    return pl.pallas_call(
        finish_kernel,
        out_shape=[shape((ROWS_DEV, D), FULL), shape((2, 2 * D), FULL)],
        compiler_params=params(),
        name="finish",
    )(rows, mods, grad_normed, grad_middle)


def near_order(n):
    return (
        n,
        lax.bitwise_xor(n, 1),
        jnp.where(n < 2, 2, 1),
        jnp.where(n < 2, 3, 0),
    )


def enter(w, n, peers):
    barrier = pltpu.get_barrier_semaphore()
    for peer in peers:
        pl.semaphore_signal(barrier, inc=1, device_id=(peer, n), device_id_type=MESH)

    @pl.when(n > 0)
    def _():
        pl.semaphore_signal(barrier, inc=1, device_id=(w, n - 1), device_id_type=MESH)

    @pl.when(n < 3)
    def _():
        pl.semaphore_signal(barrier, inc=1, device_id=(w, n + 1), device_id_type=MESH)

    ends = jnp.where(n > 0, 1, 0) + jnp.where(n < 3, 1, 0)
    pl.semaphore_wait(barrier, len(peers) + ends)


PIECES = 4
PIECE = ROWS_DEV // PIECES


def gather_kernel(shapes, line, *refs):
    count = len(shapes)
    extra = 1 if line else 0
    shards, refs = refs[:count], refs[count:]
    line_in, refs = refs[:extra], refs[extra:]
    fulls, refs = refs[:count], refs[count:]
    line_out, refs = refs[:extra], refs[extra:]
    z_send, z_recv, x_send, x_recv, y_send, y_recv, c_send, c_recv, own_sem = refs[:9]
    if line:
        rows, all_rows = line_in[0], line_out[0]
        t_send, t_recv, t_own = refs[9:]
    w = lax.axis_index("wide")
    n = lax.axis_index("narrow")
    x_peer = lax.bitwise_xor(w, 2)
    y_peer = lax.bitwise_xor(w, 4)
    c_peer = lax.bitwise_xor(w, 1)
    d_peer = lax.bitwise_xor(w, 6)
    order = near_order(n)
    enter(w, n, (x_peer, y_peer, c_peer))

    def block(k, row, col):
        rows, cols = shapes[k]
        return fulls[k].at[
            pl.ds(pl.multiple_of(row * rows, rows), rows), pl.ds(pl.multiple_of(col * cols, cols), cols)
        ]

    def copy(k, src, row, col, send, recv, to):
        return pltpu.make_async_remote_copy(
            src_ref=src,
            dst_ref=block(k, row, col),
            send_sem=send,
            recv_sem=recv,
            device_id=to,
            device_id_type=MESH,
        )

    def z_copy(k, src, col, to):
        return copy(k, src, w, col, z_send.at[k, col], z_recv.at[k, col], (w, to))

    def x_copy(k, src, row, far, col):
        return copy(k, src, row, col, x_send.at[k, far, col], x_recv.at[k, far, col], (x_peer, n))

    def y_copy(k, src, row, far, col):
        return copy(k, src, row, col, y_send.at[k, far, col], y_recv.at[k, far, col], (y_peer, n))

    def c_copy(k, src, row, chip, col):
        return copy(k, src, row, col, c_send.at[k, chip, col], c_recv.at[k, chip, col], (c_peer, n))

    up = jnp.minimum(n + 1, 3)
    down = jnp.maximum(n - 1, 0)

    def own_copy(k):
        return pltpu.make_async_copy(shards[k], block(k, w, n), own_sem.at[k])

    for k in range(count):
        own_copy(k).start()
        x_copy(k, shards[k], w, 0, n).start()
        y_copy(k, shards[k], w, 0, n).start()

        @pl.when(n < 3)
        def _():
            copy(k, shards[k], w, n, z_send.at[k, n], z_recv.at[k, n], (w, up)).start()

        @pl.when(n > 0)
        def _():
            copy(k, shards[k], w, n, z_send.at[k, 4], z_recv.at[k, n], (w, down)).start()

        c_copy(k, shards[k], w, 0, n).start()

    def z_stage(k, j):
        col = order[j]
        here = block(k, w, col)
        z_copy(k, here, col, up).wait_recv()
        x_copy(k, here, w, 0, col).start()
        y_copy(k, here, w, 0, col).start()

        @pl.when(jnp.logical_and(col < n, n < 3))
        def _():
            z_copy(k, here, col, up).start()

        @pl.when(jnp.logical_and(col > n, n > 0))
        def _():
            z_copy(k, here, col, down).start()

        c_copy(k, here, w, 0, col).start()

    def xy_stage(k, j):
        col = order[j]
        from_x = block(k, x_peer, col)
        from_y = block(k, y_peer, col)
        x_copy(k, from_x, x_peer, 0, col).wait_recv()
        if j < 2:
            y_copy(k, from_x, x_peer, 1, col).start()
        c_copy(k, from_x, x_peer, 1, col).start()
        y_copy(k, from_y, y_peer, 0, col).wait_recv()
        if j >= 2:
            x_copy(k, from_y, y_peer, 1, col).start()
        c_copy(k, from_y, y_peer, 2, col).start()

    def far_stage(k, j):
        col = order[j]
        far = block(k, d_peer, col)
        if j < 2:
            y_copy(k, far, d_peer, 1, col).wait_recv()
        else:
            x_copy(k, far, d_peer, 1, col).wait_recv()
        c_copy(k, far, d_peer, 3, col).start()

    def t_copy(p, src, col, slot, to):
        return pltpu.make_async_remote_copy(
            src_ref=src,
            dst_ref=all_rows.at[col, pl.ds(p * PIECE, PIECE)],
            send_sem=t_send.at[p, slot],
            recv_sem=t_recv.at[p, col],
            device_id=(w, to),
            device_id_type=MESH,
        )

    def t_own_copy(p):
        here = pl.ds(p * PIECE, PIECE)
        return pltpu.make_async_copy(rows.at[here], all_rows.at[n, here], t_own.at[p])

    def t_start(p):
        src = rows.at[pl.ds(p * PIECE, PIECE)]
        t_own_copy(p).start()

        @pl.when(n < 3)
        def _():
            t_copy(p, src, n, n, up).start()

        @pl.when(n > 0)
        def _():
            t_copy(p, src, n, 4, down).start()

    def t_stage(p):
        for j in range(1, 4):
            col = order[j]
            here = all_rows.at[col, pl.ds(p * PIECE, PIECE)]
            t_copy(p, here, col, col, up).wait_recv()

            @pl.when(jnp.logical_and(col < n, n < 3))
            def _():
                t_copy(p, here, col, col, up).start()

            @pl.when(jnp.logical_and(col > n, n > 0))
            def _():
                t_copy(p, here, col, col, down).start()

    def t_drain(p):
        for col in range(4):
            here = all_rows.at[col, pl.ds(p * PIECE, PIECE)]

            @pl.when(jnp.logical_or(jnp.logical_and(col <= n, n < 3), jnp.logical_and(col > n, n > 0)))
            def _():
                t_copy(p, here, col, col, up).wait_send()

        @pl.when(n > 0)
        def _():
            t_copy(p, all_rows.at[n, pl.ds(p * PIECE, PIECE)], n, 4, down).wait_send()

        t_own_copy(p).wait()

    def z_all(k):
        for j in range(1, 4):
            z_stage(k, j)

    def xy_all(k):
        for j in range(4):
            xy_stage(k, j)

    def far_all(k):
        for j in range(4):
            far_stage(k, j)

    def t_all(start, stage):
        if line:
            if start >= 0:
                t_start(start)
            if stage >= 0:
                t_stage(stage)

    z_all(0)
    t_all(0, -1)
    z_all(1)
    t_all(1, -1)
    xy_all(0)
    z_all(2)
    t_all(2, 0)
    xy_all(1)
    far_all(0)
    z_all(3)
    t_all(3, 1)
    xy_all(2)
    far_all(1)
    t_all(-1, 2)
    xy_all(3)
    far_all(2)
    t_all(-1, 3)
    far_all(3)

    if line:
        for p in range(PIECES):
            t_drain(p)
    for k in range(count):
        own_copy(k).wait()
        for col in range(4):
            here = block(k, w, col)

            @pl.when(jnp.logical_or(jnp.logical_and(col <= n, n < 3), jnp.logical_and(col > n, n > 0)))
            def _():
                z_copy(k, here, col, up).wait_send()

            x_copy(k, here, w, 0, col).wait_send()
            y_copy(k, here, w, 0, col).wait_send()

            for chip in range(4):
                c_copy(k, here, w, chip, col).wait()

        @pl.when(n > 0)
        def _():
            copy(k, shards[k], w, n, z_send.at[k, 4], z_recv.at[k, n], (w, down)).wait_send()

        for j in range(4):
            col = order[j]
            here = block(k, w, col)
            if j < 2:
                y_copy(k, here, w, 1, col).wait_send()
            else:
                x_copy(k, here, w, 1, col).wait_send()


def gather_weights(shards, line, collective_id, name):
    count = len(shards)
    shapes = tuple(s.shape for s in shards)
    lines = [] if line is None else [line]
    dma = pltpu.SemaphoreType.DMA
    line_scratch = [dma((PIECES, 5)), dma((PIECES, 4)), dma((PIECES,))]
    return pl.pallas_call(
        functools.partial(gather_kernel, shapes, bool(lines)),
        out_shape=[shape((8 * r, 4 * c), LOW) for r, c in shapes]
        + [shape((4,) + rows.shape, LOW) for rows in lines],
        in_specs=[pl.BlockSpec(memory_space=pl.ANY)] * (count + len(lines)),
        out_specs=[pl.BlockSpec(memory_space=pl.ANY)] * (count + len(lines)),
        scratch_shapes=[
            dma((count, 5)),
            dma((count, 4)),
            dma((count, 2, 4)),
            dma((count, 2, 4)),
            dma((count, 2, 4)),
            dma((count, 2, 4)),
            dma((count, 4, 4)),
            dma((count, 4, 4)),
            dma((count,)),
        ]
        + line_scratch * len(lines),
        compiler_params=pltpu.CompilerParams(collective_id=collective_id, has_side_effects=True),
        cost_estimate=pl.CostEstimate(flops=100_000_000_000, bytes_accessed=0, transcendentals=0),
        name=name,
    )(*shards, *lines)


def scatter_kernel(shapes, line, *refs):
    count = len(shapes)
    extra = 1 if line else 0
    parts, refs = refs[:count], refs[count:]
    line_part, refs = refs[:extra], refs[extra:]
    outs, refs = refs[:count], refs[count:]
    line_out, scratch = refs[:extra], refs[extra:]
    held, core_in = scratch[:count], scratch[count : 2 * count]
    far_in, near_in, z_in = (
        scratch[2 * count : 3 * count],
        scratch[3 * count : 4 * count],
        scratch[4 * count : 5 * count],
    )
    load, c_send, c_recv, d_send, d_recv, n_send, n_recv, z_send, z_recv = scratch[
        5 * count : 5 * count + 9
    ]
    if line:
        line_held, line_in, line_load, line_send, line_recv = scratch[5 * count + 9 :]
    w = lax.axis_index("wide")
    n = lax.axis_index("narrow")
    x_peer = lax.bitwise_xor(w, 2)
    y_peer = lax.bitwise_xor(w, 4)
    c_peer = lax.bitwise_xor(w, 1)
    d_peer = lax.bitwise_xor(w, 6)
    chips = (w, x_peer, y_peer, d_peer)
    order = near_order(n)
    up = jnp.minimum(n + 1, 3)
    down = jnp.maximum(n - 1, 0)
    enter(w, n, (x_peer, y_peer, c_peer))

    def source(k, row, col):
        rows, cols = shapes[k]
        return parts[k].at[
            pl.ds(pl.multiple_of(row * rows, rows), rows), pl.ds(pl.multiple_of(col * cols, cols), cols)
        ]

    def load_copy(k, chip, col):
        return pltpu.make_async_copy(
            source(k, chips[chip], col), held[k].at[chip, col], load.at[k, chip, col]
        )

    def c_copy(k, chip, col):
        row = lax.bitwise_xor(chips[chip], 1)
        return pltpu.make_async_remote_copy(
            src_ref=source(k, row, col),
            dst_ref=core_in[k].at[chip, col],
            send_sem=c_send.at[k, chip, col],
            recv_sem=c_recv.at[k, chip, col],
            device_id=(c_peer, n),
            device_id_type=MESH,
        )

    def d_copy(k, j):
        return pltpu.make_async_remote_copy(
            src_ref=held[k].at[3, order[j]],
            dst_ref=far_in[k].at[j],
            send_sem=d_send.at[k, j],
            recv_sem=d_recv.at[k, j],
            device_id=(x_peer if j < 2 else y_peer, n),
            device_id_type=MESH,
        )

    def n_copy(k, chip, col):
        return pltpu.make_async_remote_copy(
            src_ref=held[k].at[chip, col],
            dst_ref=near_in[k].at[chip - 1, col],
            send_sem=n_send.at[k, chip - 1, col],
            recv_sem=n_recv.at[k, chip - 1, col],
            device_id=(chips[chip], n),
            device_id_type=MESH,
        )

    def z_copy(k, col, slot, to):
        return pltpu.make_async_remote_copy(
            src_ref=held[k].at[0, col],
            dst_ref=z_in[k].at[slot],
            send_sem=z_send.at[k, col],
            recv_sem=z_recv.at[k, slot],
            device_id=(w, to),
            device_id_type=MESH,
        )

    def add(k, chip, col, *others):
        rows = shapes[k][0]
        step = 32

        @pl.loop(0, rows // step)
        def _(i):
            at = pl.ds(pl.multiple_of(i * step, step), step)
            total = held[k][chip, col, at, :].astype(jnp.float32)
            for ref, index in others:
                total += ref[*index, at, :].astype(jnp.float32)
            held[k][chip, col, at, :] = total.astype(jnp.bfloat16)

    def fold_core(k, chip, col):
        load_copy(k, chip, col).wait()
        c_copy(k, chip, col).wait_recv()
        add(k, chip, col, (core_in[k], (chip, col)))

    def first(k):
        for j in range(4):
            fold_core(k, 3, order[j])
            d_copy(k, j).start()
        for j in range(2):
            fold_core(k, 1, order[j])
            n_copy(k, 1, order[j]).start()
            fold_core(k, 2, order[j + 2])
            n_copy(k, 2, order[j + 2]).start()

    def second(k):
        for j in range(2):
            load_copy(k, 2, order[j]).wait()
            c_copy(k, 2, order[j]).wait_recv()
            d_copy(k, j).wait_recv()
            add(k, 2, order[j], (core_in[k], (2, order[j])), (far_in[k], (j,)))
            n_copy(k, 2, order[j]).start()
            load_copy(k, 1, order[j + 2]).wait()
            c_copy(k, 1, order[j + 2]).wait_recv()
            d_copy(k, j + 2).wait_recv()
            add(k, 1, order[j + 2], (core_in[k], (1, order[j + 2])), (far_in[k], (j + 2,)))
            n_copy(k, 1, order[j + 2]).start()

    def fold_near(k, j):
        col = order[j]
        load_copy(k, 0, col).wait()
        c_copy(k, 0, col).wait_recv()
        n_copy(k, 1, col).wait_recv()
        n_copy(k, 2, col).wait_recv()
        add(k, 0, col, (core_in[k], (0, col)), (near_in[k], (0, col)), (near_in[k], (1, col)))

    def third(k):
        for j in (3, 2, 1):
            col = order[j]
            fold_near(k, j)
            upward = col > n
            carried = jnp.logical_or(
                jnp.logical_and(upward, n > 0), jnp.logical_and(col < n, n < 3)
            )

            @pl.when(carried)
            def _():
                z_copy(k, col, col, up).wait_recv()
                add(k, 0, col, (z_in[k], (col,)))

            to = jnp.where(upward, up, down)
            slot = jnp.where(jnp.logical_and(jnp.logical_not(upward), to == col), 4, col)
            z_copy(k, col, slot, to).start()

    def last(k):
        fold_near(k, 0)
        outs[k][...] = held[k][0, n].astype(FULL)

        @pl.when(n > 0)
        def _():
            z_copy(k, n, n, up).wait_recv()
            outs[k][...] += z_in[k][n].astype(FULL)

        @pl.when(n < 3)
        def _():
            z_copy(k, n, 4, up).wait_recv()
            outs[k][...] += z_in[k][4].astype(FULL)

    def line_loads(p, col):
        return pltpu.make_async_copy(
            line_part[0].at[pl.ds(pl.multiple_of(col * ROWS_DEV + p * PIECE, 16), PIECE)],
            line_held.at[p, col],
            line_load.at[p, col],
        )

    def line_copy(p, col, slot, to):
        return pltpu.make_async_remote_copy(
            src_ref=line_held.at[p, col],
            dst_ref=line_in.at[p, slot],
            send_sem=line_send.at[p, col],
            recv_sem=line_recv.at[p, slot],
            device_id=(w, to),
            device_id_type=MESH,
        )

    def line_stage(p, j):
        col = order[j]
        line_loads(p, col).wait()
        upward = col > n
        carried = jnp.logical_or(jnp.logical_and(upward, n > 0), jnp.logical_and(col < n, n < 3))

        @pl.when(carried)
        def _():
            line_copy(p, col, col, up).wait_recv()

            @pl.loop(0, PIECE // 16)
            def _(i):
                at = pl.ds(pl.multiple_of(i * 16, 16), 16)
                total = line_held[p, col, at, :].astype(FULL) + line_in[p, col, at, :].astype(FULL)
                line_held[p, col, at, :] = total.astype(LOW)

        to = jnp.where(upward, up, down)
        slot = jnp.where(jnp.logical_and(jnp.logical_not(upward), to == col), 4, col)
        line_copy(p, col, slot, to).start()

    def line_last(p):
        here = pl.ds(p * PIECE, PIECE)
        line_loads(p, n).wait()
        line_out[0][here, :] = line_held[p, n].astype(FULL)

        @pl.when(n > 0)
        def _():
            line_copy(p, n, n, up).wait_recv()
            line_out[0][here, :] += line_in[p, n].astype(FULL)

        @pl.when(n < 3)
        def _():
            line_copy(p, n, 4, up).wait_recv()
            line_out[0][here, :] += line_in[p, 4].astype(FULL)

    def line_all(j):
        if not line:
            return
        for p in range(PIECES):
            if j:
                line_stage(p, j)
            else:
                line_last(p)

    if line:
        for j in (3, 2, 1, 0):
            for p in range(PIECES):
                line_loads(p, order[j]).start()
    for k in range(count):
        for chip in (3, 1, 2, 0):
            for j in range(4):
                c_copy(k, chip, order[j]).start()
                load_copy(k, chip, order[j]).start()
    line_all(3)
    first(0)
    line_all(2)
    second(0)
    first(1)
    line_all(1)
    second(1)
    third(0)
    for t in range(2, count + 2):
        if t < count:
            first(t)
            second(t)
        if t - 1 < count:
            third(t - 1)
        last(t - 2)
        if t == 2:
            line_all(0)
    for k in range(count):
        for chip in range(4):
            for col in range(4):
                c_copy(k, chip, col).wait_send()
        for j in range(4):
            d_copy(k, j).wait_send()
            n_copy(k, 1, j).wait_send()
            n_copy(k, 2, j).wait_send()
        for j in range(1, 4):
            z_copy(k, order[j], order[j], up).wait_send()
    if line:
        for p in range(PIECES):
            for j in range(1, 4):
                line_copy(p, order[j], order[j], up).wait_send()


def scatter_grads(partials, line, collective_id, name):
    count = len(partials)
    shapes = tuple((g.shape[0] // 8, g.shape[1] // 4) for g in partials)
    dma = pltpu.SemaphoreType.DMA
    lines = [] if line is None else [line]
    line_scratch = [
        pltpu.VMEM((PIECES, 4, PIECE, D), LOW),
        pltpu.VMEM((PIECES, 5, PIECE, D), LOW),
        dma((PIECES, 4)),
        dma((PIECES, 4)),
        dma((PIECES, 5)),
    ]
    return pl.pallas_call(
        functools.partial(scatter_kernel, shapes, bool(lines)),
        out_shape=[shape(s, FULL) for s in shapes] + [shape((ROWS_DEV, D), FULL)] * len(lines),
        in_specs=[pl.BlockSpec(memory_space=pl.ANY)] * (count + len(lines)),
        out_specs=[pl.BlockSpec(memory_space=pltpu.VMEM)] * (count + len(lines)),
        scratch_shapes=[pltpu.VMEM((4, 4) + s, LOW) for s in shapes]
        + [pltpu.VMEM((4, 4) + s, LOW) for s in shapes]
        + [pltpu.VMEM((4,) + s, LOW) for s in shapes]
        + [pltpu.VMEM((2, 4) + s, LOW) for s in shapes]
        + [pltpu.VMEM((5,) + s, LOW) for s in shapes]
        + [
            dma((count, 4, 4)),
            dma((count, 4, 4)),
            dma((count, 4, 4)),
            dma((count, 4)),
            dma((count, 4)),
            dma((count, 2, 4)),
            dma((count, 2, 4)),
            dma((count, 4)),
            dma((count, 5)),
        ]
        + line_scratch * len(lines),
        compiler_params=pltpu.CompilerParams(
            collective_id=collective_id, has_side_effects=True, vmem_limit_bytes=56 * 2**20
        ),
        cost_estimate=pl.CostEstimate(flops=100_000_000_000, bytes_accessed=0, transcendentals=0),
        name=name,
    )(*partials, *lines)


def exact(left, right, dims):
    return lax.dot_general(
        left, right, (dims, ((), ())), precision=lax.Precision.HIGHEST, preferred_element_type=FULL
    )


def joint_pattern():
    keys, queries = np.meshgrid(np.arange(CHUNK), np.arange(CHUNK), indexing="ij")
    at = (queries // SW - keys // SW + SW - 1) * SPAN_T + queries % SW - keys % SW + SW - 1
    return (jnp.arange(SPAN_T**2)[:, None] == jnp.asarray(at.reshape(-1), jnp.int32)[None, :]).astype(FULL)


def joint_table(lookup):
    flat = lookup.reshape(HEADS * (2 * TW - 1), SPAN_T**2)
    grid = exact(flat, joint_pattern(), ((1,), (0,)))
    grid = grid.reshape(HEADS // 2, 2, 2 * TW - 1, CHUNK, CHUNK)
    return jnp.concatenate([grid[:, 0], grid[:, 1]], axis=-1)


def joint_table_back(grad):
    pairs = jnp.stack([grad[..., :CHUNK], grad[..., CHUNK:]], axis=1)
    flat = pairs.reshape(HEADS * (2 * TW - 1), CHUNK * CHUNK)
    return exact(flat, joint_pattern(), ((1,), (1,))).reshape(HEADS, -1)


def space_pattern(quarter):
    query = jnp.arange(CHUNK)
    key_col = jnp.arange(2 * SW)
    gap = quarter % 2 * SW + (query % SW)[None, :] - key_col[:, None] + 2 * SW - 1
    row = jnp.broadcast_to((query // SW)[None, :], gap.shape)
    at = (row * SPAN_S + gap).reshape(-1)
    return (jnp.arange(SW * SPAN_S)[:, None] == at[None, :]).astype(FULL)


def space_table(lookup, quarter):
    grid = lookup.reshape(HEADS, SPAN_S, SPAN_S)
    seen = lax.dynamic_slice_in_dim(grid, quarter // 2 * SW, 3 * SW - 1, 1)
    rows = jnp.stack([seen[:, 2 * SW - 1 - k : 3 * SW - 1 - k] for k in range(2 * SW)])
    made = exact(rows.reshape(2 * SW * HEADS, SW * SPAN_S), space_pattern(quarter), ((1,), (0,)))
    made = made.reshape(2, SW, HEADS // 2, 2, 2, SW, CHUNK)
    made = made.transpose(2, 0, 4, 1, 5, 3, 6)
    return made.reshape(HEADS // 2, 4 * CHUNK, 2 * CHUNK)


def space_table_back(grad, quarter):
    made = grad.reshape(HEADS // 2, 2, 2, SW, SW, 2, CHUNK).transpose(1, 3, 0, 5, 2, 4, 6)
    flat = made.reshape(2 * SW * HEADS, 2 * SW * CHUNK)
    rows = exact(flat, space_pattern(quarter), ((1,), (1,))).reshape(2 * SW, HEADS, SW, SPAN_S)
    seen = sum(
        jnp.pad(rows[k], ((0, 0), (2 * SW - 1 - k, k), (0, 0))) for k in range(2 * SW)
    )
    grid = jnp.zeros((HEADS, SPAN_S, SPAN_S), FULL)
    return lax.dynamic_update_slice_in_dim(grid, seen, quarter // 2 * SW, 1).reshape(HEADS, -1)


def modulations(cond, shards):
    groups = cond.shape[0]
    rows = shards[0].shape[0]
    own = lax.dynamic_slice_in_dim(cond, lax.axis_index("wide") * rows, rows, 2)
    flat = own.reshape(groups * 2, rows)
    terms = jnp.stack([nn(flat, s).reshape(groups, 2, -1) for s in shards], axis=1)
    summed = lax.psum_scatter(terms, "wide", scatter_dimension=0, tiled=False)
    gathered = lax.all_gather(summed, "narrow", axis=0, tiled=False)
    return gathered.transpose(1, 2, 0, 3).reshape(2, 2, 6 * D)


def modulation_grads(cond, grads, rows):
    groups = cond.shape[0]
    own = lax.dynamic_slice_in_dim(cond, lax.axis_index("wide") * rows, rows, 2)
    flat = own.reshape(groups * 2, rows).astype(FULL)
    summed = lax.psum_scatter(
        grads.reshape(2, 2, 4, -1), "narrow", scatter_dimension=2, tiled=False
    )
    gathered = lax.all_gather(summed, "wide", axis=0, tiled=False)
    return [exact(flat, gathered[:, b].reshape(groups * 2, -1), ((0,), (0,))) for b in range(2)]


def gather_flat(shards):
    wide, narrow = lax.axis_size("wide"), lax.axis_size("narrow")
    project, output, expand, shrink = shards
    rows = project.shape[0]

    def settle(blocks):
        rows, cols = blocks.shape[-2:]
        blocks = blocks.reshape(wide, narrow, rows, cols).transpose(0, 2, 1, 3)
        return blocks.reshape(wide * rows, narrow * cols)

    first = lax.all_gather(
        jnp.concatenate([project, output, expand], axis=1), ("wide", "narrow"), axis=0, tiled=False
    )
    second = lax.all_gather(shrink, ("wide", "narrow"), axis=0, tiled=False)
    a, b = project.shape[1], project.shape[1] + output.shape[1]
    return settle(first[..., :a]), settle(first[..., a:b]), settle(first[..., b:]), settle(second)


def scatter_plain(partials):
    outs = []
    for g in partials:
        summed = lax.psum_scatter(g, "wide", scatter_dimension=0, tiled=True)
        outs.append(lax.psum_scatter(summed, "narrow", scatter_dimension=1, tiled=True).astype(FULL))
    return outs


def body(
    tokens,
    clip_cond,
    image_cond,
    image_count,
    space_modulate,
    space_project,
    space_output,
    space_expand,
    space_reduce,
    space_bias,
    joint_modulate,
    joint_project,
    joint_output,
    joint_expand,
    joint_reduce,
    joint_bias,
    cotangent,
):
    groups = lax.axis_size("wide")
    small = groups == 8
    narrow = lax.axis_index("narrow")
    quarter = narrow.reshape(1).astype(jnp.int32)
    live = (image_count > 0).astype(FULL)

    image_all = lax.all_gather(image_cond, "wide", axis=0, tiled=True)
    cond = jax.nn.silu(
        jnp.stack([jnp.repeat(clip_cond, 4, axis=0), image_all], axis=1).astype(FULL)
    ).astype(LOW)
    mods = modulations(cond, (space_modulate, joint_modulate))
    space_shards = (space_project, space_output, space_expand, space_reduce)
    joint_shards = (joint_project, joint_output, joint_expand, joint_reduce)
    if small:
        *space_weights, all_tokens = gather_weights(space_shards, tokens, 0, "space_gather")
        joint_weights = gather_weights(joint_shards, None, 3, "joint_gather")
    else:
        joint_weights = gather_flat(joint_shards)
        space_weights = gather_flat(space_shards)
        all_tokens = lax.all_gather(tokens, "narrow", axis=0, tiled=False)
    all_tokens = all_tokens.reshape(4 * ROWS_DEV, D)
    space_bias_table = space_table(space_bias, narrow)
    joint_bias_table = joint_table(joint_bias)

    project, output, expand, shrink = space_weights
    space_normed, space_queries, space_pairs = space_triple(quarter, all_tokens, mods[0], project)
    space_attended = space_attend(space_queries, space_pairs, space_bias_table)
    *space_saved, middle_rows = mlp(
        False, live, tokens, space_attended, mods[0], output, expand, shrink
    )

    project, output, expand, shrink = joint_weights
    joint_normed, joint_three = joint_triple(middle_rows, mods[1], project)
    joint_attended = joint_attend(joint_three, joint_bias_table)
    *joint_saved, output_tokens = mlp(
        True, live, middle_rows, joint_attended, mods[1], output, expand, shrink
    )

    grad_shrink, grad_expand, grad_output, grad_middle, grad_attended, late_mods = mlp_back(
        True, live, cotangent, joint_attended, mods[1], joint_saved, output, expand, shrink
    )
    grad_three, grad_table = joint_attend_back(joint_three, joint_bias_table, grad_attended)
    grad_project, grad_rows, early_mods = joint_project_back(
        middle_rows, mods[1], joint_normed, grad_middle, project, grad_three
    )
    joint_partials = (grad_shrink, grad_expand, grad_project, grad_output)
    joint_mods = jnp.concatenate([early_mods, late_mods[:, 2 * D :]], axis=1)
    joint_bias_grad = joint_table_back(grad_table)

    project, output, expand, shrink = space_weights
    grad_shrink, grad_expand, grad_output, grad_middle, grad_attended, late_mods = mlp_back(
        False, live, grad_rows, space_attended, mods[0], space_saved, output, expand, shrink
    )
    grad_q, grad_pairs, grad_table = space_attend_back(
        space_queries, space_pairs, space_bias_table, grad_attended
    )
    grad_project, grad_normed = space_project_back(quarter, space_normed, project, grad_q, grad_pairs)
    space_partials = (grad_shrink, grad_expand, grad_project, grad_output)
    space_bias_grad = space_table_back(grad_table, narrow)

    if small:
        joint_local = scatter_grads(joint_partials, None, 1, "joint_scatter")
        *space_local, own_normed = scatter_grads(space_partials, grad_normed, 2, "space_scatter")
    else:
        joint_local = scatter_plain(joint_partials)
        space_local = scatter_plain(space_partials)
        own_normed = lax.psum_scatter(grad_normed, "narrow", scatter_dimension=0, tiled=True)
    grad_tokens, early_mods = finish(tokens, mods[0], own_normed, grad_middle)
    space_mods = jnp.concatenate([early_mods, late_mods[:, 2 * D :]], axis=1)
    grad_space_modulate, grad_joint_modulate = modulation_grads(
        cond, jnp.stack([space_mods, joint_mods]), space_modulate.shape[0]
    )
    bias_grads = lax.psum(
        jnp.concatenate([space_bias_grad, joint_bias_grad], axis=1), ("wide", "narrow")
    )
    split = space_bias.shape[1]
    return (
        output_tokens,
        grad_tokens,
        grad_space_modulate,
        space_local[2],
        space_local[3],
        space_local[1],
        space_local[0],
        bias_grads[:, :split],
        grad_joint_modulate,
        joint_local[2],
        joint_local[3],
        joint_local[1],
        joint_local[0],
        bias_grads[:, split:],
    )


def solution(mesh):
    rows = P(("wide", "narrow"), None)
    block = P("wide", "narrow")
    in_specs = (
        (rows, P(), P("wide", None), P("wide"))
        + (block,) * 5
        + (P(),)
        + (block,) * 5
        + (P(), rows)
    )
    out_specs = (rows, rows) + ((block,) * 5 + (P(),)) * 2
    return jax.shard_map(body, mesh=mesh, in_specs=in_specs, out_specs=out_specs, check_vma=False)
```

time: 2910 us -> 971 us (0.33)
  other arithmetic: 936 us -> 7.46 us
  Pallas kernels: 0 us -> 847 us
  waiting for transfers between devices: 790 us -> 0.07 us
  local copies, waits for them, and re-layouts: 641 us -> 48.1 us
  matrix products: 382 us -> 10.1 us
  blocking collectives: 128 us -> 33.1 us
    pallas_call x0 -> x17, Pallas kernels: none -> 847 us  [the longest x2 280 us: scatter_grads(): pl.pallas_call(functools.partial(scatter_kernel, shapes, bool(lines)), ou...]
    scatter-add x11 -> x0, other arithmetic: 808 us -> none  [the longest x1 543 us: joint_back(): values[:, joint_index(TW)]]
    reduce_scatter x21 -> x0, waiting for transfers between devices: 584 us -> none  [the longest x2 266 us: settle(): lax.psum_scatter(grads[0], 'wide', scatter_dimension=0, tiled=True)]
    gather x14 -> x0, local copies, waits for them, and re-layouts: 480 us -> none  [the longest x2 374 us: joint_attention(): lookup[:, joint_index(TW)]]
    dot_general x44 -> x8, matrix products: 370 us -> 10.1 us  [the longest x6 8.8 us: exact(): lax.dot_general(left, right, (dims, ((), ())), precision=lax.Precision.HI...]
    all_gather x17 -> x0, waiting for transfers between devices: 202 us -> none  [the longest x2 72.5 us: collect_weights(): lax.all_gather(partial_rows[0], 'wide', axis=0, tiled=True)]
    convert_element_type x30 -> x2, other arithmetic: 73 us -> 0.03 us  [the longest x1 0.02 us: body(): cond = jax.nn.silu(jnp.stack([jnp.repeat(clip_cond, 4, axis=0), image_all...]
    all_gather x4 -> x3, blocking collectives: 82.1 us -> 33.1 us  [the longest x1 13.3 us: modulations(): gathered = lax.all_gather(summed, 'narrow', axis=0, tiled=False)]
  transfers between devices with their start and end apart: 39 -> 3, of which waited for: 19 -> 0; matrix products, arithmetic and copies ran while one was open for 59% -> 3% of each run, Pallas kernels for 0% -> 59%
where the time goes in v1:
time: 971 us; the launch traced here: 961 us
  Pallas kernels  847 us (87%)
  local copies, waits for them, and re-layouts  48.1 us (5%)
  blocking collectives  33.1 us (3%)
  between operations  15.4 us (2%)
  matrix products  10.1 us (1%)
    pallas_call x2, Pallas kernels, scatter_grads(): pl.pallas_call(functools.partial(scatter_kernel, shapes, bool(lines)), ou...  280 us
    pallas_call x2, Pallas kernels, gather_weights(): pl.pallas_call(functools.partial(gather_kernel, shapes, bool(lines)), out...  251 us
    pallas_call x2, Pallas kernels, mlp_back(): pl.pallas_call(functools.partial(mlp_back_kernel, first_block), grid=(FF...  82.3 us
    pallas_call x2, Pallas kernels, mlp(): pl.pallas_call(functools.partial(mlp_kernel, last_block), grid=(FF // til...  55.8 us
    pallas_call x1, Pallas kernels, space_project_back(): pl.pallas_call(space_project_back_kernel, grid=(3,), in_specs=[pl.BlockSp...  31.5 us
    pallas_call x1, Pallas kernels, space_attend_back(): pl.pallas_call(space_attend_back_kernel, grid=(HEADS // 2,), in_specs=[he...  29.3 us
    pallas_call x1, Pallas kernels, joint_attend_back(): pl.pallas_call(joint_attend_back_kernel, grid=(HEADS // 2,), in_specs=joi...  27.1 us
    pallas_call x1, Pallas kernels, space_triple(): pl.pallas_call(space_triple_kernel, grid=(3 * D // tile,), in_specs=[pl.B...  26.5 us
  transfers between devices with their start and end apart: 3, of which 0 were waited for; matrix products, arithmetic and copies ran while one was open for 3% of the time, Pallas kernels for 59%

profile of v1, /device:TPU:0, one launch (start us, length us, event | category | flops | bytes accessed | tf_op | source)
XLA Modules:
  0.0 961.1 jit_solution(14386394479591514568)
XLA Ops:
  7.3 10.8 %all-gather.1 = bf16[8,1,1024]{2,1,0:T(2,128)(2,1)S(1)} all-gather(bf16[1,1,1024]{2,1,0:T(2,128)(2,1)} %bitcast.147), channel_id=1, replica_groups=mesh['wide'=8,'narrow'=4] {'wide'}, dimensions={0}, use_global_device_ids=true | all-gather | bytes 18432 | tf_op jit(solution)/shard_map/all_gather | solution.py:1349
  18.1 0.7 broadcast_in_dim.6
  19.0 1.2 convolution_bitcast_fusion.2
  20.2 0.8 copy.60
  21.1 0.6 copy.66
  22.7 0.3 reshape.200
  23.5 0.5 reshape.218
  24.1 1.0 convolution_bitcast_fusion.3
  25.1 1.6 copy.63
  26.7 2.2 reshape.201.bias
  29.0 1.8 convolution_bitcast_fusion
  30.8 3.6 reshape.203
  34.5 5.3 slice_bitcast_fusion.1
  39.8 0.6 dynamic-slice
  40.4 0.6 dynamic-slice.2
  41.0 114.2 %joint_gather.1 = (bf16[1024,3072]{1,0:T(8,128)(2,1)}, bf16[1024,1024]{1,0:T(8,128)(2,1)}, bf16[1024,4096]{1,0:T(8,128)(2,1)}, bf16[4096,1024]{1,0:T(8,128)(2,1)}) custom-call(bf16[128,768]{1,0:T(8,128)(2,1)} %refs_0_.4, bf16[128,256]{1,0:T(8,128)(2,1)} %refs_1_.3, bf16[128,1024]{1,0:T(8,128)(2,1)} %refs_2_.3, bf16[512,256]{1,0:T(8,128)(2,1)} %refs_3_.3), custom_call_target="tpu_custom_call" | custom-call | flops 99999997952 | tf_op jit(solution)/shard_map/joint_gather/pallas_call | solution.py:890
  155.2 136.9 %space_gather.1 = (bf16[1024,3072]{1,0:T(8,128)(2,1)}, bf16[1024,1024]{1,0:T(8,128)(2,1)}, bf16[1024,4096]{1,0:T(8,128)(2,1)}, bf16[4096,1024]{1,0:T(8,128)(2,1)}, bf16[4,576,1024]{2,1,0:T(8,128)(2,1)}) custom-call(bf16[128,768]{1,0:T(8,128)(2,1)} %refs_0_.3, bf16[128,256]{1,0:T(8,128)(2,1)} %refs_1_.2, bf16[128,1024]{1,0:T(8,128)(2,1)} %refs_2_.2, ...), custom_call_target="tpu_custom_call" | custom-call | flops 99999997952 | tf_op jit(solution)/shard_map/space_gather/pallas_call | solution.py:890
  292.1 3.8 pad_maximum_fusion.1.bias
  295.9 1.4 constant_dynamic-slice_fusion
  297.3 13.3 %all_gather.10 = f32[4,2,2,1536]{3,2,1,0:T(2,128)S(1)} all-gather(f32[1,2,2,1536]{3,2,1,0:T(2,128)S(1)} %constant_dynamic-slice_fusion), channel_id=1, replica_groups=mesh['wide'=8,'narrow'=4] {'narrow'}, dimensions={0}, use_global_device_ids=true | all-gather | bytes 122880 | tf_op jit(solution)/shard_map/all_gather | solution.py:1283
  310.6 0.6 fusion.28
  311.2 26.5 %space_triple.1 = (bf16[2304,1024]{1,0:T(8,128)(2,1)}, bf16[576,1024]{1,0:T(8,128)(2,1)}, bf16[4,576,2048]{2,1,0:T(8,128)(2,1)}) custom-call(s32[1]{0:T(128)} %bitcast.quarter, bf16[2304,1024]{1,0:T(8,128)(2,1)} %bitcast.130, f32[2,6144]{1,0:T(2,128)} %bitcast.131, bf16[1024,3072]{1,0:T(8,128)(2,1)} %get-tuple-element.76.weight), custom_call_target="tpu_custom_call" | custom-call | tf_op jit(solution)/shard_map/space_triple/pallas_call | solution.py:112
  337.7 11.7 %space_attend.1.attended.refs_1_ = bf16[576,1024]{1,0:T(8,128)(2,1)} custom-call(bf16[576,1024]{1,0:T(8,128)(2,1)} %get-tuple-element.77.queries, bf16[4,576,2048]{2,1,0:T(8,128)(2,1)} %get-tuple-element.78.keys.values, bf16[4,576,2048]{2,1,0:T(8,128)(2,1)} %get-tuple-element.78.keys.values, f32[8,256,128]{2,1,0:T(8,128)} %reshape.201.bias), custom_call_target="tpu_custom_call" | custom-call | tf_op jit(solution)/shard_map/space_attend/pallas_call | solution.py:209
  349.4 27.8 %mlp.2 = (bf16[576,1024]{1,0:T(8,128)(2,1)}, f32[576,1024]{1,0:T(8,128)}, bf16[576,1024]{1,0:T(8,128)(2,1)}, bf16[576,4096]{1,0:T(8,128)(2,1)}, bf16[576,4096]{1...) custom-call(f32[1]{0:T(128)S(6)} %convert_element_type.37.live, bf16[576,1024]{1,0:T(8,128)(2,1)} %rows.3, ...), custom_call_target="tpu_custom_call" | custom-call | tf_op jit(solution)/shard_map/mlp/pallas_call | solution.py:391
  377.3 11.0 %joint_triple.1 = (bf16[576,1024]{1,0:T(8,128)(2,1)}, bf16[576,3072]{1,0:T(8,128)(2,1)}) custom-call(f32[576,1024]{1,0:T(8,128)} %get-tuple-element.82.rows, f32[2,6144]{1,0:T(2,128)} %bitcast.135, bf16[1024,3072]{1,0:T(8,128)(2,1)} %get-tuple-element.83.weight), custom_call_target="tpu_custom_call" | custom-call | tf_op jit(solution)/shard_map/joint_triple/pallas_call | solution.py:150
  388.3 15.1 %joint_attend.1.attended.refs_1_ = bf16[576,1024]{1,0:T(8,128)(2,1)} custom-call(bf16[576,3072]{1,0:T(8,128)(2,1)} %get-tuple-element.84.queries.keys.values, bf16[576,3072]{1,0:T(8,128)(2,1)} %get-tuple-element.84.queries.keys.values, bf16[576,3072]{1,0:T(8,128)(2,1)} %get-tuple-element.84.queries.keys.values, f32[8,9,64,128]{3,2,1,0:T(8,128)} %pad_maximum_fusion.1.bias), custom_call_target="tpu_custom_call" | custom-call | tf_op jit(solution)/shard_map/joint_attend/pallas_call | solution.py:292
  403.3 27.9 %mlp.3 = (bf16[576,1024]{1,0:T(8,128)(2,1)}, f32[576,1024]{1,0:T(8,128)}, bf16[576,1024]{1,0:T(8,128)(2,1)}, bf16[576,4096]{1,0:T(8,128)(2,1)}, bf16[576,4096]{1...) custom-call(f32[1]{0:T(128)S(6)} %convert_element_type.37.live, ...), custom_call_target="tpu_custom_call" | custom-call | tf_op jit(solution)/shard_map/mlp/pallas_call | solution.py:391
  431.3 41.2 %mlp_back.2 = (bf16[4096,1024]{1,0:T(8,128)(2,1)}, bf16[1024,4096]{1,0:T(8,128)(2,1)}, bf16[1024,1024]{1,0:T(8,128)(2,1)}, f32[576,1024]{1,0:T(8,128)}, bf16[576,1024]{1,0:T(8,128)(2,1)}, /*index=5*/f32[2,6144]{1,0:T(2,128)}) custom-call(f32[1]{0:T(128)S(6)} %convert_element_type.37.live, bf16[576,1024]{1,0:T(8,128)(2,1)} %refs_0_.5, ...), custom_call_target="tpu_custom_call" | custom-call | tf_op jit(solution)/shard_map/mlp_back/pallas_call | solution.py:479
  472.5 27.1 %joint_attend_back.1 = (bf16[3,576,1024]{2,1,0:T(8,128)(2,1)}, f32[8,9,64,128]{3,2,1,0:T(8,128)}) custom-call(bf16[576,3072]{1,0:T(8,128)(2,1)} %get-tuple-element.84.queries.keys.values, bf16[576,3072]{1,0:T(8,128)(2,1)} %get-tuple-element.84.queries.keys.values, bf16[576,3072]{1,0:T(8,128)(2,1)} %get-tuple-element.84.queries.keys.values, ...), custom_call_target="tpu_custom_call" | custom-call | tf_op jit(solution)/shard_map/joint_attend_back/pallas_call | solution.py:336
  499.5 18.4 %joint_project_back.1 = (bf16[1024,3072]{1,0:T(8,128)(2,1)}, f32[576,1024]{1,0:T(8,128)}, f32[2,2048]{1,0:T(2,128)}) custom-call(f32[576,1024]{1,0:T(8,128)} %get-tuple-element.82.rows, f32[2,6144]{1,0:T(2,128)} %bitcast.138, bf16[576,1024]{1,0:T(8,128)(2,1)} %get-tuple-element.89.normed, f32[576,1024]{1,0:T(8,128)} %get-tuple-element.96.grad_middle, ...), custom_call_target="tpu_custom_call" | custom-call | tf_op jit(solution)/shard_map/joint_project_back/pallas_call | solution.py:554
  517.9 41.1 %mlp_back.3 = (bf16[4096,1024]{1,0:T(8,128)(2,1)}, bf16[1024,4096]{1,0:T(8,128)(2,1)}, bf16[1024,1024]{1,0:T(8,128)(2,1)}, f32[576,1024]{1,0:T(8,128)}, bf16[576,1024]{1,0:T(8,128)(2,1)}, /*index=5*/f32[2,6144]{1,0:T(2,128)}) custom-call(f32[1]{0:T(128)S(6)} %convert_element_type.37.live, f32[576,1024]{1,0:T(8,128)} %get-tuple-element.99.refs_0_, ...), custom_call_target="tpu_custom_call" | custom-call | tf_op jit(solution)/shard_map/mlp_back/pallas_call | solution.py:479
  559.0 29.3 %space_attend_back.1 = (bf16[576,1024]{1,0:T(8,128)(2,1)}, bf16[2,4,576,1024]{3,2,1,0:T(8,128)(2,1)}, f32[8,256,128]{2,1,0:T(8,128)}) custom-call(bf16[576,1024]{1,0:T(8,128)(2,1)} %get-tuple-element.77.queries, bf16[4,576,2048]{2,1,0:T(8,128)(2,1)} %get-tuple-element.78.keys.values, bf16[4,576,2048]{2,1,0:T(8,128)(2,1)} %get-tuple-element.78.keys.values, ...), custom_call_target="tpu_custom_call" | custom-call | tf_op jit(solution)/shard_map/space_attend_back/pallas_call | solution.py:248
  588.4 0.9 slice_bitcast_fusion.3
  589.4 1.0 pad_maximum_fusion
  590.3 2.9 copy.87
  593.2 3.8 reshape.208
  597.1 2.4 fusion
  599.6 2.9 reshape.205
  602.5 1.6 copy.99
  604.2 2.0 reshape.206
  606.2 0.8 fusion.3
  607.0 0.5 fusion.26
  610.3 0.3 dynamic_update_slice.3
  610.8 0.8 pad_maximum_fusion.3
  611.7 31.5 %space_project_back.1 = (bf16[1024,3072]{1,0:T(8,128)(2,1)}, bf16[2304,1024]{1,0:T(8,128)(2,1)}) custom-call(s32[1]{0:T(128)} %bitcast.quarter, bf16[2304,1024]{1,0:T(8,128)(2,1)} %get-tuple-element.108.normed, bf16[1024,3072]{1,0:T(8,128)(2,1)} %get-tuple-element.76.weight, bf16[576,1024]{1,0:T(8,128)(2,1)} %get-tuple-element.110.grad_q, ...), custom_call_target="tpu_custom_call" | custom-call | tf_op jit(solution)/shard_map/space_project_back/pallas_call | solution.py:592
  643.2 149.9 %space_scatter.1 = (f32[512,256]{1,0:T(8,128)}, f32[128,1024]{1,0:T(8,128)}, f32[128,768]{1,0:T(8,128)}, f32[128,256]{1,0:T(8,128)}, f32[576,1024]{1,0:T(8,128)}) custom-call(bf16[4096,1024]{1,0:T(8,128)(2,1)} %get-tuple-element.106.refs_0_, bf16[1024,4096]{1,0:T(8,128)(2,1)} %get-tuple-element.107.refs_1_, bf16[1024,3072]{1,0:T(8,128)(2,1)} %get-tuple-element.112.refs_2_, ...), custom_call_target="tpu_custom_call" | custom-call | flops 99999997952 | tf_op jit(solution)/shard_map/space_scatter/pallas_call | solution.py:1191
  793.1 7.1 finish.1
  800.2 0.7 pad_maximum_fusion.5
  800.9 0.7 pad_maximum_fusion.4
  801.7 130.1 %joint_scatter.1 = (f32[512,256]{1,0:T(8,128)}, f32[128,1024]{1,0:T(8,128)}, f32[128,768]{1,0:T(8,128)}, f32[128,256]{1,0:T(8,128)}) custom-call(bf16[4096,1024]{1,0:T(8,128)(2,1)} %get-tuple-element.128.refs_0_, bf16[1024,4096]{1,0:T(8,128)(2,1)} %get-tuple-element.129.refs_1_, bf16[1024,3072]{1,0:T(8,128)(2,1)} %get-tuple-element.130.refs_2_, ...), custom_call_target="tpu_custom_call" | custom-call | flops 99999997952 | tf_op jit(solution)/shard_map/joint_scatter/pallas_call | solution.py:1191
  931.8 1.6 slice.221
  933.4 1.7 slice.223
  935.0 1.4 dynamic-slice_bitcast_fusion.16
  936.4 9.0 all-gather
  945.6 1.4 fusion.29
  947.0 1.4 fusion.30
  948.4 0.7 copy.130
  949.2 0.7 copy.131
  949.8 0.8 copy.132
  950.6 0.8 copy.133
  951.4 0.7 copy.134
  952.2 0.7 copy.135
  952.8 0.8 copy.136
  953.6 0.8 copy.137
  (126 shorter events, 4.5 us)
Async XLA Ops:
  7.2 11.6 %copy-start = (bf16[128,1536]{1,0:T(8,128)(2,1)S(1)}, bf16[128,1536]{1,0:T(8,128)(2,1)}, u32[]{:S(2)}) copy-start(bf16[128,1536]{1,0:T(8,128)(2,1)} %param.29) | copy-start | bytes 1179652
  7.2 15.5 %copy-start.15 = (f32[16,961]{1,0:T(8,128)S(1)}, f32[16,961]{1,0:T(8,128)}, u32[]{:S(2)}) copy-start(f32[16,961]{1,0:T(8,128)} %param.28) | copy-start | bytes 184516
  7.2 288.7 %all-reduce.24.cloned.1.call-start = ((), (), s32[]{:S(2)}) async-start(), calls=%async_computation.1 | async-start | bytes 393216
  21.0 910.8 %all-reduce.22.cloned.1.call-start = ((), (), s32[]{:S(2)}) async-start(), calls=%async_computation | async-start | bytes 393216 | tf_op jit(solution)/shard_map/psum | solution.py:1415
  22.5 0.6 copy-start.16
  26.7 2.2 copy-start.10
  26.7 2.3 copy-start.13
  34.5 5.3 copy-start.23
  34.5 5.9 copy-start.22
  155.2 136.9 %copy-start.3 = (f32[8,9,64,64]{3,2,1,0:T(8,128)S(1)}, f32[8,9,64,64]{3,2,1,0:T(8,128)}, u32[]{:S(2)}) copy-start(f32[8,9,64,64]{3,2,1,0:T(8,128)} %get-tuple-element.136) | copy-start | bytes 3538948
  559.0 29.4 %copy-start.19 = (f32[2,6144]{1,0:T(2,128)S(1)}, f32[2,6144]{1,0:T(2,128)}, u32[]{:S(2)}) copy-start(f32[2,6144]{1,0:T(2,128)} %get-tuple-element.121) | copy-start | bytes 147460
  559.0 29.4 %copy-start.20 = (f32[2,6144]{1,0:T(2,128)S(1)}, f32[2,6144]{1,0:T(2,128)}, u32[]{:S(2)}) copy-start(f32[2,6144]{1,0:T(2,128)} %get-tuple-element.119) | copy-start | bytes 147460
  559.0 29.4 %copy-start.2 = (f32[8,9,64,128]{3,2,1,0:T(8,128)S(1)}, f32[8,9,64,128]{3,2,1,0:T(8,128)}, u32[]{:S(2)}) copy-start(f32[8,9,64,128]{3,2,1,0:T(8,128)} %get-tuple-element.127) | copy-start | bytes 7077892
  593.2 3.9 copy-start.14
  604.2 2.0 copy-start.17
  611.6 323.4 %all-reduce.26.cloned.1.call-start = ((), (), s32[]{:S(2)}) async-start(), calls=%async_computation.2 | async-start | bytes 196608
  793.0 7.1 copy-start.21
  801.7 143.9 %copy-start.18 = (bf16[8,2,128]{2,1,0:T(2,128)(2,1)S(1)}, bf16[8,2,128]{2,1,0:T(2,128)(2,1)}, u32[]{:S(2)}) copy-start(bf16[8,2,128]{2,1,0:T(2,128)(2,1)} %copy.66) | copy-start | bytes 12292
  931.7 16.7 %copy-start.8 = (f32[128,768]{1,0:T(8,128)S(1)}, f32[128,768]{1,0:T(8,128)}, u32[]{:S(2)}) copy-start(f32[128,768]{1,0:T(8,128)} %get-tuple-element.179) | copy-start | bytes 1179652
  931.8 17.4 %copy-start.11 = (f32[128,256]{1,0:T(8,128)S(1)}, f32[128,256]{1,0:T(8,128)}, u32[]{:S(2)}) copy-start(f32[128,256]{1,0:T(8,128)} %get-tuple-element.180) | copy-start | bytes 393220
  931.8 18.1 %copy-start.5 = (f32[128,1024]{1,0:T(8,128)S(1)}, f32[128,1024]{1,0:T(8,128)}, u32[]{:S(2)}) copy-start(f32[128,1024]{1,0:T(8,128)} %get-tuple-element.181) | copy-start | bytes 1572868
  945.4 5.2 copy-start.4
  945.6 5.8 copy-start.9
  947.0 5.2 copy-start.12
  947.0 5.8 copy-start.7
  949.2 4.5 copy-start.6
  949.8 4.6 copy-start.1
Sparse Core Ops, SparseCore 0:
  21.2 53.8 all-reduce.23
  611.7 123.7 all-reduce.21
  801.8 34.4 all-reduce.25

commit v2 on v1

v2 whole, which is shorter than its diff:
```python
import functools
import math

import jax
import jax.numpy as jnp
import numpy as np
from jax import lax
from jax.experimental import pallas as pl
from jax.experimental.pallas import tpu as pltpu
from jax.sharding import PartitionSpec as P

D = 1024
HEADS = 16
HEAD_DIM = 64
FF = 4096
SW = 8
TW = 5
CHUNK = SW * SW
CLIP_ROWS = TW * CHUNK
ROWS_DEV = CLIP_ROWS + 4 * CHUNK
SPAN_S = 4 * SW - 1
SPAN_T = 2 * SW - 1
MESH = pl.DeviceIdType.MESH


epsilon = 1e-06


def normalise(values):
    centred = values - jnp.mean(values, axis=-1, keepdims=True)
    spread = jnp.mean(centred * centred, axis=-1, keepdims=True)
    scale = lax.rsqrt(spread + epsilon)
    return centred * scale, scale


def norm_back(unit, scale, grad):
    return scale * (
        grad
        - jnp.mean(grad, axis=-1, keepdims=True)
        - unit * jnp.mean(grad * unit, axis=-1, keepdims=True)
    )


def nn(left, right):
    return lax.dot_general(left, right, (((1,), (0,)), ((), ())), preferred_element_type=jnp.float32)


def nt(left, right):
    return lax.dot_general(left, right, (((1,), (1,)), ((), ())), preferred_element_type=jnp.float32)


def tn(left, right):
    return lax.dot_general(left, right, (((0,), (0,)), ((), ())), preferred_element_type=jnp.float32)


def each_chunk(body, count=ROWS_DEV // CHUNK):
    @pl.loop(0, count)
    def _(i):
        inner = lax.rem(i, ROWS_DEV // CHUNK)
        seq = jnp.where(inner >= CLIP_ROWS // CHUNK, 1, 0)
        body(pl.ds(pl.multiple_of(i * CHUNK, CHUNK), CHUNK), pl.ds(seq, 1))


def part(index):
    return slice(index * D, (index + 1) * D)


class Tiled:
    def __init__(self, block, index):
        self.block, self.index = block, index

    def spec(self):
        return pl.BlockSpec(self.block, self.index)


class Whole:
    def __init__(self, block):
        self.block = block

    def spec(self):
        rank = len(self.block)
        return pl.BlockSpec(self.block, lambda *_: (0,) * rank, pipeline_mode=pl.Buffered(1))


class Scalars:
    def spec(self):
        return pl.BlockSpec(memory_space=pltpu.SMEM)


SCALARS = Scalars()
whole, spec = Whole, Tiled


def params(limit=56):
    return pltpu.CompilerParams(vmem_limit_bytes=limit * 2**20)


def shape(dims, kind):
    return jax.ShapeDtypeStruct(dims, kind)


LOW = jnp.bfloat16
FULL = jnp.float32


class Phase:
    def __init__(self, kernel, *, grid, in_specs, out_specs, out_shape, name, ticks=1, scratch_shapes=()):
        self.kernel, self.grid, self.name, self.ticks = kernel, grid, name, ticks
        self.in_specs, self.out_specs, self.out_shape = in_specs, out_specs, out_shape
        self.scratch = list(scratch_shapes)

    def __call__(self, *args):
        return pl.pallas_call(
            functools.partial(self.kernel, lambda t: None),
            grid=self.grid,
            in_specs=[s.spec() for s in self.in_specs],
            out_specs=[s.spec() for s in self.out_specs],
            out_shape=self.out_shape,
            scratch_shapes=self.scratch,
            compiler_params=params(),
            name=self.name,
        )(*args)

    def inside(self, tick, ins, outs):
        specs = list(self.in_specs) + list(self.out_specs)
        refs = list(ins) + list(outs)
        first_out = len(ins)
        held = [i for i, s in enumerate(specs) if isinstance(s, Whole)]
        tiled = [i for i, s in enumerate(specs) if isinstance(s, Tiled)]

        def scoped(buffers, scratch, sems):
            place = dict(zip(held, buffers))
            loads = [
                pltpu.make_async_copy(refs[i], place[i], sems.at[at])
                for at, i in enumerate(held)
                if i < first_out
            ]
            for load in loads:
                load.start()
            for load in loads:
                load.wait()

            def body(*blocks):
                now = dict(zip(tiled, blocks))
                now.update(place)
                operands = [now.get(i, refs[i]) for i in range(len(refs))]
                self.kernel(tick, *operands, *scratch)

            pltpu.emit_pipeline(
                body,
                grid=self.grid,
                in_specs=[specs[i].spec() for i in tiled if i < first_out],
                out_specs=[specs[i].spec() for i in tiled if i >= first_out],
            )(*[refs[i] for i in tiled])
            stores = [
                pltpu.make_async_copy(place[i], refs[i], sems.at[at])
                for at, i in enumerate(held)
                if i >= first_out
            ]
            for store in stores:
                store.start()
            for store in stores:
                store.wait()

        kinds = [refs[i].dtype for i in held]
        pl.run_scoped(
            scoped,
            [pltpu.VMEM(specs[i].block, kind) for i, kind in zip(held, kinds)],
            self.scratch,
            pltpu.SemaphoreType.DMA((len(held),)),
        )


def space_triple_kernel(tick, rows, mods, weight, normed, queries, pairs):
    step = pl.program_id(0)

    @pl.when(step == 0)
    def _():
        def chunk(at, seq):
            unit, _ = normalise(rows[at, :].astype(FULL))
            normed[at, :] = (unit * (1.0 + mods[seq, part(1)]) + mods[seq, part(0)]).astype(LOW)

        each_chunk(chunk, 4 * ROWS_DEV // CHUNK)

    tick(0)

    @pl.when(step < 2)
    def _():
        own = span(lax.axis_index("narrow"), ROWS_DEV)
        queries[...] = nn(normed[own, :], weight[...]).astype(LOW)

    for q in range(4):
        if q:
            tick(q)

        @pl.when(step >= 2)
        def _():
            pairs[q] = nn(normed[q * ROWS_DEV : (q + 1) * ROWS_DEV, :], weight[...]).astype(LOW)


def space_triple():
    tile = 512
    return Phase(
        space_triple_kernel,
        grid=(3 * D // tile,),
        in_specs=[
            whole((4 * ROWS_DEV, D)),
            whole((2, 6 * D)),
            spec((D, tile), lambda t: (0, t)),
        ],
        out_specs=[
            whole((4 * ROWS_DEV, D)),
            spec((ROWS_DEV, tile), lambda t: (0, jnp.minimum(t, 1))),
            spec((4, ROWS_DEV, tile), lambda t: (0, 0, jnp.maximum(t - 2, 0))),
        ],
        out_shape=[
            shape((4 * ROWS_DEV, D), LOW),
            shape((ROWS_DEV, D), LOW),
            shape((4, ROWS_DEV, 2 * D), LOW),
        ],
        name="space_triple",
        ticks=4,
    )


def joint_triple_kernel(tick, rows, mods, weight, normed, triple):
    @pl.when(pl.program_id(0) == 0)
    def _():
        def chunk(at, seq):
            unit, _ = normalise(rows[at, :])
            normed[at, :] = (unit * (1.0 + mods[seq, part(1)]) + mods[seq, part(0)]).astype(LOW)

        each_chunk(chunk)

    tick(0)
    triple[...] = nn(normed[...], weight[...]).astype(LOW)


def joint_triple():
    tile = 512
    return Phase(
        joint_triple_kernel,
        grid=(3 * D // tile,),
        in_specs=[whole((ROWS_DEV, D)), whole((2, 6 * D)), spec((D, tile), lambda t: (0, t))],
        out_specs=[whole((ROWS_DEV, D)), spec((ROWS_DEV, tile), lambda t: (0, t))],
        out_shape=[shape((ROWS_DEV, D), LOW), shape((ROWS_DEV, 3 * D), LOW)],
        name="joint_triple",
        ticks=1,
    )


def half_mask():
    return lax.broadcasted_iota(jnp.int32, (1, 2 * HEAD_DIM), 1) < HEAD_DIM


def split_heads(rows):
    first = half_mask()
    zero = jnp.zeros_like(rows)
    return jnp.concatenate([jnp.where(first, rows, zero), jnp.where(first, zero, rows)], axis=0)


def join_heads(stacked):
    return jnp.where(half_mask(), stacked[:CHUNK], stacked[CHUNK:])


def softmax_keys(keys, queries, bias):
    scores = nt(keys, queries) * HEAD_DIM**-0.5 + bias
    powered = jnp.exp(scores - jnp.max(scores, axis=0, keepdims=True))
    return powered / jnp.sum(powered, axis=0, keepdims=True)


def attend(queries, keys, values, bias):
    probs = softmax_keys(keys, split_heads(queries), bias)
    return join_heads(tn(values, probs.astype(LOW)).T).astype(LOW)


def attend_back(queries, keys, values, bias, grad):
    queries, grad = split_heads(queries), split_heads(grad)
    probs = softmax_keys(keys, queries, bias)
    grad_values = nn(probs.astype(LOW), grad)
    grad_probs = nt(values, grad)
    centre = jnp.sum(probs * grad_probs, axis=0, keepdims=True)
    grad_scores = (probs * (grad_probs - centre)).astype(LOW)
    grad_queries = join_heads(tn(keys, grad_scores).T) * HEAD_DIM**-0.5
    grad_keys = nn(grad_scores, queries) * HEAD_DIM**-0.5
    return grad_queries, grad_keys, grad_values, grad_scores.astype(FULL)


def space_attend_kernel(tick, queries, keys, values, bias, out):
    table = bias[0]
    for i in range(ROWS_DEV // CHUNK):
        if i % 3 == 0:
            tick(i // 3)
        at = slice(i * CHUNK, (i + 1) * CHUNK)
        key_rows = keys[:, at, :].reshape(4 * CHUNK, 2 * HEAD_DIM)
        value_rows = values[:, at, :].reshape(4 * CHUNK, 2 * HEAD_DIM)
        out[at, :] = attend(queries[at, :], key_rows, value_rows, table)


def space_attend():
    wide = 2 * HEAD_DIM
    return Phase(
        space_attend_kernel,
        grid=(HEADS // 2,),
        in_specs=[
            spec((ROWS_DEV, wide), lambda h: (0, h)),
            spec((4, ROWS_DEV, wide), lambda h: (0, 0, h)),
            spec((4, ROWS_DEV, wide), lambda h: (0, 0, h + HEADS // 2)),
            spec((1, 4 * CHUNK, wide), lambda h: (h, 0, 0)),
        ],
        out_specs=[spec((ROWS_DEV, wide), lambda h: (0, h))],
        out_shape=[shape((ROWS_DEV, D), LOW)],
        name="space_attend",
        ticks=3,
    )


def space_attend_back_kernel(tick, queries, keys, values, bias, grad, grad_q, grad_pairs, grad_bias):
    table = bias[0]
    for i in range(ROWS_DEV // CHUNK):
        if i % 3 == 0:
            tick(i // 3)
        at = slice(i * CHUNK, (i + 1) * CHUNK)
        key_rows = keys[:, at, :].reshape(4 * CHUNK, 2 * HEAD_DIM)
        value_rows = values[:, at, :].reshape(4 * CHUNK, 2 * HEAD_DIM)
        to_q, to_k, to_v, to_bias = attend_back(
            queries[at, :], key_rows, value_rows, table, grad[at, :]
        )
        grad_q[at, :] = to_q.astype(LOW)
        grad_pairs[0, :, at, :] = to_k.astype(LOW).reshape(4, CHUNK, 2 * HEAD_DIM)
        grad_pairs[1, :, at, :] = to_v.astype(LOW).reshape(4, CHUNK, 2 * HEAD_DIM)
        if i == 0:
            grad_bias[0] = to_bias
        else:
            grad_bias[0] += to_bias


def space_attend_back():
    wide = 2 * HEAD_DIM
    head = spec((ROWS_DEV, wide), lambda h: (0, h))
    four = spec((4, ROWS_DEV, wide), lambda h: (0, 0, h))
    table = spec((1, 4 * CHUNK, wide), lambda h: (h, 0, 0))
    return Phase(
        space_attend_back_kernel,
        grid=(HEADS // 2,),
        in_specs=[
            head,
            four,
            spec((4, ROWS_DEV, wide), lambda h: (0, 0, h + HEADS // 2)),
            table,
            head,
        ],
        out_specs=[head, spec((2, 4, ROWS_DEV, wide), lambda h: (0, 0, 0, h)), table],
        out_shape=[
            shape((ROWS_DEV, D), LOW),
            shape((2, 4, ROWS_DEV, D), LOW),
            shape((HEADS // 2, 4 * CHUNK, wide), FULL),
        ],
        name="space_attend_back",
        ticks=3,
    )


def clip_table(bias, frame):
    return jnp.concatenate([bias[0, frame - t + TW - 1] for t in range(TW)], axis=0)


def joint_attend_kernel(tick, queries, keys, values, bias, out):
    for i in range(ROWS_DEV // CHUNK):
        if i % 3 == 0:
            tick(i // 3)
        at = slice(i * CHUNK, (i + 1) * CHUNK)
        seen = slice(0, CLIP_ROWS) if i < TW else at
        table = clip_table(bias, i) if i < TW else bias[0, TW - 1]
        out[at, :] = attend(queries[at, :], keys[seen, :], values[seen, :], table)


def joint_specs():
    wide = 2 * HEAD_DIM
    return [
        spec((ROWS_DEV, wide), lambda h: (0, h)),
        spec((ROWS_DEV, wide), lambda h: (0, h + HEADS // 2)),
        spec((ROWS_DEV, wide), lambda h: (0, h + HEADS)),
        spec((1, 2 * TW - 1, CHUNK, wide), lambda h: (h, 0, 0, 0)),
    ]


def joint_attend():
    return Phase(
        joint_attend_kernel,
        grid=(HEADS // 2,),
        in_specs=joint_specs(),
        out_specs=[spec((ROWS_DEV, 2 * HEAD_DIM), lambda h: (0, h))],
        out_shape=[shape((ROWS_DEV, D), LOW)],
        name="joint_attend",
        ticks=3,
    )


def joint_attend_back_kernel(
    tick, queries, keys, values, bias, grad, grads, grad_bias, sum_k, sum_v
):
    grad_bias[...] = jnp.zeros_like(grad_bias)
    for i in range(ROWS_DEV // CHUNK):
        if i % 3 == 0:
            tick(i // 3)
        at = slice(i * CHUNK, (i + 1) * CHUNK)
        seen = slice(0, CLIP_ROWS) if i < TW else at
        table = clip_table(bias, i) if i < TW else bias[0, TW - 1]
        to_q, to_k, to_v, to_bias = attend_back(
            queries[at, :], keys[seen, :], values[seen, :], table, grad[at, :]
        )
        grads[0, at, :] = to_q.astype(LOW)
        if i >= TW:
            grad_bias[0, TW - 1] += to_bias
            grads[1, at, :] = to_k.astype(LOW)
            grads[2, at, :] = to_v.astype(LOW)
            continue
        for t in range(TW):
            grad_bias[0, i - t + TW - 1] += to_bias[t * CHUNK : (t + 1) * CHUNK]
        if i == 0:
            sum_k[...] = to_k
            sum_v[...] = to_v
        elif i < TW - 1:
            sum_k[...] += to_k
            sum_v[...] += to_v
        else:
            grads[1, seen, :] = (sum_k[...] + to_k).astype(LOW)
            grads[2, seen, :] = (sum_v[...] + to_v).astype(LOW)


def joint_attend_back():
    wide = 2 * HEAD_DIM
    head = spec((ROWS_DEV, wide), lambda h: (0, h))
    return Phase(
        joint_attend_back_kernel,
        grid=(HEADS // 2,),
        in_specs=joint_specs() + [head],
        out_specs=[spec((3, ROWS_DEV, wide), lambda h: (0, 0, h)), joint_specs()[3]],
        out_shape=[
            shape((3, ROWS_DEV, D), LOW),
            shape((HEADS // 2, 2 * TW - 1, CHUNK, wide), FULL),
        ],
        scratch_shapes=[pltpu.VMEM((CLIP_ROWS, wide), FULL)] * 2,
        name="joint_attend_back",
        ticks=3,
    )


def mlp_kernel(last_block, tick, live, rows, attended, mods, output, expand, shrink, *refs):
    branch, middle, normed, active, slope, reduced, result, total = refs
    step = pl.program_id(0)

    @pl.when(step == 0)
    def _():
        def chunk(at, seq):
            grown = nn(attended[at, :], output[...])
            branch[at, :] = grown.astype(LOW)
            mixed = rows[at, :].astype(FULL) + mods[seq, part(2)] * grown
            middle[at, :] = mixed
            unit, _ = normalise(mixed)
            normed[at, :] = (unit * (1.0 + mods[seq, part(4)]) + mods[seq, part(3)]).astype(LOW)

        each_chunk(chunk)
        total[...] = jnp.zeros_like(total)

    tick(0)
    before = nn(normed[...], expand[...])
    inner = 0.5 * (1.0 + lax.erf(before * 0.5**0.5))
    low_active = (before * inner).astype(LOW)
    tick(1)
    active[...] = low_active
    slope[...] = (inner + before * jnp.exp(-0.5 * before * before) * (2.0 * math.pi) ** -0.5).astype(LOW)
    total[...] += nn(low_active, shrink[...])

    @pl.when(step == pl.num_programs(0) - 1)
    def _():
        def chunk(at, seq):
            reduced[at, :] = total[at, :].astype(LOW)
            value = middle[at, :] + mods[seq, part(5)] * total[at, :]
            if last_block:
                value = value * jnp.where(seq.start > 0, live[0], 1.0)
            result[at, :] = value.astype(result.dtype)

        each_chunk(chunk)


def mlp(last_block):
    tile = 512
    square = whole((ROWS_DEV, D))
    strip = spec((ROWS_DEV, tile), lambda f: (0, f))
    return Phase(
        functools.partial(mlp_kernel, last_block),
        grid=(FF // tile,),
        in_specs=[
            SCALARS,
            square,
            square,
            whole((2, 6 * D)),
            whole((D, D)),
            spec((D, tile), lambda f: (0, f)),
            spec((tile, D), lambda f: (f, 0)),
        ],
        out_specs=[square, square, square, strip, strip, square, square],
        out_shape=[
            shape((ROWS_DEV, D), LOW),
            shape((ROWS_DEV, D), FULL),
            shape((ROWS_DEV, D), LOW),
            shape((ROWS_DEV, FF), LOW),
            shape((ROWS_DEV, FF), LOW),
            shape((ROWS_DEV, D), LOW),
            shape((ROWS_DEV, D), LOW if last_block else FULL),
        ],
        scratch_shapes=[pltpu.VMEM((ROWS_DEV, D), FULL)],
        name="mlp",
        ticks=2,
    )


def mlp_back_kernel(first_block, tick, live, *refs):
    (grad_result, attended, mods, branch, middle, normed, reduced, output, active, slope) = refs[:10]
    expand, shrink = refs[10:12]
    grad_shrink, grad_expand, grad_output, grad_middle, grad_attended, grad_mods = refs[12:18]
    grad_reduced, normed_t, total = refs[18:]
    grad_branch = grad_reduced
    step = pl.program_id(0)

    def incoming(at, seq):
        value = grad_result[at, :].astype(FULL)
        if first_block:
            value = value * jnp.where(seq.start > 0, live[0], 1.0)
        return value

    @pl.when(step == 0)
    def _():
        grad_mods[...] = jnp.zeros_like(grad_mods)

        def chunk(at, seq):
            value = incoming(at, seq)
            grad_reduced[at, :] = (mods[seq, part(5)] * value).astype(LOW)
            grad_mods[seq, part(5)] += jnp.sum(
                reduced[at, :].astype(FULL) * value, axis=0, keepdims=True
            )

        each_chunk(chunk)
        total[...] = jnp.zeros_like(total)
        normed_t[...] = normed[...].T

    tick(0)
    grad_active = nt(grad_reduced[...], shrink[...])
    grad_before = (grad_active * slope[...].astype(FULL)).astype(LOW)
    tick(1)
    grad_shrink[...] = tn(active[...], grad_reduced[...]).astype(LOW)
    tick(2)
    grad_expand[...] = nn(normed_t[...], grad_before).astype(LOW)
    tick(3)
    total[...] += nt(grad_before, expand[...])

    @pl.when(step == pl.num_programs(0) - 1)
    def _():
        def chunk(at, seq):
            grad = total[at, :]
            unit, scale = normalise(middle[at, :])
            grad_mods[seq, part(3)] += jnp.sum(grad, axis=0, keepdims=True)
            grad_mods[seq, part(4)] += jnp.sum(unit * grad, axis=0, keepdims=True)
            value = incoming(at, seq) + norm_back(unit, scale, (1.0 + mods[seq, part(4)]) * grad)
            grad_middle[at, :] = value
            grad_mods[seq, part(2)] += jnp.sum(
                branch[at, :].astype(FULL) * value, axis=0, keepdims=True
            )
            grad_branch[at, :] = (mods[seq, part(2)] * value).astype(LOW)

        each_chunk(chunk)
        grad_attended[...] = nt(grad_branch[...], output[...]).astype(LOW)
        grad_output[...] = tn(attended[...], grad_branch[...]).astype(LOW)


def mlp_back(first_block):
    tile = 512
    square = whole((ROWS_DEV, D))
    strip = spec((ROWS_DEV, tile), lambda f: (0, f))
    across = spec((D, tile), lambda f: (0, f))
    down = spec((tile, D), lambda f: (f, 0))
    return Phase(
        functools.partial(mlp_back_kernel, first_block),
        grid=(FF // tile,),
        in_specs=[
            SCALARS,
            square,
            square,
            whole((2, 6 * D)),
            square,
            square,
            square,
            square,
            whole((D, D)),
            strip,
            strip,
            across,
            down,
        ],
        out_specs=[down, across, whole((D, D)), square, square, whole((2, 6 * D))],
        out_shape=[
            shape((FF, D), LOW),
            shape((D, FF), LOW),
            shape((D, D), LOW),
            shape((ROWS_DEV, D), FULL),
            shape((ROWS_DEV, D), LOW),
            shape((2, 6 * D), FULL),
        ],
        scratch_shapes=[
            pltpu.VMEM((ROWS_DEV, D), LOW),
            pltpu.VMEM((D, ROWS_DEV), LOW),
            pltpu.VMEM((ROWS_DEV, D), FULL),
        ],
        name="mlp_back",
        ticks=4,
    )


def finish_rows(rows, grad_normed, grad_middle, mods, grad_rows, grad_mods):
    grad_mods[...] = jnp.zeros_like(grad_mods)

    def chunk(at, seq):
        grad = grad_normed[at, :].astype(FULL)
        unit, scale = normalise(rows[at, :].astype(FULL))
        grad_mods[seq, part(0)] += jnp.sum(grad, axis=0, keepdims=True)
        grad_mods[seq, part(1)] += jnp.sum(unit * grad, axis=0, keepdims=True)
        grad_rows[at, :] = grad_middle[at, :] + norm_back(
            unit, scale, (1.0 + mods[seq, part(1)]) * grad
        )

    each_chunk(chunk)


def joint_project_back_kernel(
    tick, rows, mods, normed, grad_middle, weight, grad, grad_weight, grad_rows, grad_mods, total, normed_t
):
    step = pl.program_id(0)

    @pl.when(step == 0)
    def _():
        total[...] = jnp.zeros_like(total)
        normed_t[...] = normed[...].T

    tick(0)
    grad_weight[...] = nn(normed_t[...], grad[0]).astype(LOW)
    tick(1)
    total[...] += nt(grad[0], weight[...])

    @pl.when(step == pl.num_programs(0) - 1)
    def _():
        finish_rows(rows, total, grad_middle, mods, grad_rows, grad_mods)


def joint_project_back():
    tile = 512
    square = whole((ROWS_DEV, D))
    across = spec((D, tile), lambda t: (0, t))
    return Phase(
        joint_project_back_kernel,
        grid=(3 * D // tile,),
        in_specs=[square, whole((2, 6 * D)), square, square, across, spec((1, ROWS_DEV, tile), lambda t: (t // 2, 0, t % 2))],
        out_specs=[across, square, whole((2, 2 * D))],
        out_shape=[shape((D, 3 * D), LOW), shape((ROWS_DEV, D), FULL), shape((2, 2 * D), FULL)],
        scratch_shapes=[pltpu.VMEM((ROWS_DEV, D), FULL), pltpu.VMEM((D, ROWS_DEV), LOW)],
        name="joint_project_back",
        ticks=2,
    )


def space_project_back_kernel(tick, normed, weight, grad_q, grad_pairs, grad_weight, grad_normed, total):
    step = pl.program_id(0)
    own = span(lax.axis_index("narrow"), ROWS_DEV)

    @pl.when(step == 0)
    def _():
        total[...] = jnp.zeros_like(total)

    tick(0)

    @pl.when(step < 2)
    def _():
        grad_weight[...] = tn(normed[own, :], grad_q[...]).astype(LOW)
        total[own, :] += nt(grad_q[...], weight[...])

    @pl.when(step >= 2)
    def _():
        flat = grad_pairs[0].reshape(4 * ROWS_DEV, grad_pairs.shape[-1])
        grad_weight[...] = tn(normed[...], flat).astype(LOW)

    for q in range(4):
        tick(q + 1)

        @pl.when(step >= 2)
        def _():
            at = slice(q * ROWS_DEV, (q + 1) * ROWS_DEV)
            total[at, :] += nt(grad_pairs[0, q], weight[...])

    @pl.when(step == pl.num_programs(0) - 1)
    def _():
        grad_normed[...] = total[...].astype(LOW)


def space_project_back():
    tile = 512
    across = spec((D, tile), lambda t: (0, t))

    def pair(t):
        late = jnp.maximum(t - 2, 0)
        return (late // 2, 0, 0, late % 2)

    return Phase(
        space_project_back_kernel,
        grid=(3 * D // tile,),
        in_specs=[
            whole((4 * ROWS_DEV, D)),
            across,
            spec((ROWS_DEV, tile), lambda t: (0, jnp.minimum(t, 1))),
            spec((1, 4, ROWS_DEV, tile), pair),
        ],
        out_specs=[across, whole((4 * ROWS_DEV, D))],
        out_shape=[shape((D, 3 * D), LOW), shape((4 * ROWS_DEV, D), LOW)],
        scratch_shapes=[pltpu.VMEM((4 * ROWS_DEV, D), FULL)],
        name="space_project_back",
        ticks=5,
    )


def finish_kernel(tick, rows, mods, grad_normed, grad_middle, grad_rows, grad_mods):
    tick(0)
    finish_rows(rows, grad_normed, grad_middle, mods, grad_rows, grad_mods)


def finish():
    square = whole((ROWS_DEV, D))
    return Phase(
        finish_kernel,
        grid=(1,),
        in_specs=[square, whole((2, 6 * D)), square, square],
        out_specs=[square, whole((2, 2 * D))],
        out_shape=[shape((ROWS_DEV, D), FULL), shape((2, 2 * D), FULL)],
        name="finish",
    )


class Place:
    def __init__(self):
        self.w = lax.axis_index("wide")
        self.n = lax.axis_index("narrow")
        self.c = lax.bitwise_xor(self.w, 1)
        self.x = lax.bitwise_xor(self.w, 2)
        self.y = lax.bitwise_xor(self.w, 4)
        self.d = lax.bitwise_xor(self.w, 6)
        self.up = jnp.minimum(self.n + 1, 3)
        self.down = jnp.maximum(self.n - 1, 0)
        self.order = (
            self.n,
            lax.bitwise_xor(self.n, 1),
            jnp.where(self.n < 2, 2, 1),
            jnp.where(self.n < 2, 3, 0),
        )

    def enter(self):
        barrier = pltpu.get_barrier_semaphore()
        for peer in (self.x, self.y, self.c):
            pl.semaphore_signal(barrier, inc=1, device_id=(peer, self.n), device_id_type=MESH)

        @pl.when(self.n > 0)
        def _():
            pl.semaphore_signal(barrier, inc=1, device_id=(self.w, self.n - 1), device_id_type=MESH)

        @pl.when(self.n < 3)
        def _():
            pl.semaphore_signal(barrier, inc=1, device_id=(self.w, self.n + 1), device_id_type=MESH)

        ends = jnp.where(self.n > 0, 1, 0) + jnp.where(self.n < 3, 1, 0)
        pl.semaphore_wait(barrier, 3 + ends)

    def enter_all(self):
        barrier = pltpu.get_barrier_semaphore()
        for step in range(1, 8):
            peer = (lax.bitwise_xor(self.w, step), self.n)
            pl.semaphore_signal(barrier, inc=1, device_id=peer, device_id_type=MESH)
        for step in range(1, 4):
            peer = (self.w, lax.bitwise_xor(self.n, step))
            pl.semaphore_signal(barrier, inc=1, device_id=peer, device_id_type=MESH)
        pl.semaphore_wait(barrier, 10)

    def passes_on(self, col):
        return jnp.logical_or(
            jnp.logical_and(col < self.n, self.n < 3), jnp.logical_and(col > self.n, self.n > 0)
        )

    def carried(self, col):
        return jnp.logical_or(
            jnp.logical_and(col > self.n, self.n > 0), jnp.logical_and(col < self.n, self.n < 3)
        )


def remote(src, dst, send, recv, to):
    return pltpu.make_async_remote_copy(
        src_ref=src, dst_ref=dst, send_sem=send, recv_sem=recv, device_id=to, device_id_type=MESH
    )


def span(index, size):
    return pl.ds(pl.multiple_of(index * size, size), size)


DMA = pltpu.SemaphoreType.DMA
FOLDS = [(3, 1), (3, 3), (3, 0), (3, 2)]
FOLDS += [(2, 3), (1, 3), (2, 2), (1, 2), (1, 1), (2, 1), (1, 0), (2, 0)]
FOLDS += [(0, 3), (0, 2), (0, 1), (0, 0)]
LOADS = 2
PIECES = 4
PIECE = ROWS_DEV // PIECES


class Names:
    def __init__(self, owner):
        self.owner = owner

    def __getattr__(self, name):
        return self.owner, name


A, S, J = Names(0), Names(1), Names(2)


class Feed:
    def __init__(self, enter):
        self.enter, self.steps, self.drains = enter, [], []
        self.late_enter = lambda: None

    def add(self, function, *args):
        self.steps.append(functools.partial(function, *args))

    def drain(self, function, *args):
        self.drains.append(functools.partial(function, *args))

    def follow(self, tables):
        self.lists = []
        for table in tables:
            parts = [[]]
            for number in table:
                if number < 0:
                    parts.append([])
                else:
                    parts[-1].append(self.steps[number])
            self.lists.append(parts)
        self.slot = 0
        self.at_end = jnp.logical_or(Place().n == 0, Place().n == 3)

    def do(self, slot):
        ends, middles = (parts[slot] for parts in self.lists)

        @pl.when(self.at_end)
        def _():
            for step in ends:
                step()

        @pl.when(jnp.logical_not(self.at_end))
        def _():
            for step in middles:
                step()

    def over(self, phase):
        first, total = self.slot, phase.grid[0]
        self.do(first)
        self.slot += total * phase.ticks

        def tick(t):
            for i in range(total):
                slot = first + i * phase.ticks + t
                if slot > first and any(parts[slot] for parts in self.lists):

                    @pl.when(pl.program_id(0) == i)
                    def _():
                        self.do(slot)

        return tick

    def rest(self):
        self.do(self.slot)
        for step in self.drains:
            step()


class Gather:
    def __init__(self, shapes, line, collective_id):
        self.shapes, self.line, self.collective_id = shapes, line, collective_id
        count, lines = len(shapes), 1 if line else 0
        self.in_specs = [pl.BlockSpec(memory_space=pl.ANY)] * (count + lines)
        self.out_specs = self.in_specs
        self.out_shape = [shape((8 * r, 4 * c), LOW) for r, c in shapes]
        self.out_shape += [shape((4 * ROWS_DEV, D), LOW)] * lines
        self.scratch = [
            DMA((count, 5)),
            DMA((count, 4)),
            DMA((count, 2, 4)),
            DMA((count, 2, 4)),
            DMA((count, 2, 4)),
            DMA((count, 2, 4)),
            DMA((count, 4, 4)),
            DMA((count, 4, 4)),
            DMA((count,)),
        ]
        self.scratch += [DMA((PIECES, 5)), DMA((PIECES, 4)), DMA((PIECES,))] * lines

    def steps(self, ins, outs, scratch):
        at = Place()
        shapes, count = self.shapes, len(self.shapes)
        w, n = at.w, at.n
        shards, fulls = ins[:count], outs[:count]
        z_send, z_recv, x_send, x_recv, y_send, y_recv, c_send, c_recv, own_sem = scratch[:9]

        def block(k, row, col):
            rows, cols = shapes[k]
            return fulls[k].at[span(row, rows), span(col, cols)]

        def z_copy(k, src, col, slot, to):
            return remote(src, block(k, w, col), z_send.at[k, slot], z_recv.at[k, col], (w, to))

        def x_copy(k, src, row, far, col):
            sems = x_send.at[k, far, col], x_recv.at[k, far, col]
            return remote(src, block(k, row, col), *sems, (at.x, n))

        def y_copy(k, src, row, far, col):
            sems = y_send.at[k, far, col], y_recv.at[k, far, col]
            return remote(src, block(k, row, col), *sems, (at.y, n))

        def c_copy(k, src, row, chip, col):
            sems = c_send.at[k, chip, col], c_recv.at[k, chip, col]
            return remote(src, block(k, row, col), *sems, (at.c, n))

        def own_copy(k):
            return pltpu.make_async_copy(shards[k], block(k, w, n), own_sem.at[k])

        def own(k):
            @pl.when(n < 3)
            def _():
                z_copy(k, shards[k], n, n, at.up).start()

            @pl.when(n > 0)
            def _():
                z_copy(k, shards[k], n, 4, at.down).start()

            x_copy(k, shards[k], w, 0, n).start()
            y_copy(k, shards[k], w, 0, n).start()
            c_copy(k, shards[k], w, 0, n).start()
            own_copy(k).start()

        def z_stage(k, j):
            col = at.order[j]
            here = block(k, w, col)
            z_copy(k, here, col, col, at.up).wait_recv()

            @pl.when(at.passes_on(col))
            def _():
                z_copy(k, here, col, col, jnp.where(col < n, at.up, at.down)).start()

            x_copy(k, here, w, 0, col).start()
            y_copy(k, here, w, 0, col).start()
            c_copy(k, here, w, 0, col).start()

        def near_stage(k, j):
            col = at.order[j]
            from_x = block(k, at.x, col)
            from_y = block(k, at.y, col)
            x_copy(k, from_x, at.x, 0, col).wait_recv()
            if j < 2:
                y_copy(k, from_x, at.x, 1, col).start()
            c_copy(k, from_x, at.x, 1, col).start()
            y_copy(k, from_y, at.y, 0, col).wait_recv()
            if j >= 2:
                x_copy(k, from_y, at.y, 1, col).start()
            c_copy(k, from_y, at.y, 2, col).start()

        def far_stage(k, j):
            col = at.order[j]
            far = block(k, at.d, col)
            (y_copy if j < 2 else x_copy)(k, far, at.d, 1, col).wait_recv()
            c_copy(k, far, at.d, 3, col).start()

        def ready(k):
            own_copy(k).wait()
            for col in range(4):
                for chip in range(4):
                    c_copy(k, block(k, w, col), w, chip, col).wait_recv()

        def drain(k):
            for j in range(4):
                col = at.order[j]
                here = block(k, w, col)

                @pl.when(at.passes_on(col) if j else n < 3)
                def _():
                    z_copy(k, here, col, col, at.up).wait_send()

                x_copy(k, here, w, 0, col).wait_send()
                y_copy(k, here, w, 0, col).wait_send()
                (y_copy if j < 2 else x_copy)(k, here, w, 1, col).wait_send()
                for chip in range(4):
                    c_copy(k, here, w, chip, col).wait_send()

            @pl.when(n > 0)
            def _():
                z_copy(k, shards[k], n, 4, at.down).wait_send()

        if self.line:
            rows, all_rows = ins[count], outs[count]
            t_send, t_recv, t_own = scratch[9:]

            def piece(p, col):
                return all_rows.at[pl.ds(pl.multiple_of(col * ROWS_DEV + p * PIECE, 16), PIECE)]

            def t_copy(p, src, col, slot, to):
                dst = piece(p, col)
                return remote(src, dst, t_send.at[p, slot], t_recv.at[p, col], (w, to))

            def t_own_copy(p):
                here = pl.ds(p * PIECE, PIECE)
                return pltpu.make_async_copy(rows.at[here], piece(p, n), t_own.at[p])

            def t_start(p, late):
                src = rows.at[pl.ds(p * PIECE, PIECE)]
                if not late:
                    t_own_copy(p).start()

                @pl.when(n == 2 if late else n < 2)
                def _():
                    t_copy(p, src, n, n, at.up).start()

                @pl.when(n == 1 if late else n >= 2)
                def _():
                    t_copy(p, src, n, 4, at.down).start()

            def t_stage(p, j):
                col = at.order[j]
                here = piece(p, col)
                t_copy(p, here, col, col, at.up).wait_recv()

                @pl.when(at.passes_on(col))
                def _():
                    t_copy(p, here, col, col, jnp.where(col < n, at.up, at.down)).start()

            def t_drain(p):
                for j in range(4):
                    col = at.order[j]
                    here = piece(p, col)

                    @pl.when(at.passes_on(col) if j else n < 3)
                    def _():
                        t_copy(p, here, col, col, at.up).wait_send()

                @pl.when(n > 0)
                def _():
                    t_copy(p, piece(p, n), n, 4, at.down).wait_send()

            def t_ready():
                for p in range(PIECES):
                    t_own_copy(p).wait()

        items = Feed(at.enter)
        for k in range(count):
            items.add(own, k)
            for j in range(1, 4):
                items.add(z_stage, k, j)
            for j in range(4):
                items.add(near_stage, k, j)
            for j in range(4):
                items.add(far_stage, k, j)
            items.add(ready, k)
            items.drain(drain, k)
        if self.line:
            for p in range(PIECES):
                items.add(t_start, p, False)
                items.add(t_start, p, True)
                for j in range(1, 4):
                    items.add(t_stage, p, j)
                items.drain(t_drain, p)
            items.add(t_ready)
        return items


class Scatter:
    def __init__(self, shapes, line, collective_id):
        self.shapes, self.line, self.collective_id = shapes, line, collective_id
        count, lines = len(shapes), 1 if line else 0
        self.in_specs = [pl.BlockSpec(memory_space=pl.ANY)] * (count + lines)
        self.out_shape = [shape(s, FULL) for s in shapes] + [shape((ROWS_DEV, D), FULL)] * lines
        self.out_specs = [pl.BlockSpec(memory_space=pltpu.VMEM)] * len(self.out_shape)
        self.scratch = []
        for s in shapes:
            self.scratch += [
                pltpu.VMEM((4, 4) + s, LOW),
                pltpu.VMEM((4,) + s, LOW),
                pltpu.VMEM((2, 4) + s, LOW),
                pltpu.VMEM((5,) + s, LOW),
                pltpu.VMEM((LOADS,) + s, LOW),
            ]
        self.scratch += [
            DMA((count, 4, 4)),
            DMA((count, 4, 4)),
            DMA((count, 4, 4)),
            DMA((count, 4)),
            DMA((count, 4)),
            DMA((count, 2, 4)),
            DMA((count, 2, 4)),
            DMA((count, 4)),
            DMA((count, 5)),
        ]
        self.scratch += [
            pltpu.VMEM((PIECES, 4, PIECE, D), LOW),
            pltpu.VMEM((PIECES, 5, PIECE, D), LOW),
            DMA((PIECES, 4)),
            DMA((PIECES, 4)),
            DMA((PIECES, 5)),
        ] * lines

    def steps(self, ins, outs, scratch):
        at = Place()
        shapes, count = self.shapes, len(self.shapes)
        w, n, order = at.w, at.n, at.order
        chips = (w, at.x, at.y, at.d)
        held, far_in, near_in, z_in, staged = (scratch[i : 5 * count : 5] for i in range(5))
        load, c_send, c_recv, d_send, d_recv, n_send, n_recv, z_send, z_recv = scratch[
            5 * count : 5 * count + 9
        ]

        def source(k, row, col):
            rows, cols = shapes[k]
            return ins[k].at[span(row, rows), span(col, cols)]

        def load_copy(k, chip, j):
            slot = FOLDS.index((chip, j)) % LOADS
            return pltpu.make_async_copy(
                source(k, chips[chip], order[j]), staged[k].at[slot], load.at[k, chip, j]
            )

        def c_copy(k, chip, col):
            src = source(k, lax.bitwise_xor(chips[chip], 1), col)
            sems = c_send.at[k, chip, col], c_recv.at[k, chip, col]
            return remote(src, held[k].at[chip, col], *sems, (at.c, n))

        def d_copy(k, j):
            sems = d_send.at[k, j], d_recv.at[k, j]
            to = (at.x if j < 2 else at.y, n)
            return remote(held[k].at[3, order[j]], far_in[k].at[j], *sems, to)

        def n_copy(k, chip, col):
            sems = n_send.at[k, chip - 1, col], n_recv.at[k, chip - 1, col]
            dst = near_in[k].at[chip - 1, col]
            return remote(held[k].at[chip, col], dst, *sems, (chips[chip], n))

        def z_copy(k, col, slot, to):
            sems = z_send.at[k, col], z_recv.at[k, slot]
            return remote(held[k].at[0, col], z_in[k].at[slot], *sems, (w, to))

        def add(target, rows, *others):
            step = 64 if rows % 64 == 0 else 48

            @pl.loop(0, rows // step)
            def _(i):
                here = span(i, step)
                total = target[here, :]
                for other in others:
                    total = total + other[here, :]
                target[here, :] = total

        def fold(k, chip, j, *others):
            number = FOLDS.index((chip, j))
            load_copy(k, chip, j).wait()
            c_copy(k, chip, order[j]).wait_recv()
            add(held[k].at[chip, order[j]], shapes[k][0], staged[k].at[number % LOADS], *others)
            if number + LOADS < len(FOLDS):
                load_copy(k, *FOLDS[number + LOADS]).start()

        def begin(k):
            for chip, j in FOLDS:
                c_copy(k, chip, order[j]).start()
            for chip, j in FOLDS[:LOADS]:
                load_copy(k, chip, j).start()

        def far(k, j):
            fold(k, 3, j)
            d_copy(k, j).start()

        def near(k, j):
            chip = 2 if j >= 2 else 1
            fold(k, chip, j)
            n_copy(k, chip, order[j]).start()

        def near_far(k, j):
            chip = 1 if j >= 2 else 2
            d_copy(k, j).wait_recv()
            fold(k, chip, j, far_in[k].at[j])
            n_copy(k, chip, order[j]).start()

        def line_slot(col):
            to = jnp.where(col > n, at.up, at.down)
            return jnp.where(jnp.logical_and(col < n, to == col), 4, col), to

        def fold_near(k, j):
            col = order[j]
            n_copy(k, 1, col).wait_recv()
            n_copy(k, 2, col).wait_recv()
            fold(k, 0, j, near_in[k].at[0, col], near_in[k].at[1, col])

        def along(k, j):
            col = order[j]
            fold_near(k, j)

            @pl.when(at.carried(col))
            def _():
                z_copy(k, col, col, at.up).wait_recv()
                add(held[k].at[0, col], shapes[k][0], z_in[k].at[col])

            slot, to = line_slot(col)
            z_copy(k, col, slot, to).start()

        def last(k):
            fold_near(k, 0)
            outs[k][...] = held[k][0, n].astype(FULL)

            @pl.when(n > 0)
            def _():
                z_copy(k, n, n, at.up).wait_recv()
                outs[k][...] += z_in[k][n].astype(FULL)

            @pl.when(n < 3)
            def _():
                z_copy(k, n, 4, at.up).wait_recv()
                outs[k][...] += z_in[k][4].astype(FULL)

        def drain(k):
            for chip in range(4):
                for col in range(4):
                    c_copy(k, chip, col).wait_send()
            for j in range(4):
                d_copy(k, j).wait_send()
                n_copy(k, 1, j).wait_send()
                n_copy(k, 2, j).wait_send()
            for j in range(1, 4):
                z_copy(k, order[j], order[j], at.up).wait_send()

        if self.line:
            line_held, line_in, line_load, line_send, line_recv = scratch[5 * count + 9 :]

            def line_loads(p, col):
                here = pl.ds(pl.multiple_of(col * ROWS_DEV + p * PIECE, 16), PIECE)
                return pltpu.make_async_copy(
                    ins[count].at[here], line_held.at[p, col], line_load.at[p, col]
                )

            def line_copy(p, col, slot, to):
                sems = line_send.at[p, col], line_recv.at[p, slot]
                return remote(line_held.at[p, col], line_in.at[p, slot], *sems, (w, to))

            def line_begin():
                for j in (3, 2, 1, 0):
                    for p in range(PIECES):
                        line_loads(p, order[j]).start()

            def line_stage(j, p):
                col = order[j]
                line_loads(p, col).wait()

                @pl.when(at.carried(col))
                def _():
                    line_copy(p, col, col, at.up).wait_recv()
                    add(line_held.at[p, col], PIECE, line_in.at[p, col])

                slot, to = line_slot(col)
                line_copy(p, col, slot, to).start()

            def line_last(p):
                here = pl.ds(p * PIECE, PIECE)
                line_loads(p, n).wait()
                outs[count][here, :] = line_held[p, n].astype(FULL)

                @pl.when(n > 0)
                def _():
                    line_copy(p, n, n, at.up).wait_recv()
                    outs[count][here, :] += line_in[p, n].astype(FULL)

                @pl.when(n < 3)
                def _():
                    line_copy(p, n, 4, at.up).wait_recv()
                    outs[count][here, :] += line_in[p, 4].astype(FULL)

            def line_drain():
                for p in range(PIECES):
                    for j in range(1, 4):
                        line_copy(p, order[j], order[j], at.up).wait_send()

        items = Feed(at.enter)
        for k in range(count):
            items.add(begin, k)
            for j in (1, 3, 0, 2):
                items.add(far, k, j)
            for j in (3, 2, 1, 0):
                items.add(near, k, j)
                items.add(near_far, k, j)
            for j in (3, 2, 1):
                items.add(along, k, j)
            items.add(last, k)
            items.drain(drain, k)
        if self.line:
            for j in (3, 2, 1):
                for p in range(PIECES):
                    items.add(line_stage, j, p)
            for p in range(PIECES):
                items.add(line_last, p)
            items.add(lambda: None)
            items.drain(line_drain)
            items.enter = lambda: (at.enter(), line_begin())
            items.late_enter = line_begin
        return items


def fused(script, args, outs, engine, moved, name):
    in_specs = [SCALARS.spec() if k == A.live else pl.BlockSpec(memory_space=pl.ANY) for k in args]
    counts = [len(args), len(outs), len(engine.out_specs)]

    def kernel(*refs):
        groups = []
        for count in counts:
            groups.append(refs[:count])
            refs = refs[count:]
        named = dict(zip(list(args) + list(outs), groups[0] + groups[1]))
        feed = engine.steps([named[k] for k in moved], groups[2], refs)
        script(named, groups[2], feed)

    results = pl.pallas_call(
        kernel,
        in_specs=in_specs,
        out_specs=[pl.BlockSpec(memory_space=pl.ANY)] * len(outs) + engine.out_specs,
        out_shape=list(outs.values()) + engine.out_shape,
        scratch_shapes=engine.scratch,
        compiler_params=pltpu.CompilerParams(
            collective_id=engine.collective_id, has_side_effects=True, vmem_limit_bytes=62 * 2**20
        ),
        cost_estimate=pl.CostEstimate(flops=100_000_000_000, bytes_accessed=0, transcendentals=0),
        name=name,
    )(*args.values())
    return dict(zip(outs, results)), list(results[len(outs) :])


class Joined:
    def __init__(self, engine, other):
        self.engine, self.other = engine, other
        self.collective_id = engine.collective_id
        self.out_specs = engine.out_specs + other.out_specs
        self.out_shape = engine.out_shape + other.out_shape
        self.scratch = engine.scratch + other.scratch

    def steps(self, ins, outs, scratch):
        cuts = len(ins) - self.other.takes, len(self.engine.out_specs), len(self.engine.scratch)
        feed = self.engine.steps(ins[: cuts[0]], outs[: cuts[1]], scratch[: cuts[2]])
        for step in self.other.steps(ins[cuts[0] :], outs[cuts[1] :], scratch[cuts[2] :]):
            feed.add(step)
        begin = feed.late_enter

        def enter():
            Place().enter_all()
            begin()

        feed.enter = enter
        return feed


STRIP = 768


def strips(b, q):
    return b * 2 + q


class Modulation:
    takes = 4

    def __init__(self):
        self.out_shape = [shape((2, 6 * D), FULL)] * 2 + [shape((16, 128), FULL)]
        self.out_specs = [pl.BlockSpec(memory_space=pl.ANY)] * 2
        self.out_specs += [pl.BlockSpec(memory_space=pltpu.VMEM)]
        self.scratch = [
            pltpu.VMEM((8, 8, 128), FULL),
            pltpu.VMEM((8, 128), FULL),
            pltpu.VMEM((2, 128, 2 * STRIP), LOW),
            pltpu.VMEM((8, 8, STRIP), FULL),
            pltpu.VMEM((8, 8, STRIP), FULL),
            pltpu.VMEM((4, 8, STRIP), FULL),
            pltpu.VMEM((2, 2, 6 * D), FULL),
            DMA((3, 8)),
            DMA((3, 8)),
            DMA((6,)),
        ]

    def steps(self, ins, outs, scratch):
        at = Place()
        w, n = at.w, at.n
        images, clips, *shards = ins
        cond, clip, held, terms, arrived, got, made, send, recv, local = scratch

        def across(stage, step, src, dst):
            to = (lax.bitwise_xor(w, step), n)
            return remote(src, dst, send.at[stage, step], recv.at[stage, step], to)

        def first(step):
            return across(0, step, images.at[lax.bitwise_xor(w, step)], cond.at[w])

        def second(step):
            return across(1, step, terms.at[lax.bitwise_xor(w, step)], arrived.at[w])

        def third(step):
            to = (w, lax.bitwise_xor(n, step))
            return remote(got.at[n], got.at[n], send.at[2, step], recv.at[2, step], to)

        def loads():
            return [
                pltpu.make_async_copy(images.at[w], cond.at[w], local.at[0]),
                pltpu.make_async_copy(clips, clip, local.at[1]),
                pltpu.make_async_copy(shards[0], held.at[0], local.at[2]),
                pltpu.make_async_copy(shards[1], held.at[1], local.at[3]),
            ]

        def stores():
            return [
                pltpu.make_async_copy(made.at[b], outs[b], local.at[4 + b]) for b in range(2)
            ]

        def start():
            for copy in loads():
                copy.start()
            for step in range(1, 8):
                first(step).start()

        def project():
            for copy in loads():
                copy.wait()
            for step in range(1, 8):
                first(step).wait_recv()
            flat = jnp.concatenate([cond[:, 0, :], clip[...]], axis=0).astype(LOW)
            outs[2][8:16, :] = cond[:, 0, :]
            for g in range(8):
                outs[2][g : g + 1, :] = clip[g // 4 : g // 4 + 1, :]
            for b in range(2):
                product = nn(flat, held[b])
                for g in range(8):
                    for r, row in enumerate((8 + g // 4, g)):
                        for q in range(2):
                            to = r * 4 + strips(b, q)
                            terms[g, to : to + 1, :] = product[row : row + 1, q * STRIP : (q + 1) * STRIP]
            for step in range(1, 8):
                second(step).start()

        def total():
            value = terms[w]
            for step in range(1, 8):
                second(step).wait_recv()
                value = value + arrived[lax.bitwise_xor(w, step)]
            got[n] = value
            for step in range(1, 4):
                third(step).start()

        def spread():
            for step in range(1, 4):
                third(step).wait_recv()
            for col in range(4):
                for b in range(2):
                    for r in range(2):
                        for q in range(2):
                            here = r * 4 + strips(b, q)
                            to = col * 2 * STRIP + q * STRIP
                            made[b, r : r + 1, to : to + STRIP] = got[col, here : here + 1, :]
            for copy in stores():
                copy.start()

        def settle():
            for copy in stores():
                copy.wait()
            for step in range(1, 8):
                first(step).wait_send()
                second(step).wait_send()
            for step in range(1, 4):
                third(step).wait_send()

        return start, project, total, spread, settle


class ModulationBack:
    takes = 0

    def __init__(self):
        self.out_shape = [shape((128, 2 * STRIP), FULL)] * 2
        self.out_specs = [pl.BlockSpec(memory_space=pltpu.VMEM)] * 2
        self.scratch = [
            pltpu.VMEM((4, 8, STRIP), FULL),
            pltpu.VMEM((4, 8, STRIP), FULL),
            pltpu.VMEM((8, 8, STRIP), FULL),
            pltpu.VMEM((2, 2, 6 * D), FULL),
            pltpu.VMEM((16, 128), FULL),
            DMA((2, 8)),
            DMA((2, 8)),
            DMA((5,)),
        ]

    def steps(self, ins, outs, scratch):
        at = Place()
        w, n = at.w, at.n
        pieces, arrived, every, grads, cond, send, recv, local = scratch

        def along(step):
            to = (w, lax.bitwise_xor(n, step))
            src = pieces.at[lax.bitwise_xor(n, step)]
            return remote(src, arrived.at[n], send.at[0, step], recv.at[0, step], to)

        def across(step):
            to = (lax.bitwise_xor(w, step), n)
            return remote(every.at[w], every.at[w], send.at[1, step], recv.at[1, step], to)

        def finish(cond_ref, early, late):
            copies = [pltpu.make_async_copy(cond_ref, cond, local.at[4])]
            for b in range(2):
                cut = pl.ds(2 * D, 4 * D)
                here = grads.at[b, :, pl.ds(0, 2 * D)]
                copies.append(pltpu.make_async_copy(early[b], here, local.at[2 * b]))
                here = grads.at[b, :, cut]
                copies.append(pltpu.make_async_copy(late[b].at[:, cut], here, local.at[2 * b + 1]))
            for copy in copies:
                copy.start()
            for copy in copies:
                copy.wait()
            for col in range(4):
                for b in range(2):
                    for r in range(2):
                        for q in range(2):
                            to = r * 4 + strips(b, q)
                            here = col * 2 * STRIP + q * STRIP
                            pieces[col, to : to + 1, :] = grads[b, r : r + 1, here : here + STRIP]
            for step in range(1, 4):
                along(step).start()
            value = pieces[n]
            for step in range(1, 4):
                along(step).wait_recv()
                value = value + arrived[lax.bitwise_xor(n, step)]
            every[w] = value
            for step in range(1, 8):
                across(step).start()
            for step in range(1, 8):
                across(step).wait_recv()
            for b in range(2):
                for q in range(2):
                    rows = [every[:, r * 4 + strips(b, q), :] for r in range(2)]
                    outs[b][:, q * STRIP : (q + 1) * STRIP] = lax.dot_general(
                        cond[...],
                        jnp.concatenate(rows, axis=0),
                        (((0,), (0,)), ((), ())),
                        precision=lax.Precision.HIGHEST,
                        preferred_element_type=FULL,
                    )
            for step in range(1, 4):
                along(step).wait_send()
            for step in range(1, 8):
                across(step).wait_send()

        self.finish = finish
        return ()


FORWARD_ENDS = (
    0, 13, 125, 1, 4, 104, 109, 114, 119, 14, 17, 5, 2, 26, 126, 8, 18, 27, 21, 15, 39, 127, 9, 3,
    6, 40, 30, 22, 107, 31, 28, 19, 16, 128, 10, 43, 112, 7, 108, 44, 23, 41, 65, 66, 34, 11, 12,
    35, 117, 32, 122, 52, 20, 53, 36, 47, 113, 24, 48, 25, 118, 45, 69, 70, 123, 49, 56, 57, 29,
    105, 110, 115, 120, 129, 73, 74, 106, 60, 61, 111, 33, 116, 37, 121, 124, -1, 38, 67, 91, -1,
    -1, 71, 92, -1, -1, -1, -1, -1, 95, 42, 75, -1, -1, -1, 54, 78, -1, 96, -1, -1, -1, 79, -1, 99,
    68, -1, -1, -1, 55, -1, 46, -1, -1, -1, 58, 93, -1, -1, -1, -1, -1, -1, -1, -1, 82, 80, -1, -1,
    -1, -1, -1, -1, -1, -1, -1, -1, 100, 94, -1, -1, -1, -1, -1, -1, -1, 83, 81, 50, 72, 51, -1,
    62, 59, -1, -1, 97, -1, -1, -1, 86, -1, -1, -1, 84, -1, -1, -1, 98, -1, 76, -1, 77, -1, 63, 87,
    -1, 64, -1, 101, 85, -1, -1, 88, -1, -1, -1, 102, -1, -1, 103, -1, -1, -1, -1, 89, -1, -1, -1,
    90, -1, -1, -1, -1, -1, -1, -1, -1, -1, -1, -1, -1, -1, -1, -1, -1, -1, -1, -1, -1, -1, -1, -1,
    -1, -1, -1, -1, -1, -1, -1, -1,
)
FORWARD_MIDDLES = (
    0, 13, 125, 1, 2, 4, 104, 26, 126, 14, 15, 109, 17, 3, 5, 106, 39, 127, 6, 114, 107, 119, 8,
    111, 28, 16, 128, 30, 116, 18, 19, 21, 112, 121, 7, 108, 10, 9, 27, 41, 65, 43, 40, 23, 117,
    32, 11, 20, 12, 122, 52, 34, 22, 113, 66, 31, 118, 45, 69, 123, 36, 124, 24, 47, 25, 53, 29,
    105, 129, 110, 115, 120, 67, 44, 91, -1, 56, -1, 42, 49, 70, -1, -1, -1, 54, 78, 68, 35, -1,
    73, -1, -1, 55, -1, 57, -1, -1, -1, -1, 93, -1, 33, -1, 71, -1, -1, 80, -1, -1, 48, -1, -1, -1,
    -1, -1, 95, -1, -1, -1, -1, -1, -1, 60, -1, -1, -1, -1, -1, -1, -1, -1, -1, -1, -1, 46, -1, -1,
    74, -1, -1, -1, -1, -1, 58, 37, 75, 82, 38, 92, 72, 59, 94, 61, 50, 51, -1, 79, 62, 97, -1, -1,
    84, -1, 76, 81, -1, 77, 63, 99, -1, 64, -1, -1, 86, -1, -1, -1, 96, -1, -1, -1, 101, 98, -1,
    -1, -1, 88, 83, -1, -1, 85, -1, -1, 102, 100, -1, 103, -1, -1, -1, -1, 89, 87, -1, -1, -1, 90,
    -1, -1, -1, -1, -1, -1, -1, -1, -1, -1, -1, -1, -1, -1, -1, -1, -1, -1, -1, -1, -1, -1, -1, -1,
    -1, -1, -1, -1, -1, -1, -1, -1, -1,
)
BACK_JOINT_ENDS = (
    -1, -1, -1, -1, -1, -1, -1, -1, -1, -1, -1, -1, -1, -1, -1, -1, -1, -1, -1, -1, -1, -1, -1, -1,
    -1, -1, -1, -1, -1, -1, -1, -1, 0, -1, 1, 2, 3, 4, 5, 17, -1, 18, -1, 19, 6, 20, 7, 21, 22, 34,
    8, 35, 9, 36, 10, 37, 11, 38, 12, 39, -1, -1, -1, -1, -1, -1, -1, 13, 23, 24, -1, -1, -1, -1,
    -1, -1, -1, -1, -1, 14, 25, 26, 27, 28, 29, -1, -1, -1, -1, -1, 40, 41, -1, -1, 15, -1, 42, 43,
    44, 45, 46, -1, -1, 30, -1, 16, -1, -1, -1, 31, -1, -1, -1, 51, 32, 52, 53, 54, 55, -1, 56, 47,
    48, 49, -1, 33, -1, -1, -1, 57, 58, -1, -1, -1, 50, 59, 60, 61, 62, 63, -1, -1, 64, -1, -1, -1,
    65, -1, -1, -1, 66, -1, -1, -1, -1, -1, -1, -1, -1, 67, -1, -1, -1, -1, -1, -1, -1, -1,
)
BACK_JOINT_MIDDLES = (
    -1, -1, -1, -1, -1, -1, -1, -1, -1, -1, -1, -1, -1, -1, -1, -1, -1, -1, -1, -1, -1, -1, -1, -1,
    -1, -1, -1, -1, -1, -1, -1, -1, 0, -1, 1, 2, 3, 4, 5, 17, -1, 18, -1, 19, 6, 20, 7, 21, 22, 34,
    8, 35, 9, 36, 10, 37, 11, 38, 12, 39, -1, -1, -1, -1, -1, -1, -1, 23, 24, -1, -1, -1, -1, -1,
    -1, 13, -1, -1, -1, 25, 26, 27, 28, 29, -1, -1, -1, -1, -1, 40, 14, 41, -1, -1, 15, 42, 43, 44,
    45, 46, -1, -1, -1, -1, 16, -1, -1, -1, -1, 30, -1, -1, 51, 31, 52, 32, 53, 54, 55, 56, -1, -1,
    -1, 33, 47, -1, 48, -1, 57, 49, 58, 50, -1, -1, 59, 60, 61, 62, 63, -1, -1, -1, -1, -1, -1, -1,
    -1, 64, -1, -1, -1, 65, -1, 66, -1, -1, -1, 67, -1, -1, -1, -1, -1, -1, -1, -1, -1, -1,
)
BACK_SPACE_ENDS = (
    0, -1, 1, 2, 3, 4, 5, -1, -1, -1, -1, -1, 6, 7, 17, -1, 18, 8, 19, 9, 20, 10, 21, 11, 22, 12,
    -1, -1, 13, -1, -1, -1, -1, -1, -1, -1, -1, -1, 14, 23, 24, 34, 35, 36, 15, 37, 38, 39, -1, -1,
    -1, -1, 25, 26, 27, 28, 29, -1, -1, -1, -1, -1, -1, 30, 16, -1, -1, -1, -1, -1, -1, -1, 40, 31,
    41, 42, 43, 44, 45, 46, -1, -1, -1, -1, -1, 32, -1, -1, -1, -1, -1, 47, -1, 48, -1, 33, 49, -1,
    -1, -1, -1, -1, -1, 50, -1,
)
BACK_SPACE_MIDDLES = (
    0, -1, 1, 2, 3, 4, 5, -1, -1, -1, -1, -1, 6, 7, 17, -1, 18, 8, 19, 9, 20, 10, 21, 11, 22, 12,
    -1, -1, -1, -1, -1, -1, -1, -1, 13, -1, -1, -1, 23, 24, 34, 35, 36, 37, 38, 39, -1, -1, 14, 15,
    -1, -1, 25, 26, 27, 28, 29, -1, -1, -1, -1, -1, -1, 16, -1, -1, -1, -1, -1, -1, -1, 30, 40, 41,
    42, 43, 44, 45, 46, -1, -1, -1, -1, -1, 31, 32, -1, -1, -1, -1, -1, -1, -1, 33, -1, 47, -1, 48,
    -1, 49, -1, 50, -1, -1, -1,
)
LAST_ENDS = (
    0, 17, 18, 19, 20, 21, 22, 23, 24, 25, 26, 27, 28, 1, 2, 3, 4, 5, 6, 7, 8, 9, 10, 11, 12, 13,
    29, 14, 30, 15, 31, 32, 33, -1, -1, 16,
)
LAST_MIDDLES = (
    0, 1, 2, 3, 4, 5, 6, 7, 17, 8, 9, 10, 11, 12, 18, 25, 19, 26, 20, 27, 21, 28, 22, 23, 24, 29,
    30, 31, 32, 33, -1, 13, -1, 14, 15, 16,
)


def exact(left, right, dims):
    return lax.dot_general(
        left, right, (dims, ((), ())), precision=lax.Precision.HIGHEST, preferred_element_type=FULL
    )


def joint_pattern():
    keys, queries = np.meshgrid(np.arange(CHUNK), np.arange(CHUNK), indexing="ij")
    at = (queries // SW - keys // SW + SW - 1) * SPAN_T + queries % SW - keys % SW + SW - 1
    return (jnp.arange(SPAN_T**2)[:, None] == jnp.asarray(at.reshape(-1), jnp.int32)[None, :]).astype(FULL)


def joint_table(lookup):
    flat = lookup.reshape(HEADS * (2 * TW - 1), SPAN_T**2)
    grid = exact(flat, joint_pattern(), ((1,), (0,)))
    grid = grid.reshape(HEADS // 2, 2, 2 * TW - 1, CHUNK, CHUNK)
    return jnp.concatenate([grid[:, 0], grid[:, 1]], axis=-1)


def joint_table_back(grad):
    pairs = jnp.stack([grad[..., :CHUNK], grad[..., CHUNK:]], axis=1)
    flat = pairs.reshape(HEADS * (2 * TW - 1), CHUNK * CHUNK)
    return exact(flat, joint_pattern(), ((1,), (1,))).reshape(HEADS, -1)


def space_pattern(quarter):
    query = jnp.arange(CHUNK)
    key_col = jnp.arange(2 * SW)
    gap = quarter % 2 * SW + (query % SW)[None, :] - key_col[:, None] + 2 * SW - 1
    row = jnp.broadcast_to((query // SW)[None, :], gap.shape)
    at = (row * SPAN_S + gap).reshape(-1)
    return (jnp.arange(SW * SPAN_S)[:, None] == at[None, :]).astype(FULL)


def space_table(lookup, quarter):
    grid = lookup.reshape(HEADS, SPAN_S, SPAN_S)
    seen = lax.dynamic_slice_in_dim(grid, quarter // 2 * SW, 3 * SW - 1, 1)
    rows = jnp.stack([seen[:, 2 * SW - 1 - k : 3 * SW - 1 - k] for k in range(2 * SW)])
    made = exact(rows.reshape(2 * SW * HEADS, SW * SPAN_S), space_pattern(quarter), ((1,), (0,)))
    made = made.reshape(2, SW, HEADS // 2, 2, 2, SW, CHUNK)
    made = made.transpose(2, 0, 4, 1, 5, 3, 6)
    return made.reshape(HEADS // 2, 4 * CHUNK, 2 * CHUNK)


def space_table_back(grad, quarter):
    made = grad.reshape(HEADS // 2, 2, 2, SW, SW, 2, CHUNK).transpose(1, 3, 0, 5, 2, 4, 6)
    flat = made.reshape(2 * SW * HEADS, 2 * SW * CHUNK)
    rows = exact(flat, space_pattern(quarter), ((1,), (1,))).reshape(2 * SW, HEADS, SW, SPAN_S)
    seen = sum(
        jnp.pad(rows[k], ((0, 0), (2 * SW - 1 - k, k), (0, 0))) for k in range(2 * SW)
    )
    grid = jnp.zeros((HEADS, SPAN_S, SPAN_S), FULL)
    return lax.dynamic_update_slice_in_dim(grid, seen, quarter // 2 * SW, 1).reshape(HEADS, -1)


def modulations(cond, shards):
    groups = cond.shape[0]
    rows = shards[0].shape[0]
    own = lax.dynamic_slice_in_dim(cond, lax.axis_index("wide") * rows, rows, 2)
    flat = own.reshape(groups * 2, rows)
    terms = jnp.stack([nn(flat, s).reshape(groups, 2, -1) for s in shards], axis=1)
    summed = lax.psum_scatter(terms, "wide", scatter_dimension=0, tiled=False)
    gathered = lax.all_gather(summed, "narrow", axis=0, tiled=False)
    return gathered.transpose(1, 2, 0, 3).reshape(2, 2, 6 * D)


def modulation_grads(cond, grads, rows):
    groups = cond.shape[0]
    own = lax.dynamic_slice_in_dim(cond, lax.axis_index("wide") * rows, rows, 2)
    flat = own.reshape(groups * 2, rows).astype(FULL)
    summed = lax.psum_scatter(
        grads.reshape(2, 2, 4, -1), "narrow", scatter_dimension=2, tiled=False
    )
    gathered = lax.all_gather(summed, "wide", axis=0, tiled=False)
    return [exact(flat, gathered[:, b].reshape(groups * 2, -1), ((0,), (0,))) for b in range(2)]


def gather_flat(shards):
    wide, narrow = lax.axis_size("wide"), lax.axis_size("narrow")
    project, output, expand, shrink = shards
    rows = project.shape[0]

    def settle(blocks):
        rows, cols = blocks.shape[-2:]
        blocks = blocks.reshape(wide, narrow, rows, cols).transpose(0, 2, 1, 3)
        return blocks.reshape(wide * rows, narrow * cols)

    first = lax.all_gather(
        jnp.concatenate([project, output, expand], axis=1), ("wide", "narrow"), axis=0, tiled=False
    )
    second = lax.all_gather(shrink, ("wide", "narrow"), axis=0, tiled=False)
    a, b = project.shape[1], project.shape[1] + output.shape[1]
    return settle(first[..., :a]), settle(first[..., a:b]), settle(first[..., b:]), settle(second)


def scatter_plain(partials):
    outs = []
    for g in partials:
        summed = lax.psum_scatter(g, "wide", scatter_dimension=0, tiled=True)
        outs.append(lax.psum_scatter(summed, "narrow", scatter_dimension=1, tiled=True).astype(FULL))
    return outs


def saved(b):
    return b.branch, b.middle, b.normed, b.active, b.slope, b.reduced


def mlp_takes(b):
    return A.live, b.rows, b.attended, b.mods, b.output, b.expand, b.shrink


def back_takes(b, grad):
    early = A.live, grad, b.attended, b.mods, b.branch, b.middle, b.normed, b.reduced
    return early + (b.output, b.active, b.slope, b.expand, b.shrink)


def back_gives(b):
    return b.to_shrink, b.to_expand, b.to_output, b.to_middle, b.to_attended, b.late


def weights_of(b):
    return b.project, b.output, b.expand, b.shrink


def shards_of(b):
    return b.own_project, b.own_output, b.own_expand, b.own_shrink


def partials_of(b):
    return b.to_shrink, b.to_expand, b.to_output, b.to_project


def grads_of(b):
    return b.grad_shrink, b.grad_expand, b.grad_output, b.grad_project


def stages():
    return {
        S.triple: (
            space_triple(),
            (A.all_rows, S.mods, S.project),
            (S.first, S.queries, S.pairs),
        ),
        S.attend: (
            space_attend(),
            (S.queries, S.pairs, S.pairs, S.table),
            (S.attended,),
        ),
        S.mlp: (
            mlp(False),
            mlp_takes(S),
            saved(S) + (J.rows,),
        ),
        J.triple: (
            joint_triple(),
            (J.rows, J.mods, J.project),
            (J.first, J.three),
        ),
        J.attend: (
            joint_attend(),
            (J.three,) * 3 + (J.table,),
            (J.attended,),
        ),
        J.mlp: (
            mlp(True),
            mlp_takes(J),
            saved(J) + (A.output_tokens,),
        ),
        J.mlp_back: (
            mlp_back(True),
            back_takes(J, A.cotangent),
            back_gives(J),
        ),
        J.attend_back: (
            joint_attend_back(),
            (J.three,) * 3 + (J.table, J.to_attended),
            (J.to_three, J.to_table),
        ),
        J.project_back: (
            joint_project_back(),
            (J.rows, J.mods, J.first, J.to_middle, J.project, J.to_three),
            (J.to_project, J.to_rows, J.early),
        ),
        S.mlp_back: (
            mlp_back(False),
            back_takes(S, J.to_rows),
            back_gives(S),
        ),
        S.attend_back: (
            space_attend_back(),
            (S.queries, S.pairs, S.pairs, S.table, S.to_attended),
            (S.to_queries, S.to_pairs, S.to_table),
        ),
        S.project_back: (
            space_project_back(),
            (S.first, S.project, S.to_queries, S.to_pairs),
            (S.to_project, A.to_first),
        ),
        A.finish: (
            finish(),
            (S.rows, S.mods, A.own_first, S.to_middle),
            (A.grad_tokens, S.early),
        ),
    }


def apart(values, names):
    for name in names:
        phase, takes, gives = stages()[name]
        values.update(zip(gives, phase(*[values[k] for k in takes])))


def together(values, plan, tables, engine, moved, brought, name, more=(), final=None):
    table = stages()
    outs, args = {}, {}
    for phase_name in plan:
        phase, takes, gives = table[phase_name]
        outs.update(zip(gives, phase.out_shape))
    for phase_name in plan:
        for k in table[phase_name][1]:
            if k not in outs and k not in brought:
                args[k] = values[k]
    for k in tuple(moved) + tuple(more):
        if k not in outs:
            args[k] = values[k]

    def script(refs, engine_outs, feed):
        refs.update(zip(brought, engine_outs))
        feed.follow(tables)
        feed.enter()
        for phase_name in plan:
            phase, takes, gives = table[phase_name]
            phase.inside(feed.over(phase), [refs[k] for k in takes], [refs[k] for k in gives])
        if final is not None:
            feed.do(feed.slot)
            feed.slot += 1
            final(refs)
        feed.rest()

    made, arrived = fused(script, args, outs, engine, moved, name)
    values.update(made)
    values.update(zip(brought, arrived))


def body(
    tokens,
    clip_cond,
    image_cond,
    image_count,
    space_modulate,
    space_project,
    space_output,
    space_expand,
    space_reduce,
    space_bias,
    joint_modulate,
    joint_project,
    joint_output,
    joint_expand,
    joint_reduce,
    joint_bias,
    cotangent,
):
    small = lax.axis_size("wide") == 8
    narrow = lax.axis_index("narrow")
    wide = lax.axis_index("wide")
    rows = space_modulate.shape[0]
    low_clips = jax.nn.silu(clip_cond.astype(FULL)).astype(LOW)
    low_images = jax.nn.silu(image_cond.astype(FULL)).astype(LOW)
    values = {
        A.live: (image_count > 0).astype(FULL),
        S.rows: tokens,
        A.cotangent: cotangent,
        S.table: space_table(space_bias, narrow),
        J.table: joint_table(joint_bias),
    }
    weights = weights_of(S) + weights_of(J)
    space_shards = space_project, space_output, space_expand, space_reduce
    joint_shards = joint_project, joint_output, joint_expand, joint_reduce

    if small:
        moved = shards_of(S) + shards_of(J)
        shapes = [v.shape for v in space_shards + joint_shards]
        values.update(zip(moved, space_shards + joint_shards))
        values[A.images] = jnp.broadcast_to(low_images.astype(FULL).reshape(8, 1, rows), (8, 8, rows))
        own_clips = lax.dynamic_slice_in_dim(low_clips, wide * rows, rows, 1).astype(FULL)
        values[A.clips] = jnp.pad(own_clips, ((0, 6), (0, 0)))
        values[S.own_modulate] = space_modulate
        values[J.own_modulate] = joint_modulate
        gather = Gather(shapes, True, 0)
        together(
            values,
            FORWARD,
            (FORWARD_ENDS, FORWARD_MIDDLES),
            Joined(gather, Modulation()),
            moved + (S.rows, A.images, A.clips, S.own_modulate, J.own_modulate),
            weights + (A.all_rows, S.mods, J.mods, A.cond),
            "forward",
        )
        project_shape, output_shape, expand_shape, shrink_shape = shapes[:4]
        shapes = [shrink_shape, expand_shape, output_shape, project_shape]
        engine = Scatter(shapes, False, 1)
        tables = BACK_JOINT_ENDS, BACK_JOINT_MIDDLES
        together(values, BACK_JOINT, tables, engine, partials_of(J), grads_of(J), "back_joint")
        engine = Scatter(shapes[:3], False, 2)
        tables = BACK_SPACE_ENDS, BACK_SPACE_MIDDLES
        takes, gives = partials_of(S)[:3], grads_of(S)[:3]
        together(values, BACK_SPACE, tables, engine, takes, gives, "back_space")
        back = ModulationBack()
        late = (A.cond, S.late, J.early, J.late)

        def final(refs):
            early = refs[S.early], refs[J.early]
            back.finish(refs[A.cond], early, (refs[S.late], refs[J.late]))

        together(
            values,
            LAST,
            (LAST_ENDS, LAST_MIDDLES),
            Joined(Scatter(shapes[3:], True, 3), back),
            (S.to_project, A.to_first),
            (S.grad_project, A.own_first, S.modulate, J.modulate),
            "last_sums",
            late,
            final,
        )
        modulate = values[S.modulate], values[J.modulate]
    else:
        image_all = lax.all_gather(low_images, "wide", axis=0, tiled=True)
        cond = jnp.stack([jnp.repeat(low_clips, 4, axis=0), image_all], axis=1)
        values[S.mods], values[J.mods] = modulations(
            cond, (space_modulate, joint_modulate)
        )
        values.update(zip(weights[:4], gather_flat(space_shards)))
        values.update(zip(weights[4:], gather_flat(joint_shards)))
        values[A.all_rows] = lax.all_gather(tokens, "narrow", axis=0, tiled=True)
        apart(values, FORWARD + BACK_JOINT + BACK_SPACE)
        for b in (J, S):
            values.update(zip(grads_of(b), scatter_plain([values[k] for k in partials_of(b)])))
        values[A.own_first] = lax.psum_scatter(
            values[A.to_first].astype(FULL), "narrow", scatter_dimension=0, tiled=True
        )
        apart(values, [A.finish])
        both = [
            jnp.concatenate([values[b.early], values[b.late][:, 2 * D :]], axis=1) for b in (S, J)
        ]
        modulate = modulation_grads(cond, jnp.stack(both), rows)
    bias = lax.psum(
        jnp.concatenate(
            [
                space_table_back(values[S.to_table], narrow),
                joint_table_back(values[J.to_table]),
            ],
            axis=1,
        ),
        ("wide", "narrow"),
    )
    split = space_bias.shape[1]
    bias = (bias[:, :split], bias[:, split:])
    outs = [values[A.output_tokens], values[A.grad_tokens]]
    for i, b in enumerate((S, J)):
        outs += [modulate[i]] + [values[k] for k in reversed(grads_of(b))] + [bias[i]]
    return tuple(outs)


FORWARD = S.triple, S.attend, S.mlp, J.triple, J.attend, J.mlp
BACK_JOINT = J.mlp_back, J.attend_back, J.project_back, S.mlp_back
BACK_SPACE = S.attend_back, S.project_back
LAST = (A.finish,)


def solution(mesh):
    rows = P(("wide", "narrow"), None)
    block = P("wide", "narrow")
    in_specs = (
        (rows, P(), P("wide", None), P("wide"))
        + (block,) * 5
        + (P(),)
        + (block,) * 5
        + (P(), rows)
    )
    out_specs = (rows, rows) + ((block,) * 5 + (P(),)) * 2
    return jax.shard_map(body, mesh=mesh, in_specs=in_specs, out_specs=out_specs, check_vma=False)
```

time: 971 us -> 814 us (0.84)
  Pallas kernels: 847 us -> 713 us
  blocking collectives: 33.1 us -> 0 us
  waiting for transfers between devices: 0.07 us -> 10.5 us
    pallas_call x17 -> x4, Pallas kernels: 847 us -> 713 us  [fused(): pl.pallas_call(kernel, in_specs=in_specs, out_specs=[pl.BlockSpec(memory_...]
    all_gather x3 -> x0, blocking collectives: 33.1 us -> none  [the longest x1 13.3 us: modulations(): gathered = lax.all_gather(summed, 'narrow', axis=0, tiled=False)]
    psum x1, waiting for transfers between devices: 0.02 us -> 10.5 us  [body(): lax.psum(jnp.concatenate([space_table_back(values[S.to_table], narrow), j...]
  transfers between devices with their start and end apart: 3 -> 1, of which waited for: 0 -> 1; matrix products, arithmetic and copies ran while one was open for 3% -> 0% of each run, Pallas kernels for 59% -> 14%
where the time goes in v2:
time: 814 us; the launch traced here: 803 us
  Pallas kernels  713 us (88%)
  local copies, waits for them, and re-layouts  52.6 us (6%)
  between operations  15.4 us (2%)
  waiting for transfers between devices  10.5 us (1%)
    pallas_call x4, Pallas kernels, fused(): pl.pallas_call(kernel, in_specs=in_specs, out_specs=[pl.BlockSpec(memory_...  713 us
  transfers between devices with their start and end apart: 1, of which 1 were waited for; matrix products, arithmetic and copies ran while one was open for 0% of the time, Pallas kernels for 14%

profile of v2, /device:TPU:0, one launch (start us, length us, event | category | flops | bytes accessed | tf_op | source)
XLA Modules:
  0.0 803.4 jit_solution(9820269393639960820)
XLA Ops:
  7.2 1.1 reshape.170
  8.9 0.5 reshape.182
  9.5 0.2 iota_compare_fusion.3
  9.7 0.4 copy-done.16
  10.1 1.0 convolution_bitcast_fusion.1
  11.1 1.6 copy.37
  12.7 2.1 reshape.171.refs_0_.refs_2_
  14.9 0.6 pad_convert_fusion.refs_13_
  15.5 0.1 reshape.172
  15.7 1.8 convolution_bitcast_fusion
  17.5 3.6 reshape.173
  21.1 3.1 slice_bitcast_fusion.1
  24.9 2.1 pad_maximum_fusion.1.refs_3_.refs_14_
  27.0 0.6 broadcast_in_dim.14.refs_12_
  27.6 318.1 %forward.1 = (bf16[2304,1024]{1,0:T(8,128)(2,1)}, bf16[576,1024]{1,0:T(8,128)(2,1)}, bf16[4,576,2048]{2,1,0:T(8,128)(2,1)}, bf16[576,1024]{1,0:T(8,128)(2,1)}, b...) custom-call(f32[8,256,128]{2,1,0:T(8,128)} %reshape.171.refs_0_.refs, ...), custom_call_target="tpu_custom_call" | custom-call | flops 99999997952 | tf_op jit(solution)/shard_map/forward/pallas_call | solution.py:1336
  345.7 182.8 %back_joint.1 = (bf16[4096,1024]{1,0:T(8,128)(2,1)}, bf16[1024,4096]{1,0:T(8,128)(2,1)}, bf16[1024,1024]{1,0:T(8,128)(2,1)}, f32[576,1024]{1,0:T(8,128)}, bf16[5...) custom-call(f32[1]{0:T(128)S(6)} %convert_element_type.44.refs_1_.re, ...), custom_call_target="tpu_custom_call" | custom-call | flops 99999997952 | tf_op jit(solution)/shard_map/back_joint/pallas_call | solution.py:1336
  528.5 98.8 %back_space.1 = (bf16[576,1024]{1,0:T(8,128)(2,1)}, bf16[2,4,576,1024]{3,2,1,0:T(8,128)(2,1)}, f32[8,256,128]{2,1,0:T(8,128)}, bf16[1024,3072]{1,0:T(8,128)(2,1)...) custom-call(bf16[576,1024]{1,0:T(8,128)(2,1)} %get-tuple-element.97.refs_0_, ...), custom_call_target="tpu_custom_call" | custom-call | flops 99999997952 | tf_op jit(solution)/shard_map/back_space/pallas_call | solution.py:1336
  627.3 2.5 reshape.174
  629.8 1.6 copy.69
  631.5 2.2 reshape.175
  633.7 0.8 fusion.3
  634.4 1.2 fusion.25
  635.7 0.7 squeeze.56
  636.5 0.7 squeeze.57
  637.3 0.7 squeeze.58
  638.1 0.7 squeeze.59
  638.8 0.7 squeeze.60
  639.6 1.1 copy.46
  640.7 0.7 squeeze.61
  641.4 1.0 copy.47
  642.4 0.7 squeeze.62
  643.3 0.1 squeeze.64
  643.5 0.1 squeeze.65
  643.6 0.1 squeeze.66
  643.8 0.1 squeeze.67
  644.0 0.1 squeeze.68
  644.1 0.7 squeeze.69
  645.2 1.3 pad_add_fusion
  646.5 0.3 dynamic_update_slice.3
  646.8 0.2 reshape.176
  646.9 0.9 slice_bitcast_fusion.3
  647.9 1.0 pad_maximum_fusion
  648.9 2.9 copy.57
  651.8 3.8 reshape.177
  655.6 2.4 fusion
  658.1 0.1 reshape.178
  658.2 0.8 pad_maximum_fusion.2
  659.0 113.2 %last_sums.1 = (f32[576,1024]{1,0:T(8,128)}, f32[2,2048]{1,0:T(2,128)}, f32[128,768]{1,0:T(8,128)}, f32[576,1024]{1,0:T(8,128)}, f32[128,1536]{1,0:T(8,128)}, /*index=5*/f32[128,1536]{1,0:T(8,128)}) custom-call(bf16[576,1024]{1,0:T(8,128)(2,1)} %refs_0_.1, f32[2,6144]{1,0:T(2,128)} %get-tuple-element.70.refs_19_.refs_1_, ...), custom_call_target="tpu_custom_call" | custom-call | flops 99999997952 | tf_op jit(solution)/shard_map/last_sums/pallas_call | solution.py:1336
  772.2 10.5 %all-reduce.19.cloned.1.call-done = f32[16,2986]{1,0:T(8,128)} async-done(((f32[16,2986]{1,0:T(8,128)}), f32[16,2986]{1,0:T(8,128)}) %all-reduce.19.cloned.1.call-update) | async-done | bytes 191120 | tf_op jit(solution)/shard_map/psum | solution.py:1988
  782.7 1.7 slice.187
  784.4 1.5 slice.186
  785.9 1.0 copy.102
  786.9 1.4 copy.103
  788.3 0.3 copy-done.4
  788.6 0.9 copy.104
  789.5 0.7 copy.105
  790.2 0.7 copy.106
  790.9 0.8 copy.107
  791.7 0.8 copy.108
  792.5 0.9 copy.109
  793.3 0.7 copy.110
  794.1 0.7 copy.111
  794.8 0.8 copy.112
  795.5 0.8 copy.113
  (80 shorter events, 1.7 us)
Async XLA Ops:
  7.2 775.5 %all-reduce.19.cloned.1.call-start = ((), (), s32[]{:S(2)}) async-start(), calls=%async_computation | async-start | bytes 393216 | tf_op jit(solution)/shard_map/psum | solution.py:1988
  9.5 0.6 copy-start.16
  12.7 2.2 copy-start.18
  12.7 2.8 copy-start.11
  12.7 2.9 copy-start.14
  21.1 3.8 copy-start.19
  631.5 2.2 copy-start.17
  639.6 7.4 copy-start
  651.8 3.9 copy-start.15
  659.0 126.9 %copy-start.2 = (bf16[576,1024]{1,0:T(8,128)(2,1)S(1)}, bf16[576,1024]{1,0:T(8,128)(2,1)}, u32[]{:S(2)}) copy-start(bf16[576,1024]{1,0:T(8,128)(2,1)} %get-tuple-element.160) | copy-start | bytes 3538948
  772.2 14.7 %copy-start.1 = (f32[576,1024]{1,0:T(8,128)S(1)}, f32[576,1024]{1,0:T(8,128)}, u32[]{:S(2)}) copy-start(f32[576,1024]{1,0:T(8,128)} %get-tuple-element.161) | copy-start | bytes 7077892
  786.9 1.7 copy-start.4
  786.9 2.6 copy-start.10
  788.6 1.6 copy-start.13
  788.6 2.3 copy-start.8
  788.6 3.1 copy-start.7
  788.6 3.9 copy-start.3
  789.5 3.9 copy-start.9
  790.2 3.9 copy-start.12
  790.9 3.9 copy-start.6
  791.7 3.9 copy-start.5
Sparse Core Ops, SparseCore 0:
  659.1 123.5 all-reduce.18

commit v3 on v2

--- a/solution.py
+++ b/solution.py
@@ -329,6 +329,7 @@
         grad_q[at, :] = to_q.astype(LOW)
         grad_pairs[0, :, at, :] = to_k.astype(LOW).reshape(4, CHUNK, 2 * HEAD_DIM)
         grad_pairs[1, :, at, :] = to_v.astype(LOW).reshape(4, CHUNK, 2 * HEAD_DIM)
+        to_bias = to_bias.reshape(2, 2, SW, SW, 2 * HEAD_DIM)
         if i == 0:
             grad_bias[0] = to_bias
         else:
@@ -350,11 +351,15 @@
             table,
             head,
         ],
-        out_specs=[head, spec((2, 4, ROWS_DEV, wide), lambda h: (0, 0, 0, h)), table],
+        out_specs=[
+            head,
+            spec((2, 4, ROWS_DEV, wide), lambda h: (0, 0, 0, h)),
+            spec((1, 2, 2, SW, SW, wide), lambda h: (h, 0, 0, 0, 0, 0)),
+        ],
         out_shape=[
             shape((ROWS_DEV, D), LOW),
             shape((2, 4, ROWS_DEV, D), LOW),
-            shape((HEADS // 2, 4 * CHUNK, wide), FULL),
+            shape((HEADS // 2, 2, 2, SW, SW, wide), FULL),
         ],
         name="space_attend_back",
         ticks=3,
@@ -412,12 +417,12 @@
         )
         grads[0, at, :] = to_q.astype(LOW)
         if i >= TW:
-            grad_bias[0, TW - 1] += to_bias
+            grad_bias[TW - 1] += to_bias
             grads[1, at, :] = to_k.astype(LOW)
             grads[2, at, :] = to_v.astype(LOW)
             continue
         for t in range(TW):
-            grad_bias[0, i - t + TW - 1] += to_bias[t * CHUNK : (t + 1) * CHUNK]
+            grad_bias[i - t + TW - 1] += to_bias[t * CHUNK : (t + 1) * CHUNK]
         if i == 0:
             sum_k[...] = to_k
             sum_v[...] = to_v
@@ -436,10 +441,13 @@
         joint_attend_back_kernel,
         grid=(HEADS // 2,),
         in_specs=joint_specs() + [head],
-        out_specs=[spec((3, ROWS_DEV, wide), lambda h: (0, 0, h)), joint_specs()[3]],
+        out_specs=[
+            spec((3, ROWS_DEV, wide), lambda h: (0, 0, h)),
+            spec((2 * TW - 1, CHUNK, wide), lambda h: (h, 0, 0)),
+        ],
         out_shape=[
             shape((3, ROWS_DEV, D), LOW),
-            shape((HEADS // 2, 2 * TW - 1, CHUNK, wide), FULL),
+            shape((HEADS // 2 * (2 * TW - 1), CHUNK, wide), FULL),
         ],
         scratch_shapes=[pltpu.VMEM((CLIP_ROWS, wide), FULL)] * 2,
         name="joint_attend_back",
@@ -727,6 +735,93 @@
     )
 
 
+def space_first_back(feed, ticks, order, weight, grad_q, grad_pairs, out):
+    half = ROWS_DEV // 2
+    first = feed.slot
+    feed.slot += ticks
+
+    def scoped(weights, queries, pairs, sems):
+        def pair_load(j):
+            return pltpu.make_async_copy(
+                grad_pairs.at[:, order[j]], pairs.at[(3 - j) % 2], sems.at[(3 - j) % 2]
+            )
+
+        loads = [
+            pltpu.make_async_copy(weight, weights, sems.at[2]),
+            pltpu.make_async_copy(grad_q, queries, sems.at[3]),
+        ]
+        for load in loads:
+            load.start()
+        pair_load(3).start()
+        for load in loads:
+            load.wait()
+        for step in range(4):
+            j = 3 - step
+            if j:
+                pair_load(j - 1).start()
+            pair_load(j).wait()
+            for side in range(2):
+                feed.do(first + 2 * step + side)
+                rows = slice(side * half, (side + 1) * half)
+                value = nt(pairs[step % 2, 0, rows, :], weights[:, part(1)])
+                value += nt(pairs[step % 2, 1, rows, :], weights[:, part(2)])
+                if j == 0:
+                    value += nt(queries[rows, :], weights[:, part(0)])
+                for p in range(2):
+                    piece = value[p * (half // 2) : (p + 1) * (half // 2)]
+                    out[2 * side + p, order[j]] = piece.astype(LOW)
+
+    pl.run_scoped(
+        scoped,
+        pltpu.VMEM((D, 3 * D), LOW),
+        pltpu.VMEM((ROWS_DEV, D), LOW),
+        pltpu.VMEM((2, 2, ROWS_DEV, D), LOW),
+        pltpu.SemaphoreType.DMA((4,)),
+    )
+
+
+def space_weight_back_kernel(tick, normed, grad_q, grad_pairs, grad_weight):
+    step = pl.program_id(0)
+    own = span(lax.axis_index("narrow"), ROWS_DEV)
+    tick(0)
+
+    @pl.when(step < 2)
+    def _():
+        grad_weight[...] = tn(normed[own, :], grad_q[...]).astype(LOW)
+
+    for side in range(2):
+        if side:
+            tick(1)
+
+        @pl.when(step >= 2)
+        def _():
+            columns = slice(side * 256, (side + 1) * 256)
+            flat = grad_pairs[0, :, :, columns].reshape(4 * ROWS_DEV, 256)
+            grad_weight[:, columns] = tn(normed[...], flat).astype(LOW)
+
+
+def space_weight_back():
+    tile = 512
+
+    def pair(t):
+        late = jnp.maximum(t - 2, 0)
+        return (late // 2, 0, 0, late % 2)
+
+    return Phase(
+        space_weight_back_kernel,
+        grid=(3 * D // tile,),
+        in_specs=[
+            whole((4 * ROWS_DEV, D)),
+            spec((ROWS_DEV, tile), lambda t: (0, jnp.minimum(t, 1))),
+            spec((1, 4, ROWS_DEV, tile), pair),
+        ],
+        out_specs=[spec((D, tile), lambda t: (0, t))],
+        out_shape=[shape((D, 3 * D), LOW)],
+        name="space_weight_back",
+        ticks=2,
+    )
+
+
 def finish_kernel(tick, rows, mods, grad_normed, grad_middle, grad_rows, grad_mods):
     tick(0)
     finish_rows(rows, grad_normed, grad_middle, mods, grad_rows, grad_mods)
@@ -831,7 +926,6 @@
 class Feed:
     def __init__(self, enter):
         self.enter, self.steps, self.drains = enter, [], []
-        self.late_enter = lambda: None
 
     def add(self, function, *args):
         self.steps.append(functools.partial(function, *args))
@@ -1088,7 +1182,6 @@
     def __init__(self, shapes, line, collective_id):
         self.shapes, self.line, self.collective_id = shapes, line, collective_id
         count, lines = len(shapes), 1 if line else 0
-        self.in_specs = [pl.BlockSpec(memory_space=pl.ANY)] * (count + lines)
         self.out_shape = [shape(s, FULL) for s in shapes] + [shape((ROWS_DEV, D), FULL)] * lines
         self.out_specs = [pl.BlockSpec(memory_space=pltpu.VMEM)] * len(self.out_shape)
         self.scratch = []
@@ -1115,7 +1208,6 @@
             pltpu.VMEM((PIECES, 4, PIECE, D), LOW),
             pltpu.VMEM((PIECES, 5, PIECE, D), LOW),
             DMA((PIECES, 4)),
-            DMA((PIECES, 4)),
             DMA((PIECES, 5)),
         ] * lines
 
@@ -1246,26 +1338,15 @@
                 z_copy(k, order[j], order[j], at.up).wait_send()
 
         if self.line:
-            line_held, line_in, line_load, line_send, line_recv = scratch[5 * count + 9 :]
-
-            def line_loads(p, col):
-                here = pl.ds(pl.multiple_of(col * ROWS_DEV + p * PIECE, 16), PIECE)
-                return pltpu.make_async_copy(
-                    ins[count].at[here], line_held.at[p, col], line_load.at[p, col]
-                )
+            line_held, line_in, line_send, line_recv = scratch[5 * count + 9 :]
+            self.line_held = line_held
 
             def line_copy(p, col, slot, to):
                 sems = line_send.at[p, col], line_recv.at[p, slot]
                 return remote(line_held.at[p, col], line_in.at[p, slot], *sems, (w, to))
 
-            def line_begin():
-                for j in (3, 2, 1, 0):
-                    for p in range(PIECES):
-                        line_loads(p, order[j]).start()
-
             def line_stage(j, p):
                 col = order[j]
-                line_loads(p, col).wait()
 
                 @pl.when(at.carried(col))
                 def _():
@@ -1277,7 +1358,6 @@
 
             def line_last(p):
                 here = pl.ds(p * PIECE, PIECE)
-                line_loads(p, n).wait()
                 outs[count][here, :] = line_held[p, n].astype(FULL)
 
                 @pl.when(n > 0)
@@ -1315,8 +1395,6 @@
                 items.add(line_last, p)
             items.add(lambda: None)
             items.drain(line_drain)
-            items.enter = lambda: (at.enter(), line_begin())
-            items.late_enter = line_begin
         return items
 
 
@@ -1361,13 +1439,7 @@
         feed = self.engine.steps(ins[: cuts[0]], outs[: cuts[1]], scratch[: cuts[2]])
         for step in self.other.steps(ins[cuts[0] :], outs[cuts[1] :], scratch[cuts[2] :]):
             feed.add(step)
-        begin = feed.late_enter
-
-        def enter():
-            Place().enter_all()
-            begin()
-
-        feed.enter = enter
+        feed.enter = Place().enter_all
         return feed
 
 
@@ -1521,7 +1593,8 @@
             to = (lax.bitwise_xor(w, step), n)
             return remote(every.at[w], every.at[w], send.at[1, step], recv.at[1, step], to)
 
-        def finish(cond_ref, early, late):
+        def begin():
+            cond_ref, early, late = self.sources
             copies = [pltpu.make_async_copy(cond_ref, cond, local.at[4])]
             for b in range(2):
                 cut = pl.ds(2 * D, 4 * D)
@@ -1542,6 +1615,8 @@
                             pieces[col, to : to + 1, :] = grads[b, r : r + 1, here : here + STRIP]
             for step in range(1, 4):
                 along(step).start()
+
+        def finish():
             value = pieces[n]
             for step in range(1, 4):
                 along(step).wait_recv()
@@ -1566,8 +1641,161 @@
             for step in range(1, 8):
                 across(step).wait_send()
 
-        self.finish = finish
-        return ()
+        return begin, finish
+
+
+TILES = 32
+JOINT_TILES = 18
+
+
+def thirds(value):
+    high = value.astype(LOW)
+    rest = value - high.astype(FULL)
+    middle = rest.astype(LOW)
+    return high, middle, (rest - middle.astype(FULL)).astype(LOW)
+
+
+def gathered_by(value, pattern):
+    first = half_mask()
+    zero = jnp.zeros_like(value)
+    both = jnp.concatenate([jnp.where(first, value, zero), jnp.where(first, zero, value)], axis=0)
+    parts = [nn(part, pattern) for part in thirds(both)]
+    return parts[0] + (parts[1] + parts[2])
+
+
+class BiasBack:
+    takes = 2
+
+    def __init__(self):
+        self.out_shape = [shape((TILES, 8, 256), FULL)]
+        self.out_specs = [pl.BlockSpec(memory_space=pltpu.VMEM)]
+        gaps = HEADS // 2 * (2 * TW - 1)
+        self.scratch = [
+            pltpu.VMEM((CHUNK, gaps, 128), FULL),
+            pltpu.VMEM((2 * SW, 8, 2, SW, 128), FULL),
+            pltpu.VMEM((2 * gaps, 256), FULL),
+            pltpu.VMEM((2, 8, 2 * SW, 256), FULL),
+            pltpu.VMEM((TILES, 8, 256), FULL),
+            pltpu.VMEM((8, 4, 8, 256), FULL),
+            pltpu.VMEM((4, 4, 8, 256), FULL),
+            DMA((CHUNK + 2 * SW,)),
+            DMA((3, 8)),
+            DMA((3, 8)),
+        ]
+
+    def steps(self, ins, outs, scratch):
+        at = Place()
+        w, n = at.w, at.n
+        joint_grad, space_grad = ins
+        (result,) = outs
+        joint_rows, space_rows, joint_sum, space_sum, tiles, groups, line, local, send, recv = scratch
+        query = lax.broadcasted_iota(jnp.int32, (128, 256), 0) % CHUNK
+        column = lax.broadcasted_iota(jnp.int32, (128, 256), 1)
+
+        def load(k):
+            if k < CHUNK:
+                return pltpu.make_async_copy(joint_grad.at[:, k, :], joint_rows.at[k], local.at[k])
+            k -= CHUNK
+            src = space_grad.at[:, :, k // SW, :, k % SW, :]
+            return pltpu.make_async_copy(src, space_rows.at[k], local.at[CHUNK + k])
+
+        def start():
+            joint_sum[...] = jnp.zeros_like(joint_sum)
+            space_sum[...] = jnp.zeros_like(space_sum)
+            tiles[...] = jnp.zeros_like(tiles)
+            for k in range(CHUNK + 2 * SW):
+                load(k).start()
+
+        def joint_part(part):
+            for k in range(part * SW, (part + 1) * SW):
+                load(k).wait()
+
+            @pl.loop(0, SW)
+            def _(col):
+                to = (query // SW - part + SW - 1) * SPAN_T + query % SW - col + SW - 1
+                pattern = jnp.where(column == to, 1.0, 0.0).astype(LOW)
+                joint_sum[...] += gathered_by(joint_rows[part * SW + col], pattern)
+
+        def space_part(part):
+            for k in range(CHUNK + part * 4, CHUNK + part * 4 + 4):
+                load(k).wait()
+
+            @pl.loop(0, 4)
+            def _(i):
+                col = part * 4 + i
+                to = query // SW * SPAN_S + lax.rem(n, 2) * SW + query % SW - col + 2 * SW - 1
+                pattern = jnp.where(column == to, 1.0, 0.0).astype(LOW)
+                value = gathered_by(space_rows[col].reshape(128, 128), pattern)
+                space_sum[...] += value.reshape(2, 8, 2 * SW, 256)
+
+        def across(stage, step, src, dst):
+            to = (lax.bitwise_xor(w, step), n)
+            return remote(src, dst, send.at[stage, step], recv.at[stage, step], to)
+
+        def first(step):
+            src = tiles.at[span(lax.bitwise_xor(w, step), 4)]
+            return across(0, step, src, groups.at[w])
+
+        def second(step):
+            to = (w, lax.bitwise_xor(n, step))
+            return remote(line.at[n], line.at[n], send.at[1, step], recv.at[1, step], to)
+
+        def third(step):
+            here = result.at[span(w, 4)]
+            return across(2, step, here, here)
+
+        def settle():
+            for t in range(JOINT_TILES):
+                tiles[t] = joint_sum[t * 8 : (t + 1) * 8, :]
+            for half in range(2):
+                total = jnp.zeros((8, 1024), FULL)
+                for row in range(2 * SW):
+                    here = space_sum[half, :, row, :]
+                    here = jnp.concatenate([here, jnp.zeros((8, 768), FULL)], axis=1)
+                    total = total + pltpu.roll(here, (2 * SW - 1 - row) * SPAN_S, 1)
+                moved = pltpu.roll(total, SW * SPAN_S, 1)
+                total = jnp.where(n >= 2, moved, total)
+                for q in range(4):
+                    tiles[JOINT_TILES + half * 4 + q] = total[:, q * 256 : (q + 1) * 256]
+            for step in range(1, 8):
+                first(step).start()
+
+        def sum_groups():
+            value = tiles[span(w, 4)]
+            for step in range(1, 8):
+                first(step).wait_recv()
+                value = value + groups[lax.bitwise_xor(w, step)]
+            line[n] = value
+            for step in range(1, 4):
+                second(step).start()
+
+        def sum_line():
+            for step in range(1, 4):
+                second(step).wait_recv()
+            result[span(w, 4)] = (line[0] + line[1]) + (line[2] + line[3])
+            for step in range(1, 8):
+                third(step).start()
+
+        def done():
+            for step in range(1, 8):
+                third(step).wait_recv()
+            for step in range(1, 8):
+                first(step).wait_send()
+                third(step).wait_send()
+            for step in range(1, 4):
+                second(step).wait_send()
+
+        made = [start] + [functools.partial(joint_part, p) for p in range(SW)]
+        made += [functools.partial(space_part, p) for p in range(4)]
+        return made + [settle, sum_groups, sum_line, done]
+
+
+def bias_tables(tiles):
+    gaps = 2 * TW - 1
+    joint = tiles[:JOINT_TILES].reshape(2, HEADS // 2, gaps, 256)[..., : SPAN_T**2]
+    space = tiles[JOINT_TILES : JOINT_TILES + 8].reshape(2, 4, 8, 256)
+    space = space.transpose(2, 0, 1, 3).reshape(HEADS, 1024)[:, : SPAN_S**2]
+    return space, joint.transpose(1, 0, 2, 3).reshape(HEADS, -1)
 
 
 FORWARD_ENDS = (
@@ -1585,7 +1813,7 @@
 )
 FORWARD_MIDDLES = (
     0, 13, 125, 1, 2, 4, 104, 26, 126, 14, 15, 109, 17, 3, 5, 106, 39, 127, 6, 114, 107, 119, 8,
-    111, 28, 16, 128, 30, 116, 18, 19, 21, 112, 121, 7, 108, 10, 9, 27, 41, 65, 43, 40, 23, 117,
+    111, 28, 16, 30, 128, 116, 18, 19, 21, 112, 121, 7, 108, 10, 9, 27, 41, 65, 43, 40, 23, 117,
     32, 11, 20, 12, 122, 52, 34, 22, 113, 66, 31, 118, 45, 69, 123, 36, 124, 24, 47, 25, 53, 29,
     105, 129, 110, 115, 120, 67, 44, 91, -1, 56, -1, 42, 49, 70, -1, -1, -1, 54, 78, 68, 35, -1,
     73, -1, -1, 55, -1, 57, -1, -1, -1, -1, 93, -1, 33, -1, 71, -1, -1, 80, -1, -1, 48, -1, -1, -1,
@@ -1615,26 +1843,22 @@
     -1, 64, -1, -1, -1, 65, -1, 66, -1, -1, -1, 67, -1, -1, -1, -1, -1, -1, -1, -1, -1, -1,
 )
 BACK_SPACE_ENDS = (
-    0, -1, 1, 2, 3, 4, 5, -1, -1, -1, -1, -1, 6, 7, 17, -1, 18, 8, 19, 9, 20, 10, 21, 11, 22, 12,
-    -1, -1, 13, -1, -1, -1, -1, -1, -1, -1, -1, -1, 14, 23, 24, 34, 35, 36, 15, 37, 38, 39, -1, -1,
-    -1, -1, 25, 26, 27, 28, 29, -1, -1, -1, -1, -1, -1, 30, 16, -1, -1, -1, -1, -1, -1, -1, 40, 31,
-    41, 42, 43, 44, 45, 46, -1, -1, -1, -1, -1, 32, -1, -1, -1, -1, -1, 47, -1, 48, -1, 33, 49, -1,
-    -1, -1, -1, -1, -1, 50, -1,
+    0, -1, 1, 2, 3, 4, 5, -1, -1, -1, -1, -1, 6, 7, -1, -1, -1, -1, 8, 9, 10, 11, 17, 12, 18, 13,
+    19, 20, 21, -1, 22, -1, -1, 14, -1, -1, -1, -1, -1, 15, -1, -1, -1, -1, -1, -1, -1, 23, 16, 24,
+    -1, 68, 69, 70, 71, 25, 26, 27, 28, 34, 29, 35, 30, 36, 37, 38, 39, -1, 31, -1, 72, 73, 74, 75,
+    32, -1, -1, 76, 77, 78, 79, 40, 41, 42, 43, 44, 45, 46, -1, 47, 48, 49, -1, 80, 81, -1, -1, -1,
+    82, -1, -1, -1, -1, -1, 83, 84, -1, -1, -1, 33, -1, 51, 87, 52, 88, 53, 89, 54, 90, 55, 91, 56,
+    92, 57, 93, 58, 94, 59, 95, 60, 96, 61, 97, 62, 98, 63, 99, 64, 100, 65, 101, 66, -1, 50, 102,
+    85, 103, 86, 67,
 )
 BACK_SPACE_MIDDLES = (
-    0, -1, 1, 2, 3, 4, 5, -1, -1, -1, -1, -1, 6, 7, 17, -1, 18, 8, 19, 9, 20, 10, 21, 11, 22, 12,
-    -1, -1, -1, -1, -1, -1, -1, -1, 13, -1, -1, -1, 23, 24, 34, 35, 36, 37, 38, 39, -1, -1, 14, 15,
-    -1, -1, 25, 26, 27, 28, 29, -1, -1, -1, -1, -1, -1, 16, -1, -1, -1, -1, -1, -1, -1, 30, 40, 41,
-    42, 43, 44, 45, 46, -1, -1, -1, -1, -1, 31, 32, -1, -1, -1, -1, -1, -1, -1, 33, -1, 47, -1, 48,
-    -1, 49, -1, 50, -1, -1, -1,
-)
-LAST_ENDS = (
-    0, 17, 18, 19, 20, 21, 22, 23, 24, 25, 26, 27, 28, 1, 2, 3, 4, 5, 6, 7, 8, 9, 10, 11, 12, 13,
-    29, 14, 30, 15, 31, 32, 33, -1, -1, 16,
-)
-LAST_MIDDLES = (
-    0, 1, 2, 3, 4, 5, 6, 7, 17, 8, 9, 10, 11, 12, 18, 25, 19, 26, 20, 27, 21, 28, 22, 23, 24, 29,
-    30, 31, 32, 33, -1, 13, -1, 14, 15, 16,
+    0, -1, 1, 2, 3, 4, 5, -1, -1, -1, -1, -1, 6, 7, -1, -1, -1, -1, 8, 9, 10, 11, 17, 12, 18, -1,
+    19, 20, 21, 22, -1, -1, -1, -1, 13, -1, -1, -1, -1, 14, -1, -1, 15, -1, -1, -1, -1, 16, 23, 24,
+    -1, 25, 26, 27, 28, 34, 29, 35, 36, 37, 38, 39, -1, 68, -1, -1, -1, 69, -1, 76, 70, -1, 40, 77,
+    41, 42, 43, 44, 45, 46, 71, -1, 78, -1, 30, -1, -1, -1, -1, 79, 31, -1, -1, -1, 32, -1, 72, -1,
+    -1, 51, 87, 73, 52, 74, 88, 53, 75, 89, 54, 90, 55, 33, 91, 56, 92, 57, 80, 93, 58, 94, 59, 81,
+    95, 60, 96, 61, 82, 97, 62, 98, 63, 83, 99, 47, 84, 100, 48, 101, 49, -1, 50, 64, 102, 85, 65,
+    103, 66, 86, 67,
 )
 
 
@@ -1658,6 +1882,7 @@
 
 
 def joint_table_back(grad):
+    grad = grad.reshape(HEADS // 2, 2 * TW - 1, CHUNK, 2 * CHUNK)
     pairs = jnp.stack([grad[..., :CHUNK], grad[..., CHUNK:]], axis=1)
     flat = pairs.reshape(HEADS * (2 * TW - 1), CHUNK * CHUNK)
     return exact(flat, joint_pattern(), ((1,), (1,))).reshape(HEADS, -1)
@@ -1836,6 +2061,11 @@
             (S.first, S.project, S.to_queries, S.to_pairs),
             (S.to_project, A.to_first),
         ),
+        S.weight_back: (
+            space_weight_back(),
+            (S.first, S.to_queries, S.to_pairs),
+            (S.to_project,),
+        ),
         A.finish: (
             finish(),
             (S.rows, S.mods, A.own_first, S.to_middle),
@@ -1850,13 +2080,14 @@
         values.update(zip(gives, phase(*[values[k] for k in takes])))
 
 
-def together(values, plan, tables, engine, moved, brought, name, more=(), final=None):
+def together(values, plan, tables, engine, moved, brought, name, more=(), prepare=None, inline={}):
     table = stages()
     outs, args = {}, {}
-    for phase_name in plan:
+    steps = [k for k in plan if k not in inline]
+    for phase_name in steps:
         phase, takes, gives = table[phase_name]
         outs.update(zip(gives, phase.out_shape))
-    for phase_name in plan:
+    for phase_name in steps:
         for k in table[phase_name][1]:
             if k not in outs and k not in brought:
                 args[k] = values[k]
@@ -1866,15 +2097,17 @@
 
     def script(refs, engine_outs, feed):
         refs.update(zip(brought, engine_outs))
+        if prepare is not None:
+            prepare(refs)
         feed.follow(tables)
         feed.enter()
         for phase_name in plan:
+            if phase_name in inline:
+                feed.do(feed.slot)
+                inline[phase_name](refs, feed)
+                continue
             phase, takes, gives = table[phase_name]
             phase.inside(feed.over(phase), [refs[k] for k in takes], [refs[k] for k in gives])
-        if final is not None:
-            feed.do(feed.slot)
-            feed.slot += 1
-            final(refs)
         feed.rest()
 
     made, arrived = fused(script, args, outs, engine, moved, name)
@@ -1942,29 +2175,31 @@
         engine = Scatter(shapes, False, 1)
         tables = BACK_JOINT_ENDS, BACK_JOINT_MIDDLES
         together(values, BACK_JOINT, tables, engine, partials_of(J), grads_of(J), "back_joint")
-        engine = Scatter(shapes[:3], False, 2)
-        tables = BACK_SPACE_ENDS, BACK_SPACE_MIDDLES
-        takes, gives = partials_of(S)[:3], grads_of(S)[:3]
-        together(values, BACK_SPACE, tables, engine, takes, gives, "back_space")
         back = ModulationBack()
-        late = (A.cond, S.late, J.early, J.late)
-
-        def final(refs):
+        engine = Scatter(shapes, True, 2)
+
+        def first_back(refs, feed):
+            takes = refs[S.project], refs[S.to_queries], refs[S.to_pairs]
+            space_first_back(feed, 8, Place().order, *takes, engine.line_held)
+
+        def prepare(refs):
             early = refs[S.early], refs[J.early]
-            back.finish(refs[A.cond], early, (refs[S.late], refs[J.late]))
+            back.sources = refs[A.cond], early, (refs[S.late], refs[J.late])
 
         together(
             values,
-            LAST,
-            (LAST_ENDS, LAST_MIDDLES),
-            Joined(Scatter(shapes[3:], True, 3), back),
-            (S.to_project, A.to_first),
-            (S.grad_project, A.own_first, S.modulate, J.modulate),
-            "last_sums",
-            late,
-            final,
+            BACK_SPACE,
+            (BACK_SPACE_ENDS, BACK_SPACE_MIDDLES),
+            Joined(Joined(engine, back), BiasBack()),
+            partials_of(S) + (J.to_table, S.to_table),
+            grads_of(S) + (A.own_first, S.modulate, J.modulate, A.bias),
+            "back_space",
+            (A.cond, S.late, J.early, J.late, S.project),
+            prepare,
+            {A.first_back: first_back},
         )
         modulate = values[S.modulate], values[J.modulate]
+        bias = bias_tables(values[A.bias])
     else:
         image_all = lax.all_gather(low_images, "wide", axis=0, tiled=True)
         cond = jnp.stack([jnp.repeat(low_clips, 4, axis=0), image_all], axis=1)
@@ -1974,7 +2209,7 @@
         values.update(zip(weights[:4], gather_flat(space_shards)))
         values.update(zip(weights[4:], gather_flat(joint_shards)))
         values[A.all_rows] = lax.all_gather(tokens, "narrow", axis=0, tiled=True)
-        apart(values, FORWARD + BACK_JOINT + BACK_SPACE)
+        apart(values, FORWARD + BACK_JOINT + (S.attend_back, S.project_back))
         for b in (J, S):
             values.update(zip(grads_of(b), scatter_plain([values[k] for k in partials_of(b)])))
         values[A.own_first] = lax.psum_scatter(
@@ -1985,18 +2220,11 @@
             jnp.concatenate([values[b.early], values[b.late][:, 2 * D :]], axis=1) for b in (S, J)
         ]
         modulate = modulation_grads(cond, jnp.stack(both), rows)
-    bias = lax.psum(
-        jnp.concatenate(
-            [
-                space_table_back(values[S.to_table], narrow),
-                joint_table_back(values[J.to_table]),
-            ],
-            axis=1,
-        ),
-        ("wide", "narrow"),
-    )
-    split = space_bias.shape[1]
-    bias = (bias[:, :split], bias[:, split:])
+        space_grad = space_table_back(values[S.to_table], narrow)
+        grads = jnp.concatenate([space_grad, joint_table_back(values[J.to_table])], axis=1)
+        bias = lax.psum(grads, ("wide", "narrow"))
+        split = space_bias.shape[1]
+        bias = bias[:, :split], bias[:, split:]
     outs = [values[A.output_tokens], values[A.grad_tokens]]
     for i, b in enumerate((S, J)):
         outs += [modulate[i]] + [values[k] for k in reversed(grads_of(b))] + [bias[i]]
@@ -2005,8 +2233,7 @@
 
 FORWARD = S.triple, S.attend, S.mlp, J.triple, J.attend, J.mlp
 BACK_JOINT = J.mlp_back, J.attend_back, J.project_back, S.mlp_back
-BACK_SPACE = S.attend_back, S.project_back
-LAST = (A.finish,)
+BACK_SPACE = S.attend_back, A.first_back, S.weight_back, A.finish
 
 
 def solution(mesh):

time: 814 us -> 735 us (0.903)
  Pallas kernels: 713 us -> 684 us
  local copies, waits for them, and re-layouts: 52.6 us -> 33 us
  between operations: 15.4 us -> 1.81 us
  waiting for transfers between devices: 10.5 us -> 0 us
    pallas_call x4 -> x3, Pallas kernels: 713 us -> 684 us  [fused(): pl.pallas_call(kernel, in_specs=in_specs, out_specs=[pl.BlockSpec(memory_...]
    psum x1 -> x0, waiting for transfers between devices: 10.5 us -> none  [body(): lax.psum(jnp.concatenate([space_table_back(values[S.to_table], narrow), j...]
  transfers between devices with their start and end apart: 1 -> 0, of which waited for: 1 -> 0; matrix products, arithmetic and copies ran while one was open for 0% -> 0% of each run, Pallas kernels for 14% -> 0%
where the time goes in v3:
time: 735 us; the launch traced here: 726 us
  Pallas kernels  684 us (93%)
  local copies, waits for them, and re-layouts  33 us (4%)
    pallas_call x3, Pallas kernels, fused(): pl.pallas_call(kernel, in_specs=in_specs, out_specs=[pl.BlockSpec(memory_...  684 us

profile of v3, /device:TPU:0, one launch (start us, length us, event | category | flops | bytes accessed | tf_op | source)
XLA Modules:
  0.0 725.5 jit_solution(7482779361442035746)
XLA Ops:
  1.3 0.7 convert_convert_fusion
  2.1 0.1 add.74
  2.1 0.7 convert_element_type.24
  2.8 0.6 pad_convert_fusion.refs_13_
  3.4 0.6 broadcast_in_dim.24.refs_12_
  4.1 1.0 reshape.135
  5.1 0.2 iota_compare_fusion.2
  5.3 1.1 reshape.133
  6.9 0.5 reshape.144
  7.4 1.0 convolution_bitcast_fusion.1
  8.5 1.6 copy.37
  10.1 0.0 copy-start.12
  10.1 2.1 reshape.134.refs_0_.refs_2_
  12.2 0.0 copy-done.12
  12.2 1.8 convolution_bitcast_fusion
  14.0 3.6 reshape.136
  17.6 3.1 slice_bitcast_fusion.1
  20.7 2.1 pad_maximum_fusion.refs_3_.refs_14_
  22.8 318.5 %forward.1 = (bf16[2304,1024]{1,0:T(8,128)(2,1)}, bf16[576,1024]{1,0:T(8,128)(2,1)}, bf16[4,576,2048]{2,1,0:T(8,128)(2,1)}, bf16[576,1024]{1,0:T(8,128)(2,1)}, b...) custom-call(f32[8,256,128]{2,1,0:T(8,128)} %reshape.134.refs_0_.refs, ...), custom_call_target="tpu_custom_call" | custom-call | flops 99999997952 | tf_op jit(solution)/shard_map/forward/pallas_call | solution.py:1414
  341.3 182.6 %back_joint.1 = (bf16[4096,1024]{1,0:T(8,128)(2,1)}, bf16[1024,4096]{1,0:T(8,128)(2,1)}, bf16[1024,1024]{1,0:T(8,128)(2,1)}, f32[576,1024]{1,0:T(8,128)}, bf16[5...) custom-call(f32[1]{0:T(128)S(6)} %convert_element_type.21.refs_1_.re, ...), custom_call_target="tpu_custom_call" | custom-call | flops 99999997952 | tf_op jit(solution)/shard_map/back_joint/pallas_call | solution.py:1414
  524.0 182.4 %back_space.1 = (bf16[576,1024]{1,0:T(8,128)(2,1)}, bf16[2,4,576,1024]{3,2,1,0:T(8,128)(2,1)}, f32[8,2,2,8,8,128]{5,4,3,2,1,0:T(8,128)}, bf16[1024,3072]{1,0:T(8...) custom-call(bf16[576,1024]{1,0:T(8,128)(2,1)} %get-tuple-element.68., ...), custom_call_target="tpu_custom_call" | custom-call | flops 99999997952 | tf_op jit(solution)/shard_map/back_space/pallas_call | solution.py:1414
  706.4 0.0 copy-start.1
  706.4 0.9 slice.84
  707.3 0.0 copy-start
  707.4 1.7 slice.86
  709.1 0.6 copy.50
  709.8 1.6 reshape.139
  711.4 1.0 slice_bitcast_fusion.2
  712.4 0.7 copy.41
  713.1 1.7 reshape.140
  714.8 0.0 copy-done.1
  714.8 1.0 copy.83
  715.8 0.0 copy-done
  715.8 0.0 copy-start.3
  715.8 0.0 copy-start.9
  715.8 1.4 copy.84
  717.3 0.3 copy-done.3
  717.5 0.0 copy-start.11
  717.5 0.0 copy-start.7
  717.5 0.0 copy-start.6
  717.5 0.0 copy-start.2
  717.5 0.9 copy.85
  718.4 0.0 copy-done.9
  718.4 0.0 copy-start.8
  718.4 0.7 copy.86
  719.2 0.0 copy-done.11
  719.2 0.0 copy-start.10
  719.2 0.7 copy.87
  719.8 0.0 copy-done.7
  719.8 0.0 copy-start.5
  719.8 0.8 copy.88
  720.6 0.0 copy-done.6
  720.6 0.0 copy-start.4
  720.6 0.8 copy.89
  721.4 0.0 copy-done.2
  721.4 0.9 copy.90
  722.3 0.0 copy-done.8
  722.3 0.7 copy.91
  723.1 0.0 copy-done.10
  723.1 0.7 copy.92
  723.7 0.0 copy-done.5
  723.7 0.8 copy.93
  724.5 0.0 copy-done.4
  724.5 0.8 copy.94
  (20 shorter events, 0.4 us)
Async XLA Ops:
  10.1 2.1 copy-start.12
  706.4 8.4 %copy-start.1 = (bf16[576,1024]{1,0:T(8,128)(2,1)S(1)}, bf16[576,1024]{1,0:T(8,128)(2,1)}, u32[]{:S(2)}) copy-start(bf16[576,1024]{1,0:T(8,128)(2,1)} %get-tuple-element.138) | copy-start | bytes 3538948
  707.3 8.5 %copy-start = (f32[576,1024]{1,0:T(8,128)S(1)}, f32[576,1024]{1,0:T(8,128)}, u32[]{:S(2)}) copy-start(f32[576,1024]{1,0:T(8,128)} %get-tuple-element.139) | copy-start | bytes 7077892
  715.8 1.7 copy-start.3
  715.8 2.6 copy-start.9
  717.5 1.6 copy-start.11
  717.5 2.3 copy-start.7
  717.5 3.1 copy-start.6
  717.5 3.9 copy-start.2
  718.4 3.9 copy-start.8
  719.2 3.9 copy-start.10
  719.8 3.9 copy-start.5
  720.6 3.9 copy-start.4

commit v4 on v3

--- a/solution.py
+++ b/solution.py
@@ -220,6 +220,71 @@
         ],
         name="space_triple",
         ticks=4,
+    )
+
+
+def space_triple_parts(feed, ticks, order, own_rows, all_rows, mods, weight, first, queries, pairs):
+    tile = 512
+    slot = feed.slot
+    feed.slot += ticks
+
+    def scoped(weights, modulation, rows, normed, made, sems):
+        loads = [
+            pltpu.make_async_copy(weight, weights, sems.at[0]),
+            pltpu.make_async_copy(mods, modulation, sems.at[1]),
+        ]
+        for load in loads:
+            load.start()
+        stores = []
+        at_slot = slot
+        for j in range(4):
+            side = j % 2
+            here = span(order[j], ROWS_DEV)
+            if j:
+                feed.do(at_slot)
+            source = all_rows.at[here] if j else own_rows
+            fetch = pltpu.make_async_copy(source, rows.at[side], sems.at[2 + j])
+            fetch.start()
+            if j == 0:
+                for load in loads:
+                    load.wait()
+            if j >= 2:
+                for store in stores[j - 2]:
+                    store.wait()
+            fetch.wait()
+
+            def chunk(at, seq):
+                unit, _ = normalise(rows[side, at, :].astype(FULL))
+                value = unit * (1.0 + modulation[seq, part(1)]) + modulation[seq, part(0)]
+                normed[side, at, :] = value.astype(LOW)
+
+            each_chunk(chunk)
+            stores.append([pltpu.make_async_copy(normed.at[side], first.at[here], sems.at[6 + j])])
+            stores[j][0].start()
+            for t in range(2 if j else 0, 3 * D // tile):
+                if t > (2 if j else 0):
+                    feed.do(at_slot)
+                at_slot += 1
+                columns = slice(t * tile, (t + 1) * tile)
+                made[side, :, columns] = nn(normed[side], weights[:, columns]).astype(LOW)
+            out = made.at[side, :, pl.ds(D, 2 * D)]
+            stores[j].append(pltpu.make_async_copy(out, pairs.at[order[j]], sems.at[10 + j]))
+            if j == 0:
+                out = made.at[0, :, pl.ds(0, D)]
+                stores[j].append(pltpu.make_async_copy(out, queries, sems.at[14]))
+            for store in stores[j][1:]:
+                store.start()
+        for store in stores[2] + stores[3]:
+            store.wait()
+
+    pl.run_scoped(
+        scoped,
+        pltpu.VMEM((D, 3 * D), LOW),
+        pltpu.VMEM((2, 6 * D), FULL),
+        pltpu.VMEM((2, ROWS_DEV, D), LOW),
+        pltpu.VMEM((2, ROWS_DEV, D), LOW),
+        pltpu.VMEM((2, ROWS_DEV, 3 * D), LOW),
+        pltpu.SemaphoreType.DMA((15,)),
     )
 
 
@@ -996,8 +1061,8 @@
             DMA((count, 2, 4)),
             DMA((count, 2, 4)),
             DMA((count, 2, 4)),
-            DMA((count, 4, 4)),
-            DMA((count, 4, 4)),
+            DMA((count, 4)),
+            DMA((count, 4)),
             DMA((count,)),
         ]
         self.scratch += [DMA((PIECES, 5)), DMA((PIECES, 4)), DMA((PIECES,))] * lines
@@ -1024,9 +1089,10 @@
             sems = y_send.at[k, far, col], y_recv.at[k, far, col]
             return remote(src, block(k, row, col), *sems, (at.y, n))
 
-        def c_copy(k, src, row, chip, col):
-            sems = c_send.at[k, chip, col], c_recv.at[k, chip, col]
-            return remote(src, block(k, row, col), *sems, (at.c, n))
+        def c_copy(k, chip):
+            row = (w, at.x, at.y, at.d)[chip]
+            here = fulls[k].at[span(row, shapes[k][0])]
+            return remote(here, here, c_send.at[k, chip], c_recv.at[k, chip], (at.c, n))
 
         def own_copy(k):
             return pltpu.make_async_copy(shards[k], block(k, w, n), own_sem.at[k])
@@ -1042,7 +1108,6 @@
 
             x_copy(k, shards[k], w, 0, n).start()
             y_copy(k, shards[k], w, 0, n).start()
-            c_copy(k, shards[k], w, 0, n).start()
             own_copy(k).start()
 
         def z_stage(k, j):
@@ -1056,7 +1121,6 @@
 
             x_copy(k, here, w, 0, col).start()
             y_copy(k, here, w, 0, col).start()
-            c_copy(k, here, w, 0, col).start()
 
         def near_stage(k, j):
             col = at.order[j]
@@ -1065,23 +1129,26 @@
             x_copy(k, from_x, at.x, 0, col).wait_recv()
             if j < 2:
                 y_copy(k, from_x, at.x, 1, col).start()
-            c_copy(k, from_x, at.x, 1, col).start()
             y_copy(k, from_y, at.y, 0, col).wait_recv()
             if j >= 2:
                 x_copy(k, from_y, at.y, 1, col).start()
-            c_copy(k, from_y, at.y, 2, col).start()
 
         def far_stage(k, j):
             col = at.order[j]
             far = block(k, at.d, col)
             (y_copy if j < 2 else x_copy)(k, far, at.d, 1, col).wait_recv()
-            c_copy(k, far, at.d, 3, col).start()
+
+        def rows_on(k):
+            own_copy(k).wait()
+            for chip in range(3):
+                c_copy(k, chip).start()
+
+        def far_on(k):
+            c_copy(k, 3).start()
 
         def ready(k):
-            own_copy(k).wait()
-            for col in range(4):
-                for chip in range(4):
-                    c_copy(k, block(k, w, col), w, chip, col).wait_recv()
+            for chip in range(4):
+                c_copy(k, chip).wait_recv()
 
         def drain(k):
             for j in range(4):
@@ -1095,8 +1162,8 @@
                 x_copy(k, here, w, 0, col).wait_send()
                 y_copy(k, here, w, 0, col).wait_send()
                 (y_copy if j < 2 else x_copy)(k, here, w, 1, col).wait_send()
-                for chip in range(4):
-                    c_copy(k, here, w, chip, col).wait_send()
+            for chip in range(4):
+                c_copy(k, chip).wait_send()
 
             @pl.when(n > 0)
             def _():
@@ -1165,6 +1232,8 @@
                 items.add(near_stage, k, j)
             for j in range(4):
                 items.add(far_stage, k, j)
+            items.add(rows_on, k)
+            items.add(far_on, k)
             items.add(ready, k)
             items.drain(drain, k)
         if self.line:
@@ -1799,30 +1868,30 @@
 
 
 FORWARD_ENDS = (
-    0, 13, 125, 1, 4, 104, 109, 114, 119, 14, 17, 5, 2, 26, 126, 8, 18, 27, 21, 15, 39, 127, 9, 3,
-    6, 40, 30, 22, 107, 31, 28, 19, 16, 128, 10, 43, 112, 7, 108, 44, 23, 41, 65, 66, 34, 11, 12,
-    35, 117, 32, 122, 52, 20, 53, 36, 47, 113, 24, 48, 25, 118, 45, 69, 70, 123, 49, 56, 57, 29,
-    105, 110, 115, 120, 129, 73, 74, 106, 60, 61, 111, 33, 116, 37, 121, 124, -1, 38, 67, 91, -1,
-    -1, 71, 92, -1, -1, -1, -1, -1, 95, 42, 75, -1, -1, -1, 54, 78, -1, 96, -1, -1, -1, 79, -1, 99,
-    68, -1, -1, -1, 55, -1, 46, -1, -1, -1, 58, 93, -1, -1, -1, -1, -1, -1, -1, -1, 82, 80, -1, -1,
-    -1, -1, -1, -1, -1, -1, -1, -1, 100, 94, -1, -1, -1, -1, -1, -1, -1, 83, 81, 50, 72, 51, -1,
-    62, 59, -1, -1, 97, -1, -1, -1, 86, -1, -1, -1, 84, -1, -1, -1, 98, -1, 76, -1, 77, -1, 63, 87,
-    -1, 64, -1, 101, 85, -1, -1, 88, -1, -1, -1, 102, -1, -1, 103, -1, -1, -1, -1, 89, -1, -1, -1,
-    90, -1, -1, -1, -1, -1, -1, -1, -1, -1, -1, -1, -1, -1, -1, -1, -1, -1, -1, -1, -1, -1, -1, -1,
-    -1, -1, -1, -1, -1, -1, -1, -1,
+    0, 15, 30, 141, 1, 4, 16, 19, 31, 34, 121, 126, 131, 136, 2, 5, 45, 142, 8, 46, 20, 17, 23,
+    120, 143, 125, 130, 135, 32, 35, 75, 3, 38, 6, 122, 76, 9, 127, 49, 132, 50, 10, 24, 21, 137,
+    60, 25, 36, 47, 90, 39, 79, 91, 40, 18, 144, 7, 12, 80, 33, 145, 77, 53, 92, 54, 48, 64, 11,
+    13, 14, -1, 51, 123, -1, 61, -1, 94, 83, -1, -1, -1, -1, 128, 95, -1, 22, 27, 84, -1, -1, 133,
+    55, 37, 42, 81, 138, -1, -1, 26, 28, -1, 96, 29, -1, 124, 41, 43, 85, 52, 57, 44, 129, 68, 100,
+    65, 134, 56, 58, 98, 59, 139, 140, -1, -1, -1, 62, 99, 105, -1, -1, -1, 69, -1, -1, 106, -1,
+    -1, 78, -1, -1, -1, 66, -1, -1, -1, -1, 63, -1, -1, -1, -1, -1, -1, 109, -1, -1, -1, -1, 93,
+    -1, -1, 110, 82, 87, 107, 70, -1, -1, -1, 67, 108, 72, -1, 113, -1, -1, 86, 88, -1, 89, 97,
+    102, -1, -1, -1, 114, -1, 71, 73, -1, -1, 74, 111, -1, -1, -1, 112, 101, 117, 103, -1, -1, 115,
+    -1, -1, -1, 104, 116, 118, -1, -1, -1, -1, 119, -1, -1, -1, -1, -1, -1, -1, -1, -1, -1, -1, -1,
+    -1, -1, -1, -1, -1, -1, -1, -1, -1, -1, -1, -1, -1, -1, -1, -1, -1, -1, -1, -1, -1, -1, -1, -1,
 )
 FORWARD_MIDDLES = (
-    0, 13, 125, 1, 2, 4, 104, 26, 126, 14, 15, 109, 17, 3, 5, 106, 39, 127, 6, 114, 107, 119, 8,
-    111, 28, 16, 30, 128, 116, 18, 19, 21, 112, 121, 7, 108, 10, 9, 27, 41, 65, 43, 40, 23, 117,
-    32, 11, 20, 12, 122, 52, 34, 22, 113, 66, 31, 118, 45, 69, 123, 36, 124, 24, 47, 25, 53, 29,
-    105, 129, 110, 115, 120, 67, 44, 91, -1, 56, -1, 42, 49, 70, -1, -1, -1, 54, 78, 68, 35, -1,
-    73, -1, -1, 55, -1, 57, -1, -1, -1, -1, 93, -1, 33, -1, 71, -1, -1, 80, -1, -1, 48, -1, -1, -1,
-    -1, -1, 95, -1, -1, -1, -1, -1, -1, 60, -1, -1, -1, -1, -1, -1, -1, -1, -1, -1, -1, 46, -1, -1,
-    74, -1, -1, -1, -1, -1, 58, 37, 75, 82, 38, 92, 72, 59, 94, 61, 50, 51, -1, 79, 62, 97, -1, -1,
-    84, -1, 76, 81, -1, 77, 63, 99, -1, 64, -1, -1, 86, -1, -1, -1, 96, -1, -1, -1, 101, 98, -1,
-    -1, -1, 88, 83, -1, -1, 85, -1, -1, 102, 100, -1, 103, -1, -1, -1, -1, 89, 87, -1, -1, -1, 90,
+    0, 15, 30, 141, 1, 2, 4, 45, 142, 16, 17, 19, 31, 32, 34, 143, 3, 121, 5, 75, 126, 131, 136, 6,
+    47, 90, 18, 46, 120, 125, 130, 8, 135, 33, 144, 77, 49, 145, 20, 122, 21, 23, 92, 127, 35, 48,
+    132, 36, 123, 10, 38, 137, 60, 76, 128, 7, 12, 9, 133, 79, 61, 138, 51, 91, 94, 124, 22, 27,
+    25, 129, 50, 37, 42, 134, 81, 139, 140, 53, 40, 24, 62, 105, 78, 96, 63, 11, 13, 39, 14, -1,
+    93, -1, 52, 57, -1, 107, 55, -1, 64, -1, 80, -1, 83, -1, 26, 28, -1, 65, 29, -1, -1, -1, 41,
+    85, 95, 43, -1, -1, -1, 44, -1, 98, -1, -1, -1, 54, -1, -1, -1, -1, -1, -1, -1, 66, -1, -1,
+    100, -1, -1, -1, -1, -1, -1, -1, -1, -1, 109, -1, -1, 82, 87, -1, -1, -1, -1, 67, 72, 106, 56,
+    58, 97, 102, 59, -1, 108, 111, -1, -1, 70, 68, 86, 84, 88, -1, 89, -1, -1, 71, 69, 73, -1, -1,
+    74, -1, 99, -1, -1, -1, 101, 113, 103, -1, -1, 104, -1, 110, -1, -1, 115, 112, 117, -1, -1,
+    114, -1, -1, 116, 118, -1, -1, 119, -1, -1, -1, -1, -1, -1, -1, -1, -1, -1, -1, -1, -1, -1, -1,
     -1, -1, -1, -1, -1, -1, -1, -1, -1, -1, -1, -1, -1, -1, -1, -1, -1, -1, -1, -1, -1, -1, -1, -1,
-    -1, -1, -1, -1, -1, -1, -1, -1, -1,
 )
 BACK_JOINT_ENDS = (
     -1, -1, -1, -1, -1, -1, -1, -1, -1, -1, -1, -1, -1, -1, -1, -1, -1, -1, -1, -1, -1, -1, -1, -1,
@@ -2080,9 +2149,9 @@
         values.update(zip(gives, phase(*[values[k] for k in takes])))
 
 
-def together(values, plan, tables, engine, moved, brought, name, more=(), prepare=None, inline={}):
+def together(values, plan, tables, engine, moved, brought, name, more=(), prepare=None, inline={}, made={}):
     table = stages()
-    outs, args = {}, {}
+    outs, args = dict(made), {}
     steps = [k for k in plan if k not in inline]
     for phase_name in steps:
         phase, takes, gives = table[phase_name]
@@ -2110,8 +2179,8 @@
             phase.inside(feed.over(phase), [refs[k] for k in takes], [refs[k] for k in gives])
         feed.rest()
 
-    made, arrived = fused(script, args, outs, engine, moved, name)
-    values.update(made)
+    results, arrived = fused(script, args, outs, engine, moved, name)
+    values.update(results)
     values.update(zip(brought, arrived))
 
 
@@ -2161,6 +2230,13 @@
         values[S.own_modulate] = space_modulate
         values[J.own_modulate] = joint_modulate
         gather = Gather(shapes, True, 0)
+
+        def triple(refs, feed):
+            takes = refs[S.rows], refs[A.all_rows], refs[S.mods], refs[S.project]
+            gives = refs[S.first], refs[S.queries], refs[S.pairs]
+            space_triple_parts(feed, 18, Place().order, *takes, *gives)
+
+        whole_triple = stages()[S.triple]
         together(
             values,
             FORWARD,
@@ -2169,6 +2245,8 @@
             moved + (S.rows, A.images, A.clips, S.own_modulate, J.own_modulate),
             weights + (A.all_rows, S.mods, J.mods, A.cond),
             "forward",
+            inline={A.triple: triple},
+            made=dict(zip(whole_triple[2], whole_triple[0].out_shape)),
         )
         project_shape, output_shape, expand_shape, shrink_shape = shapes[:4]
         shapes = [shrink_shape, expand_shape, output_shape, project_shape]
@@ -2209,7 +2287,7 @@
         values.update(zip(weights[:4], gather_flat(space_shards)))
         values.update(zip(weights[4:], gather_flat(joint_shards)))
         values[A.all_rows] = lax.all_gather(tokens, "narrow", axis=0, tiled=True)
-        apart(values, FORWARD + BACK_JOINT + (S.attend_back, S.project_back))
+        apart(values, (S.triple,) + FORWARD[1:] + BACK_JOINT + (S.attend_back, S.project_back))
         for b in (J, S):
             values.update(zip(grads_of(b), scatter_plain([values[k] for k in partials_of(b)])))
         values[A.own_first] = lax.psum_scatter(
@@ -2231,7 +2309,7 @@
     return tuple(outs)
 
 
-FORWARD = S.triple, S.attend, S.mlp, J.triple, J.attend, J.mlp
+FORWARD = A.triple, S.attend, S.mlp, J.triple, J.attend, J.mlp
 BACK_JOINT = J.mlp_back, J.attend_back, J.project_back, S.mlp_back
 BACK_SPACE = S.attend_back, A.first_back, S.weight_back, A.finish
 

time: 735 us -> 707 us (0.962)
  Pallas kernels: 684 us -> 656 us
    pallas_call x3, Pallas kernels: 684 us -> 656 us  [fused(): pl.pallas_call(kernel, in_specs=in_specs, out_specs=[pl.BlockSpec(memory_...]
where the time goes in v4:
time: 707 us; the launch traced here: 698 us
  Pallas kernels  656 us (93%)
  local copies, waits for them, and re-layouts  33 us (5%)
    pallas_call x3, Pallas kernels, fused(): pl.pallas_call(kernel, in_specs=in_specs, out_specs=[pl.BlockSpec(memory_...  656 us

profile of v4, /device:TPU:0, one launch (start us, length us, event | category | flops | bytes accessed | tf_op | source)
XLA Modules:
  0.0 697.5 jit_solution(8584265913426158685)
XLA Ops:
  1.3 0.7 convert_convert_fusion
  2.1 0.1 add.74
  2.1 0.7 convert_element_type.24
  2.8 0.6 pad_convert_fusion.refs_13_
  3.4 0.6 broadcast_in_dim.24.refs_12_
  4.1 1.0 reshape.135
  5.1 0.2 iota_compare_fusion.2
  5.3 1.1 reshape.133
  6.9 0.5 reshape.144
  7.4 1.0 convolution_bitcast_fusion.1
  8.5 1.6 copy.37
  10.1 0.0 copy-start.12
  10.1 2.1 reshape.134.refs_0_.refs_2_
  12.2 0.0 copy-done.12
  12.2 1.8 convolution_bitcast_fusion
  14.0 3.6 reshape.136
  17.6 3.1 slice_bitcast_fusion.1
  20.7 2.1 pad_maximum_fusion.refs_3_.refs_14_
  22.8 291.1 %forward.1 = (bf16[2304,1024]{1,0:T(8,128)(2,1)}, bf16[576,1024]{1,0:T(8,128)(2,1)}, bf16[4,576,2048]{2,1,0:T(8,128)(2,1)}, bf16[576,1024]{1,0:T(8,128)(2,1)}, b...) custom-call(f32[8,256,128]{2,1,0:T(8,128)} %reshape.134.refs_0_.refs, ...), custom_call_target="tpu_custom_call" | custom-call | flops 99999997952 | tf_op jit(solution)/shard_map/forward/pallas_call | solution.py:1483
  313.9 182.2 %back_joint.1 = (bf16[4096,1024]{1,0:T(8,128)(2,1)}, bf16[1024,4096]{1,0:T(8,128)(2,1)}, bf16[1024,1024]{1,0:T(8,128)(2,1)}, f32[576,1024]{1,0:T(8,128)}, bf16[5...) custom-call(f32[1]{0:T(128)S(6)} %convert_element_type.21.refs_1_.re, ...), custom_call_target="tpu_custom_call" | custom-call | flops 99999997952 | tf_op jit(solution)/shard_map/back_joint/pallas_call | solution.py:1483
  496.1 182.3 %back_space.1 = (bf16[576,1024]{1,0:T(8,128)(2,1)}, bf16[2,4,576,1024]{3,2,1,0:T(8,128)(2,1)}, f32[8,2,2,8,8,128]{5,4,3,2,1,0:T(8,128)}, bf16[1024,3072]{1,0:T(8...) custom-call(bf16[576,1024]{1,0:T(8,128)(2,1)} %get-tuple-element.68., ...), custom_call_target="tpu_custom_call" | custom-call | flops 99999997952 | tf_op jit(solution)/shard_map/back_space/pallas_call | solution.py:1483
  678.4 0.0 copy-start.1
  678.4 0.9 slice.84
  679.4 0.0 copy-start
  679.4 1.7 slice.86
  681.1 0.6 copy.50
  681.8 1.6 reshape.139
  683.4 1.0 slice_bitcast_fusion.2
  684.4 0.7 copy.41
  685.1 1.7 reshape.140
  686.8 0.0 copy-done.1
  686.8 1.0 copy.83
  687.9 0.0 copy-done
  687.9 0.0 copy-start.3
  687.9 0.0 copy-start.9
  687.9 1.4 copy.84
  689.3 0.3 copy-done.3
  689.5 0.0 copy-start.11
  689.5 0.0 copy-start.7
  689.5 0.0 copy-start.6
  689.5 0.0 copy-start.2
  689.5 0.9 copy.85
  690.4 0.0 copy-done.9
  690.4 0.0 copy-start.8
  690.4 0.7 copy.86
  691.2 0.0 copy-done.11
  691.2 0.0 copy-start.10
  691.2 0.7 copy.87
  691.8 0.0 copy-done.7
  691.8 0.0 copy-start.5
  691.8 0.8 copy.88
  692.6 0.0 copy-done.6
  692.6 0.0 copy-start.4
  692.6 0.8 copy.89
  693.4 0.0 copy-done.2
  693.4 0.9 copy.90
  694.3 0.0 copy-done.8
  694.3 0.7 copy.91
  695.1 0.0 copy-done.10
  695.1 0.7 copy.92
  695.7 0.0 copy-done.5
  695.7 0.8 copy.93
  696.5 0.0 copy-done.4
  696.5 0.8 copy.94
  (20 shorter events, 0.4 us)
Async XLA Ops:
  10.1 2.1 copy-start.12
  678.4 8.4 %copy-start.1 = (bf16[576,1024]{1,0:T(8,128)(2,1)S(1)}, bf16[576,1024]{1,0:T(8,128)(2,1)}, u32[]{:S(2)}) copy-start(bf16[576,1024]{1,0:T(8,128)(2,1)} %get-tuple-element.138) | copy-start | bytes 3538948
  679.4 8.5 %copy-start = (f32[576,1024]{1,0:T(8,128)S(1)}, f32[576,1024]{1,0:T(8,128)}, u32[]{:S(2)}) copy-start(f32[576,1024]{1,0:T(8,128)} %get-tuple-element.139) | copy-start | bytes 7077892
  687.9 1.7 copy-start.3
  687.9 2.6 copy-start.9
  689.5 1.6 copy-start.11
  689.5 2.3 copy-start.7
  689.5 3.1 copy-start.6
  689.5 3.9 copy-start.2
  690.4 3.9 copy-start.8
  691.2 3.9 copy-start.10
  691.8 3.9 copy-start.5
  692.6 3.9 copy-start.4

commit v5 on v4

--- a/solution.py
+++ b/solution.py
@@ -826,7 +826,8 @@
                 pair_load(j - 1).start()
             pair_load(j).wait()
             for side in range(2):
-                feed.do(first + 2 * step + side)
+                if step + side:
+                    feed.do(first + 2 * step + side)
                 rows = slice(side * half, (side + 1) * half)
                 value = nt(pairs[step % 2, 0, rows, :], weights[:, part(1)])
                 value += nt(pairs[step % 2, 1, rows, :], weights[:, part(2)])
@@ -1895,39 +1896,39 @@
 )
 BACK_JOINT_ENDS = (
     -1, -1, -1, -1, -1, -1, -1, -1, -1, -1, -1, -1, -1, -1, -1, -1, -1, -1, -1, -1, -1, -1, -1, -1,
-    -1, -1, -1, -1, -1, -1, -1, -1, 0, -1, 1, 2, 3, 4, 5, 17, -1, 18, -1, 19, 6, 20, 7, 21, 22, 34,
-    8, 35, 9, 36, 10, 37, 11, 38, 12, 39, -1, -1, -1, -1, -1, -1, -1, 13, 23, 24, -1, -1, -1, -1,
-    -1, -1, -1, -1, -1, 14, 25, 26, 27, 28, 29, -1, -1, -1, -1, -1, 40, 41, -1, -1, 15, -1, 42, 43,
-    44, 45, 46, -1, -1, 30, -1, 16, -1, -1, -1, 31, -1, -1, -1, 51, 32, 52, 53, 54, 55, -1, 56, 47,
-    48, 49, -1, 33, -1, -1, -1, 57, 58, -1, -1, -1, 50, 59, 60, 61, 62, 63, -1, -1, 64, -1, -1, -1,
-    65, -1, -1, -1, 66, -1, -1, -1, -1, -1, -1, -1, -1, 67, -1, -1, -1, -1, -1, -1, -1, -1,
+    -1, -1, -1, -1, -1, -1, -1, -1, 0, -1, 1, -1, 2, 3, 4, 17, 5, -1, -1, -1, 18, 19, 6, 20, 7, 21,
+    34, 22, -1, -1, 35, 8, 36, 9, 37, 10, 38, 11, 39, 12, -1, -1, -1, -1, -1, -1, -1, 13, -1, 23,
+    24, -1, -1, -1, -1, -1, -1, -1, -1, -1, -1, 25, 14, 26, 27, 28, 29, -1, -1, 40, 41, -1, -1, -1,
+    15, -1, 42, 43, 44, 45, 46, -1, -1, 30, -1, -1, 16, -1, 51, -1, 31, 52, 53, 54, 55, 56, -1, -1,
+    32, -1, -1, -1, 47, -1, -1, 48, -1, 49, -1, -1, 33, -1, -1, 57, 58, -1, -1, -1, 50, 59, 60, 61,
+    62, 63, -1, -1, 64, -1, -1, -1, 65, -1, -1, -1, 66, -1, -1, -1, -1, -1, -1, -1, -1, 67,
 )
 BACK_JOINT_MIDDLES = (
     -1, -1, -1, -1, -1, -1, -1, -1, -1, -1, -1, -1, -1, -1, -1, -1, -1, -1, -1, -1, -1, -1, -1, -1,
-    -1, -1, -1, -1, -1, -1, -1, -1, 0, -1, 1, 2, 3, 4, 5, 17, -1, 18, -1, 19, 6, 20, 7, 21, 22, 34,
-    8, 35, 9, 36, 10, 37, 11, 38, 12, 39, -1, -1, -1, -1, -1, -1, -1, 23, 24, -1, -1, -1, -1, -1,
-    -1, 13, -1, -1, -1, 25, 26, 27, 28, 29, -1, -1, -1, -1, -1, 40, 14, 41, -1, -1, 15, 42, 43, 44,
-    45, 46, -1, -1, -1, -1, 16, -1, -1, -1, -1, 30, -1, -1, 51, 31, 52, 32, 53, 54, 55, 56, -1, -1,
-    -1, 33, 47, -1, 48, -1, 57, 49, 58, 50, -1, -1, 59, 60, 61, 62, 63, -1, -1, -1, -1, -1, -1, -1,
-    -1, 64, -1, -1, -1, 65, -1, 66, -1, -1, -1, 67, -1, -1, -1, -1, -1, -1, -1, -1, -1, -1,
+    -1, -1, -1, -1, -1, -1, -1, -1, 0, -1, 1, -1, 2, 3, 4, 17, 5, -1, -1, -1, 18, 19, 6, 20, 7, 21,
+    34, 22, -1, -1, 35, 8, 36, 9, 37, 10, 38, 11, 39, 12, -1, -1, -1, -1, -1, -1, -1, -1, 23, 24,
+    -1, -1, -1, -1, -1, 13, -1, -1, -1, -1, -1, 25, 26, 27, 28, 29, -1, -1, 40, 41, -1, -1, 14, -1,
+    15, -1, 42, 43, 44, 45, 46, -1, -1, -1, -1, 16, -1, 51, 30, -1, 52, 53, 54, 55, 56, -1, -1, -1,
+    -1, -1, 31, 32, -1, -1, -1, -1, -1, 47, 33, -1, 48, -1, 57, 49, 58, -1, 50, -1, 59, 60, 61, 62,
+    63, -1, -1, -1, -1, -1, -1, -1, -1, 64, -1, -1, -1, 65, -1, 66, -1, -1, -1, -1, 67, -1,
 )
 BACK_SPACE_ENDS = (
-    0, -1, 1, 2, 3, 4, 5, -1, -1, -1, -1, -1, 6, 7, -1, -1, -1, -1, 8, 9, 10, 11, 17, 12, 18, 13,
-    19, 20, 21, -1, 22, -1, -1, 14, -1, -1, -1, -1, -1, 15, -1, -1, -1, -1, -1, -1, -1, 23, 16, 24,
-    -1, 68, 69, 70, 71, 25, 26, 27, 28, 34, 29, 35, 30, 36, 37, 38, 39, -1, 31, -1, 72, 73, 74, 75,
-    32, -1, -1, 76, 77, 78, 79, 40, 41, 42, 43, 44, 45, 46, -1, 47, 48, 49, -1, 80, 81, -1, -1, -1,
-    82, -1, -1, -1, -1, -1, 83, 84, -1, -1, -1, 33, -1, 51, 87, 52, 88, 53, 89, 54, 90, 55, 91, 56,
-    92, 57, 93, 58, 94, 59, 95, 60, 96, 61, 97, 62, 98, 63, 99, 64, 100, 65, 101, 66, -1, 50, 102,
-    85, 103, 86, 67,
+    0, -1, 1, -1, 2, 3, 4, -1, 5, -1, -1, -1, -1, 6, 7, -1, -1, -1, -1, -1, 8, 9, 10, 11, 17, 12,
+    -1, 18, 13, 19, 20, 21, -1, 22, -1, -1, -1, 14, -1, -1, -1, -1, 15, -1, -1, -1, -1, -1, 68, 69,
+    70, 71, 23, 24, -1, 16, 25, 26, 27, 28, 34, 29, -1, 35, 30, 72, 73, 74, 75, 36, 37, 38, 39, -1,
+    31, -1, 76, 77, 78, 79, -1, 32, -1, 80, -1, 40, 41, 42, 43, 81, 44, 45, 46, -1, 47, -1, 48, 49,
+    -1, -1, 82, -1, -1, -1, -1, 83, 84, -1, -1, -1, 51, 87, 52, 88, 53, 89, 54, 90, 55, 91, 56, 92,
+    57, 93, 58, 33, 94, 59, 95, 60, 96, 61, 97, 62, 98, 63, 99, 64, 100, 65, 101, 66, -1, 102, 85,
+    103, 50, 86, 67,
 )
 BACK_SPACE_MIDDLES = (
-    0, -1, 1, 2, 3, 4, 5, -1, -1, -1, -1, -1, 6, 7, -1, -1, -1, -1, 8, 9, 10, 11, 17, 12, 18, -1,
-    19, 20, 21, 22, -1, -1, -1, -1, 13, -1, -1, -1, -1, 14, -1, -1, 15, -1, -1, -1, -1, 16, 23, 24,
-    -1, 25, 26, 27, 28, 34, 29, 35, 36, 37, 38, 39, -1, 68, -1, -1, -1, 69, -1, 76, 70, -1, 40, 77,
-    41, 42, 43, 44, 45, 46, 71, -1, 78, -1, 30, -1, -1, -1, -1, 79, 31, -1, -1, -1, 32, -1, 72, -1,
-    -1, 51, 87, 73, 52, 74, 88, 53, 75, 89, 54, 90, 55, 33, 91, 56, 92, 57, 80, 93, 58, 94, 59, 81,
-    95, 60, 96, 61, 82, 97, 62, 98, 63, 83, 99, 47, 84, 100, 48, 101, 49, -1, 50, 64, 102, 85, 65,
-    103, 66, 86, 67,
+    0, -1, 1, -1, 2, 3, 4, -1, 5, -1, -1, -1, -1, 6, 7, -1, -1, -1, -1, -1, 8, 9, 10, 11, 17, 12,
+    -1, 18, -1, 19, 20, 21, -1, 22, -1, -1, -1, -1, 13, -1, -1, -1, -1, 14, -1, -1, 15, -1, 16, 23,
+    24, -1, -1, -1, 25, 26, 68, 27, 28, 34, 29, -1, 35, 36, 69, 37, 38, 39, -1, 76, -1, 70, 77, -1,
+    -1, 71, -1, -1, 40, 78, 41, 42, 43, 44, 45, 30, 46, -1, -1, -1, 79, -1, 72, -1, -1, -1, -1, 51,
+    87, 73, 52, 74, 88, 53, 75, 89, 54, 90, 55, 31, 91, 56, 32, 92, 57, 80, 93, 58, 94, 59, 81, 95,
+    60, 96, 61, 82, 97, 62, 98, 63, 83, 99, 84, 100, 33, 101, 47, -1, 48, 102, 64, 85, 49, 103, 65,
+    50, 66, 86, 67,
 )
 
 

time: 707 us -> 694 us (0.982)
  Pallas kernels: 656 us -> 643 us
    pallas_call x3, Pallas kernels: 656 us -> 643 us  [fused(): pl.pallas_call(kernel, in_specs=in_specs, out_specs=[pl.BlockSpec(memory_...]
where the time goes in v5:
time: 694 us; the launch traced here: 685 us
  Pallas kernels  643 us (93%)
  local copies, waits for them, and re-layouts  33 us (5%)
    pallas_call x3, Pallas kernels, fused(): pl.pallas_call(kernel, in_specs=in_specs, out_specs=[pl.BlockSpec(memory_...  643 us

profile of v5, /device:TPU:0, one launch (start us, length us, event | category | flops | bytes accessed | tf_op | source)
XLA Modules:
  0.0 684.8 jit_solution(15557401773136711241)
XLA Ops:
  1.3 0.7 convert_convert_fusion
  2.1 0.1 add.74
  2.1 0.7 convert_element_type.24
  2.8 0.6 pad_convert_fusion.refs_13_
  3.4 0.6 broadcast_in_dim.24.refs_12_
  4.1 1.0 reshape.135
  5.1 0.2 iota_compare_fusion.2
  5.3 1.1 reshape.133
  6.9 0.5 reshape.144
  7.4 1.0 convolution_bitcast_fusion.1
  8.5 1.6 copy.37
  10.1 0.0 copy-start.12
  10.1 2.1 reshape.134.refs_0_.refs_2_
  12.2 0.0 copy-done.12
  12.2 1.8 convolution_bitcast_fusion
  14.0 3.6 reshape.136
  17.6 3.1 slice_bitcast_fusion.1
  20.7 2.1 pad_maximum_fusion.refs_3_.refs_14_
  22.8 291.1 %forward.1 = (bf16[2304,1024]{1,0:T(8,128)(2,1)}, bf16[576,1024]{1,0:T(8,128)(2,1)}, bf16[4,576,2048]{2,1,0:T(8,128)(2,1)}, bf16[576,1024]{1,0:T(8,128)(2,1)}, b...) custom-call(f32[8,256,128]{2,1,0:T(8,128)} %reshape.134.refs_0_.refs, ...), custom_call_target="tpu_custom_call" | custom-call | flops 99999997952 | tf_op jit(solution)/shard_map/forward/pallas_call | solution.py:1484
  313.9 172.1 %back_joint.1 = (bf16[4096,1024]{1,0:T(8,128)(2,1)}, bf16[1024,4096]{1,0:T(8,128)(2,1)}, bf16[1024,1024]{1,0:T(8,128)(2,1)}, f32[576,1024]{1,0:T(8,128)}, bf16[5...) custom-call(f32[1]{0:T(128)S(6)} %convert_element_type.21.refs_1_.re, ...), custom_call_target="tpu_custom_call" | custom-call | flops 99999997952 | tf_op jit(solution)/shard_map/back_joint/pallas_call | solution.py:1484
  486.0 179.6 %back_space.1 = (bf16[576,1024]{1,0:T(8,128)(2,1)}, bf16[2,4,576,1024]{3,2,1,0:T(8,128)(2,1)}, f32[8,2,2,8,8,128]{5,4,3,2,1,0:T(8,128)}, bf16[1024,3072]{1,0:T(8...) custom-call(bf16[576,1024]{1,0:T(8,128)(2,1)} %get-tuple-element.68., ...), custom_call_target="tpu_custom_call" | custom-call | flops 99999997952 | tf_op jit(solution)/shard_map/back_space/pallas_call | solution.py:1484
  665.6 0.0 copy-start.1
  665.7 0.9 slice.84
  666.6 0.0 copy-start
  666.6 1.7 slice.86
  668.4 0.6 copy.50
  669.0 1.6 reshape.139
  670.6 1.0 slice_bitcast_fusion.2
  671.6 0.7 copy.41
  672.3 1.7 reshape.140
  674.1 0.0 copy-done.1
  674.1 1.0 copy.83
  675.1 0.0 copy-done
  675.1 0.0 copy-start.3
  675.1 0.0 copy-start.9
  675.1 1.4 copy.84
  676.5 0.3 copy-done.3
  676.8 0.0 copy-start.11
  676.8 0.0 copy-start.7
  676.8 0.0 copy-start.6
  676.8 0.0 copy-start.2
  676.8 0.9 copy.85
  677.7 0.0 copy-done.9
  677.7 0.0 copy-start.8
  677.7 0.7 copy.86
  678.4 0.0 copy-done.11
  678.4 0.0 copy-start.10
  678.4 0.7 copy.87
  679.1 0.0 copy-done.7
  679.1 0.0 copy-start.5
  679.1 0.8 copy.88
  679.9 0.0 copy-done.6
  679.9 0.0 copy-start.4
  679.9 0.8 copy.89
  680.7 0.0 copy-done.2
  680.7 0.9 copy.90
  681.5 0.0 copy-done.8
  681.6 0.7 copy.91
  682.3 0.0 copy-done.10
  682.3 0.7 copy.92
  683.0 0.0 copy-done.5
  683.0 0.8 copy.93
  683.8 0.0 copy-done.4
  683.8 0.8 copy.94
  (20 shorter events, 0.4 us)
Async XLA Ops:
  10.1 2.1 copy-start.12
  665.6 8.4 %copy-start.1 = (bf16[576,1024]{1,0:T(8,128)(2,1)S(1)}, bf16[576,1024]{1,0:T(8,128)(2,1)}, u32[]{:S(2)}) copy-start(bf16[576,1024]{1,0:T(8,128)(2,1)} %get-tuple-element.138) | copy-start | bytes 3538948
  666.6 8.5 %copy-start = (f32[576,1024]{1,0:T(8,128)S(1)}, f32[576,1024]{1,0:T(8,128)}, u32[]{:S(2)}) copy-start(f32[576,1024]{1,0:T(8,128)} %get-tuple-element.139) | copy-start | bytes 7077892
  675.1 1.7 copy-start.3
  675.1 2.6 copy-start.9
  676.8 1.6 copy-start.11
  676.8 2.3 copy-start.7
  676.8 3.1 copy-start.6
  676.8 3.9 copy-start.2
  677.7 3.9 copy-start.8
  678.4 3.9 copy-start.10
  679.1 3.9 copy-start.5
  679.9 3.9 copy-start.4
